TPU v7x, 32 devices: a whole 2x2x4 slice. The times are simulated.
32 devices in a mesh: east: 2 (over core), north: 16 (over z, y, x).
Axes of the slice: x: 2, y: 2, z: 4, core: 2. Of those that a mesh axis runs over, the one named last changes fastest.
Arguments:
- adjoint_start: float32 [5, 32, 512, 256], P(None, 'east', 'north'), may hold values from -3 to 3
- adjoint_source: float32 [5, 32, 512, 256], P(None, 'east', 'north'), may hold values from -6 to 6
- base_flow: float32 [3, 32, 512, 256], P(None, 'east', 'north'), may hold values from -3 to 3
- eddy_visc: float32 [32, 512, 256], P('east', 'north'), may hold values from 0.1 to 3
- rotor_count: int32 [2, 16], P('east', 'north'), may hold values from 128 to 1024, as said below
- rotor_cell: int32 [2, 16, 1024], P('east', 'north'), may hold values from 0 to 131071
- rotor_turbine: int32 [2, 16, 1024], P('east', 'north'), may hold values from 0 to 191
- rotor_sector: int32 [2, 16, 1024], P('east', 'north'), may hold values from 0 to 7
- rotor_weight: float32 [2, 16, 1024], P('east', 'north'), may hold values from 0.25 to 1
Outputs:
- adjoint_final: float32 [5, 32, 512, 256], P(None, 'east', 'north')
- thrust_grad: float32 [4, 8, 192], P(None, None, 'north')
Inputs may be any that keep to these rules, and one draw needn't show every extreme that they name: `rotor_count`: an eighth of the tiles (at least one), drawn from the seed, hold 1024 live entries; the others hold 128 to 256.
All inputs are finite; a program needn't handle non-finite values.
Results may differ from a plain program's by a relative error of at most 0.0001.
Values sent between devices are 32-bit elements; how exact they have to be, the bound alone decides.
No kernel may reach another device: no remote copies, remote signals or barrier semaphores. Data moves between devices by JAX's collectives and lax.ppermute only.
A program may use at most 192 MiB of HBM per device.

v0:
```python
import jax
import jax.numpy as jnp
from jax import lax
from jax.sharding import PartitionSpec as P

SECT = 8
TURB_DEV = 12


def extended(shard, sides, width):
    for axis, dim in sides:
        size, length = (lax.axis_size(axis), shard.shape[dim])
        up = [(i, (i + 1) % size) for i in range(size - 1)]
        down = [(j, i) for i, j in up]
        last = lax.slice_in_dim(shard, length - width, length, axis=dim)
        leading = lax.slice_in_dim(shard, 0, width, axis=dim)
        before = lax.ppermute(last, axis, up)
        after = lax.ppermute(leading, axis, down)
        shard = jnp.concatenate([before, shard, after], axis=dim)
    return shard


def spread(field):
    return jnp.pad(field, ((0, 0), (0, 0), (0, 0), (1, 1)))


def beside_all(padded):
    total = padded[:, 2:, 1:-1, 1:-1] + padded[:, :-2, 1:-1, 1:-1]
    total = total + padded[:, 1:-1, 2:, 1:-1] + padded[:, 1:-1, :-2, 1:-1]
    return total + padded[:, 1:-1, 1:-1, 2:] + padded[:, 1:-1, 1:-1, :-2]


def slopes(padded):
    return [
        padded[:, 2:, 1:-1, 1:-1] - padded[:, :-2, 1:-1, 1:-1],
        padded[:, 1:-1, 2:, 1:-1] - padded[:, 1:-1, :-2, 1:-1],
        padded[:, 1:-1, 1:-1, 2:] - padded[:, 1:-1, 1:-1, :-2],
    ]


def relax(state_pad, base_pad, source):
    full = spread(state_pad)
    base_full = spread(base_pad)
    centre = full[:, 1:-1, 1:-1, 1:-1]
    base_centre = base_full[:, 1:-1, 1:-1, 1:-1]
    neighbours = beside_all(full)
    diffs = slopes(full)
    velocity_base = base_centre[:3]
    viscous = 1.0 + base_centre[3]
    convect = (
        velocity_base[0] * diffs[0][:3]
        + velocity_base[1] * diffs[1][:3]
        + velocity_base[2] * diffs[2][:3]
    )
    pressure_grad = jnp.stack([diffs[0][3], diffs[1][3], diffs[2][3]])
    velocity = (source[:3] + viscous * neighbours[:3] + 0.5 * convect - 0.5 * pressure_grad) / (
        6.0 * viscous + 1.0
    )
    diverge = diffs[0][0] + diffs[1][1] + diffs[2][2]
    pressure = (source[3] + neighbours[3] - 0.5 * diverge) / 7.0
    curvature = beside_all(base_full[:3]) - 6.0 * velocity_base
    eddy_new = (
        source[4] + viscous * neighbours[4] + 0.25 * jnp.sum(centre[:3] * curvature, axis=0)
    ) / (6.0 * viscous + 2.0)
    return jnp.concatenate([velocity, pressure[None], eddy_new[None]], axis=0)


def shards(
    adjoint_start,
    adjoint_source,
    base_flow,
    eddy_visc,
    rotor_count,
    rotor_cell,
    rotor_turbine,
    rotor_sector,
    rotor_weight,
):
    base_four = jnp.concatenate([base_flow, eddy_visc[None]], axis=0)
    base_pad = extended(base_four, (("east", 1), ("north", 2)), 1)
    state = adjoint_start
    for sweep in range(2):
        state_pad = extended(state, (("east", 1), ("north", 2)), 1)
        state = relax(state_pad, base_pad, adjoint_source)
    cells = rotor_cell.reshape(-1)
    flat_state = state.reshape(5, -1)
    values = flat_state[:, cells]
    chosen = jnp.stack([values[0], values[1], values[2], values[4]])
    upstream = base_flow[0].reshape(-1)[cells]
    slot_count = cells.shape[0]
    live = jnp.arange(slot_count, dtype=jnp.int32) < rotor_count.reshape(-1)[0]
    factor = jnp.where(live, rotor_weight.reshape(-1) * upstream * jnp.abs(upstream), 0.0)
    terms = chosen * factor[None]
    sector_hot = (
        rotor_sector.reshape(-1)[None, :] == jnp.arange(SECT, dtype=jnp.int32)[:, None]
    ).astype(jnp.float32)
    combined = (terms[:, None, :] * sector_hot[None]).reshape(4 * SECT, slot_count)
    turbine_total_count = TURB_DEV * lax.axis_size("north")
    turbine_hot = (
        rotor_turbine.reshape(-1)[:, None]
        == jnp.arange(turbine_total_count, dtype=jnp.int32)[None, :]
    ).astype(jnp.float32)
    partial_grad = jnp.dot(
        combined, turbine_hot, precision=lax.Precision.HIGHEST, preferred_element_type=jnp.float32
    )
    summed = lax.psum(partial_grad, ("east", "north"))
    owned = lax.dynamic_slice_in_dim(summed, lax.axis_index("north") * TURB_DEV, TURB_DEV, 1)
    return (state, owned.reshape(4, SECT, TURB_DEV))


def solution(mesh):
    placed = (
        P(None, "east", "north", None),
        P(None, "east", "north", None),
        P(None, "east", "north", None),
        P("east", "north", None),
        P("east", "north"),
        P("east", "north", None),
        P("east", "north", None),
        P("east", "north", None),
        P("east", "north", None),
    )
    return jax.shard_map(
        shards,
        mesh=mesh,
        in_specs=placed,
        out_specs=(P(None, "east", "north", None), P(None, None, "north")),
        check_vma=False,
    )
```

profile of v0, /device:TPU:0, one launch (start us, length us, event | category | flops | bytes accessed | tf_op | source)
XLA Modules:
  0.0 187.2 jit_solution(10360540264879836349)
XLA Ops:
  0.6 1.9 pad_maximum_fusion.37
  2.5 3.0 %collective-permute-start.5 = (f32[4,1,32,256]{3,2,1,0:T(8,128)}, f32[4,1,32,256]{3,2,1,0:T(8,128)}, u32[]{:S(2)}, u32[]{:S(2)}) collective-permute-start(f32[4,1,32,256]{3,2,1,0:T(8,128)} %get-tuple-element.27), channel_id=1, source_target_pairs={{0,16},{1,17},{2,18},{3,19},{4,20},{5,21},{6,22},{7,23},{8,24},{9,... | collective-permute-start | bytes 393224 | tf_op jit(solution)/shard_map/ppermute | solution.py:17
  5.5 1.3 collective-permute-start.4
  6.8 1.7 fusion.45
  8.5 1.3 collective-permute-start
  9.9 3.7 %collective-permute-start.1 = (f32[5,1,32,256]{3,2,1,0:T(8,128)}, f32[5,1,32,256]{3,2,1,0:T(8,128)S(1)}, u32[]{:S(2)}, u32[]{:S(2)}) collective-permute-start(f32[5,1,32,256]{3,2,1,0:T(8,128)} %get-tuple-element.24), channel_id=1, source_target_pairs={{0,16},{1,17},{2,18},{3,19},{4,20},{5,21},{6,22},{7,23},{8,24},{9,... | collective-permute-start | bytes 491528 | tf_op jit(solution)/shard_map/ppermute | solution.py:17
  14.5 1.5 fusion.46
  17.3 1.3 copy.25
  18.6 6.2 %gather_fusion.1 = f32[1024]{0:T(1024)S(1)} fusion(f32[131072]{0:T(1024)S(1)} %bitcast.42, s32[1024]{0:T(1024)S(1)} %broadcast_clamp_fusion), kind=kCustom, calls=%fused_computation.1 | custom fusion | bytes 12288 | tf_op jit(solution)/shard_map/gather | solution.py:89
  25.8 4.2 %collective-permute-start.7 = (f32[4,18,1,256]{3,2,1,0:T(1,128)S(1)}, f32[4,18,1,256]{3,2,1,0:T(1,128)S(1)}, u32[]{:S(2)}, u32[]{:S(2)}) collective-permute-start(f32[4,18,1,256]{3,2,1,0:T(1,128)S(1)} %get-tuple-element.25), channel_id=1, source_target_pairs={{0,1},{1,2},{2,3},{3,4},{4,5},{5,6},{6,7},{7,8},{8,9},{9,10},{10,1... | collective-permute-start | bytes 221192 | tf_op jit(solution)/shard_map/ppermute | solution.py:17
  30.1 1.3 collective-permute-start.6
  32.2 4.6 %collective-permute-start.3 = (f32[5,18,1,256]{3,2,1,0:T(1,128)S(1)}, f32[5,18,1,256]{3,2,1,0:T(1,128)S(1)}, u32[]{:S(2)}, u32[]{:S(2)}) collective-permute-start(f32[5,18,1,256]{3,2,1,0:T(1,128)S(1)} %get-tuple-element.14), channel_id=1, source_target_pairs={{0,1},{1,2},{2,3},{3,4},{4,5},{5,6},{6,7},{7,8},{8,9},{9,10},{10,1... | collective-permute-start | bytes 276488 | tf_op jit(solution)/shard_map/ppermute | solution.py:17
  36.7 1.3 collective-permute-start.2
  38.9 5.5 %select_maximum_fusion.8 = f32[4,18,34,258]{3,2,1,0:T(8,128)S(1)} fusion(f32[4,18,1,256]{3,2,1,0:T(1,128)S(1)} %collective-permute-done.6, f32[4,18,1,256]{3,2,1,0:T(1,128)S(1)} %collective-permute-done.7, f32[4,1,32,256]{3,2,1,0:T(8,128)} %collective-permute-done.4, f32[4,1,32,256]{3,2,1,0:T(8,128)} %collective-permute-done.5, ...), kind=kLoop, calls=%fused_computation.15 | loop fusion | flops 8842176 | bytes 5033088 | tf_op jit(solution)/shard_map/concatenate | solution.py:19
  44.4 3.0 %select_maximum_fusion.6 = f32[5,18,34,258]{3,2,1,0:T(8,128)S(1)} fusion(f32[5,18,1,256]{3,2,1,0:T(1,128)S(1)} %collective-permute-done.2, f32[5,18,32,256]{3,2,1,0:T(8,128)S(1)} %constant_dynamic-update-slice_fusion, f32[5,18,1,256]{3,2,1,0:T(1,128)S(1)} %collective-permute-done.3), kind=kLoop, calls=%fused_computation.12 | loop fusion | flops 6315840 | bytes 6291360 | tf_op jit(solution)/shard_map/concatenate | solution.py:19
  47.5 3.6 %slice_subtract_fusion.1 = (f32[5,16,32,256]{3,2,1,0:T(8,128)S(1)}, f32[5,16,32,256]{3,2,1,0:T(8,128)S(1)}, f32[5,16,32,256]{3,2,1,0:T(8,128)S(1)}) fusion(f32[5,18,34,258]{3,2,1,0:T(8,128)S(1)} %select_maximum_fusion.6, f32[5,18,32,256]{3,2,1,0:T(8,128)S(1)} %constant_dynamic-update-slice_fusion, f32[5,18,1,256]{3,2,1,0:T(1,128)S(1)} %collective-permute-done.3, ...), kind=kLoop, calls=%fused_computation.46 | loop fusion | flops 7208960 | bytes 19189760 | tf_op jit(solution)/shard_map/sub | solution.py:37
  51.2 5.9 %multiply_reduce_fusion = (f32[16,32,256]{2,1,0:T(8,128)}, f32[16,32,256]{2,1,0:T(8,128)}, f32[3,16,32,256]{3,2,1,0:T(8,128)S(1)}) fusion(f32[5,16,32,256]{3,2,1,0:T(8,128)S(1)} %copy-done.2, f32[16,32,256]{2,1,0:T(8,128)S(1)} %copy-done.5, f32[1,16,32,256]{3,2,1,0:T(8,128)S(1)} %slice.361, f32[1,16,32,256]{3,2,1,0:T(8,128)S(1)} %slice.360, ...), kind=kLoop, calls=%fused_computation.91 | loop fusion | flops 14286848 | bytes 21905408 | tf_op jit(solution)/shard_map/reduce_sum | solution.py:63
  57.2 2.0 %fusion.36 = (f32[1,16,32,256]{3,2,1,0:T(8,128)S(1)}, f32[1,16,32,256]{3,2,1,0:T(8,128)S(1)}) fusion(f32[5,16,32,256]{3,2,1,0:T(8,128)S(1)} %get-tuple-element.5, f32[5,16,32,256]{3,2,1,0:T(8,128)S(1)} %get-tuple-element.11, f32[5,16,32,256]{3,2,1,0:T(8,128)} %copy-done.3, f32[5,16,32,256]{3,2,1,0:T(8,128)S(1)} %get-tuple-element.6, ...), kind=kLoop, calls=%fused_computation.114 | loop fusion | flops 1835008 | bytes 5767168 | tf_op jit(solution)/shard_map/div | solution.py:60
  59.3 1.3 collective-permute-start.9
  60.6 1.3 collective-permute-start.8
  61.9 2.0 %collective-permute-done.8 = f32[5,1,32,256]{3,2,1,0:T(8,128)S(1)} collective-permute-done((f32[5,1,32,256]{3,2,1,0:T(8,128)S(1)}, f32[5,1,32,256]{3,2,1,0:T(8,128)S(1)}, u32[]{:S(2)}, u32[]{:S(2)}) %collective-permute-start.8) | collective-permute-done | bytes 163872 | tf_op jit(solution)/shard_map/ppermute | solution.py:18
  64.0 4.9 %collective-permute-start.11 = (f32[5,18,1,256]{3,2,1,0:T(1,128)S(1)}, f32[5,18,1,256]{3,2,1,0:T(1,128)S(1)}, u32[]{:S(2)}, u32[]{:S(2)}) collective-permute-start(f32[5,18,1,256]{3,2,1,0:T(1,128)S(1)} %get-tuple-element.12), channel_id=1, source_target_pairs={{0,1},{1,2},{2,3},{3,4},{4,5},{5,6},{6,7},{7,8},{8,9},{9,10},{10,1... | collective-permute-start | bytes 276488 | tf_op jit(solution)/shard_map/ppermute | solution.py:17
  68.9 1.3 collective-permute-start.10
  71.1 5.3 %collective-permute-done.10 = f32[5,18,1,256]{3,2,1,0:T(1,128)S(1)} collective-permute-done((f32[5,18,1,256]{3,2,1,0:T(1,128)S(1)}, f32[5,18,1,256]{3,2,1,0:T(1,128)S(1)}, u32[]{:S(2)}, u32[]{:S(2)}) %collective-permute-start.10) | collective-permute-done | bytes 92192 | tf_op jit(solution)/shard_map/ppermute | solution.py:18
  76.5 6.1 %select_maximum_fusion = f32[5,18,34,258]{3,2,1,0:T(8,128)S(1)} fusion(f32[5,18,1,256]{3,2,1,0:T(1,128)S(1)} %collective-permute-done.10, f32[5,18,1,256]{3,2,1,0:T(1,128)S(1)} %collective-permute-done.11, f32[5,1,32,256]{3,2,1,0:T(8,128)S(1)} %collective-permute-done.8, f32[5,1,32,256]{3,2,1,0:T(8,128)S(1)} %collective-permute-done.9, ...), kind=kLoop, calls=%fused_computation.6 | loop fusion | flops 12631680 | bytes 6291360 | tf_op jit(solution)/shard_map/concatenate | solution.py:19
  84.6 4.5 %add_add_fusion = f32[5,16,32,256]{3,2,1,0:T(8,128)S(1)} fusion(f32[5,18,34,258]{3,2,1,0:T(8,128)S(1)} %select_maximum_fusion, f32[5,1,32,256]{3,2,1,0:T(8,128)S(1)} %collective-permute-done.8, f32[1,16,32,256]{3,2,1,0:T(8,128)S(1)} %get-tuple-element.10, f32[1,16,32,256]{3,2,1,0:T(8,128)S(1)} %get-tuple-element.9, ...), kind=kLoop, calls=%fused_computation.43 | loop fusion | flops 13762560 | bytes 10997760 | tf_op jit(solution)/shard_map/add | solution.py:30
  91.0 1.5 fusion.8
  92.5 1.8 pad_maximum_fusion.21
  95.3 3.3 %pad_maximum_fusion = f32[5,131072]{1,0:T(8,128)} fusion(f32[1,131072]{1,0:T(1,128)S(1)} %bitcast.53, f32[1,131072]{1,0:T(1,128)S(1)} %bitcast.54, f32[3,131072]{1,0:T(4,128)S(1)} %bitcast.48), kind=kLoop, calls=%fused_computation.21 | loop fusion | flops 1310720 | bytes 5242880 | tf_op jit(solution)/shard_map/concatenate | solution.py:65
  98.7 30.3 %copy.18 = f32[5,131072]{0,1:T(8,128)} copy(f32[5,131072]{1,0:T(8,128)} %pad_maximum_fusion) | data formatting | bytes 5242880 | tf_op jit(solution)/shard_map/concatenate | solution.py:65
  128.9 10.5 %gather_fusion = f32[1024,5]{1,0:T(8,128)S(1)} fusion(f32[5,131072]{0,1:T(8,128)} %copy.18, s32[1024]{0:T(1024)S(1)} %broadcast_clamp_fusion), kind=kCustom, calls=%fused_computation | custom fusion | bytes 45056 | tf_op jit(solution)/shard_map/gather | solution.py:87
  141.2 45.3 %psum.7 = f32[32,192]{0,1:T(8,128)S(1)} all-reduce(f32[32,192]{0,1:T(8,128)S(1)} %fusion.23), channel_id=1, replica_groups=mesh['east'=2,'north'=16] {'east','north'}, use_global_device_ids=true, to_apply=%region_2.3 | all-reduce | flops 6144 | bytes 49152 | tf_op jit(solution)/shard_map/psum | solution.py:106
  (71 shorter events, 12.9 us)
Async XLA Ops:
  0.6 13.9 %copy-start = (f32[3,16,32,256]{3,2,1,0:T(8,128)S(1)}, f32[3,16,32,256]{3,2,1,0:T(8,128)}, u32[]{:S(2)}) copy-start(f32[3,16,32,256]{3,2,1,0:T(8,128)} %param.11) | copy-start | bytes 4718596
  0.6 12.9 %copy-start.1 = (f32[16,32,256]{2,1,0:T(8,128)S(1)}, f32[16,32,256]{2,1,0:T(8,128)}, u32[]{:S(2)}) copy-start(f32[16,32,256]{2,1,0:T(8,128)} %param.12) | copy-start | bytes 1572868
  2.5 22.2 %collective-permute-start.5 = (f32[4,1,32,256]{3,2,1,0:T(8,128)}, f32[4,1,32,256]{3,2,1,0:T(8,128)}, u32[]{:S(2)}, u32[]{:S(2)}) collective-permute-start(f32[4,1,32,256]{3,2,1,0:T(8,128)} %get-tuple-element.27), channel_id=1, source_target_pairs={{0,16},{1,17},{2,18},{3,19},{4,20},{5,21},{6,22},{7,23},{8,24},{9,... | collective-permute-start | bytes 393224 | tf_op jit(solution)/shard_map/ppermute | solution.py:17
  5.5 19.2 %collective-permute-start.4 = (f32[4,1,32,256]{3,2,1,0:T(8,128)}, f32[4,1,32,256]{3,2,1,0:T(8,128)}, u32[]{:S(2)}, u32[]{:S(2)}) collective-permute-start(f32[4,1,32,256]{3,2,1,0:T(8,128)} %get-tuple-element.28), channel_id=1, source_target_pairs={{16,0},{17,1},{18,2},{19,3},{20,4},{21,5},{22,6},{23,7},{24,8},{25... | collective-permute-start | bytes 393224 | tf_op jit(solution)/shard_map/ppermute | solution.py:18
  8.5 22.9 %collective-permute-start = (f32[5,1,32,256]{3,2,1,0:T(8,128)}, f32[5,1,32,256]{3,2,1,0:T(8,128)S(1)}, u32[]{:S(2)}, u32[]{:S(2)}) collective-permute-start(f32[5,1,32,256]{3,2,1,0:T(8,128)} %get-tuple-element.23), channel_id=1, source_target_pairs={{16,0},{17,1},{18,2},{19,3},{20,4},{21,5},{22,6},{23,7},{24,8},{25... | collective-permute-start | bytes 491528 | tf_op jit(solution)/shard_map/ppermute | solution.py:18
  9.8 6.1 %copy-start.14 = (s32[1,1,1024]{2,1,0:T(1,128)S(1)}, s32[1,1,1024]{2,1,0:T(1,128)}, u32[]{:S(2)}) copy-start(s32[1,1,1024]{2,1,0:T(1,128)} %param.14) | copy-start | bytes 12292
  9.8 6.1 %copy-start.12 = (s32[1,1,1024]{2,1,0:T(1,128)S(1)}, s32[1,1,1024]{2,1,0:T(1,128)}, u32[]{:S(2)}) copy-start(s32[1,1,1024]{2,1,0:T(1,128)} %param.16) | copy-start | bytes 12292
  9.9 21.5 %collective-permute-start.1 = (f32[5,1,32,256]{3,2,1,0:T(8,128)}, f32[5,1,32,256]{3,2,1,0:T(8,128)S(1)}, u32[]{:S(2)}, u32[]{:S(2)}) collective-permute-start(f32[5,1,32,256]{3,2,1,0:T(8,128)} %get-tuple-element.24), channel_id=1, source_target_pairs={{0,16},{1,17},{2,18},{3,19},{4,20},{5,21},{6,22},{7,23},{8,24},{9,... | collective-permute-start | bytes 491528 | tf_op jit(solution)/shard_map/ppermute | solution.py:17
  24.7 6.7 %copy-start.2 = (f32[5,16,32,256]{3,2,1,0:T(8,128)S(1)}, f32[5,16,32,256]{3,2,1,0:T(8,128)}, u32[]{:S(2)}) copy-start(f32[5,16,32,256]{3,2,1,0:T(8,128)} %param.9) | copy-start | bytes 7864324
  25.8 13.1 %collective-permute-start.7 = (f32[4,18,1,256]{3,2,1,0:T(1,128)S(1)}, f32[4,18,1,256]{3,2,1,0:T(1,128)S(1)}, u32[]{:S(2)}, u32[]{:S(2)}) collective-permute-start(f32[4,18,1,256]{3,2,1,0:T(1,128)S(1)} %get-tuple-element.25), channel_id=1, source_target_pairs={{0,1},{1,2},{2,3},{3,4},{4,5},{5,6},{6,7},{7,8},{8,9},{9,10},{10,1... | collective-permute-start | bytes 221192 | tf_op jit(solution)/shard_map/ppermute | solution.py:17
  30.1 8.8 %collective-permute-start.6 = (f32[4,18,1,256]{3,2,1,0:T(1,128)S(1)}, f32[4,18,1,256]{3,2,1,0:T(1,128)S(1)}, u32[]{:S(2)}, u32[]{:S(2)}) collective-permute-start(f32[4,18,1,256]{3,2,1,0:T(1,128)S(1)} %get-tuple-element.26), channel_id=1, source_target_pairs={{1,0},{2,1},{3,2},{4,3},{5,4},{6,5},{7,6},{8,7},{9,8},{10,9},{11,1... | collective-permute-start | bytes 221192 | tf_op jit(solution)/shard_map/ppermute | solution.py:18
  32.0 12.4 %copy-start.3 = (f32[5,16,32,256]{3,2,1,0:T(8,128)}, f32[5,16,32,256]{3,2,1,0:T(8,128)S(1)}, u32[]{:S(2)}) copy-start(f32[5,16,32,256]{3,2,1,0:T(8,128)S(1)} %get-tuple-element.21) | copy-start | bytes 7864324
  32.2 12.2 %collective-permute-start.3 = (f32[5,18,1,256]{3,2,1,0:T(1,128)S(1)}, f32[5,18,1,256]{3,2,1,0:T(1,128)S(1)}, u32[]{:S(2)}, u32[]{:S(2)}) collective-permute-start(f32[5,18,1,256]{3,2,1,0:T(1,128)S(1)} %get-tuple-element.14), channel_id=1, source_target_pairs={{0,1},{1,2},{2,3},{3,4},{4,5},{5,6},{6,7},{7,8},{8,9},{9,10},{10,1... | collective-permute-start | bytes 276488 | tf_op jit(solution)/shard_map/ppermute | solution.py:17
  36.7 7.7 %collective-permute-start.2 = (f32[5,18,1,256]{3,2,1,0:T(1,128)S(1)}, f32[5,18,1,256]{3,2,1,0:T(1,128)S(1)}, u32[]{:S(2)}, u32[]{:S(2)}) collective-permute-start(f32[5,18,1,256]{3,2,1,0:T(1,128)S(1)} %get-tuple-element.15), channel_id=1, source_target_pairs={{1,0},{2,1},{3,2},{4,3},{5,4},{6,5},{7,6},{8,7},{9,8},{10,9},{11,1... | collective-permute-start | bytes 276488 | tf_op jit(solution)/shard_map/ppermute | solution.py:18
  38.9 5.5 %copy-start.10 = (f32[4,18,1,256]{3,2,1,0:T(1,128)}, f32[4,18,1,256]{3,2,1,0:T(1,128)S(1)}, u32[]{:S(2)}) copy-start(f32[4,18,1,256]{3,2,1,0:T(1,128)S(1)} %collective-permute-done.6) | copy-start | bytes 221188
  47.5 3.7 %copy-start.5 = (f32[16,32,256]{2,1,0:T(8,128)S(1)}, f32[16,32,256]{2,1,0:T(8,128)}, u32[]{:S(2)}) copy-start(f32[16,32,256]{2,1,0:T(8,128)} %get-tuple-element.34) | copy-start | bytes 1572868
  47.5 3.7 %copy-start.6 = (f32[16,32,256]{2,1,0:T(8,128)S(1)}, f32[16,32,256]{2,1,0:T(8,128)}, u32[]{:S(2)}) copy-start(f32[16,32,256]{2,1,0:T(8,128)} %get-tuple-element.30) | copy-start | bytes 1572868
  47.5 3.7 %copy-start.7 = (f32[16,32,256]{2,1,0:T(8,128)S(1)}, f32[16,32,256]{2,1,0:T(8,128)}, u32[]{:S(2)}) copy-start(f32[16,32,256]{2,1,0:T(8,128)} %get-tuple-element.31) | copy-start | bytes 1572868
  59.2 2.7 %copy-start.13 = (f32[1,1,1024]{2,1,0:T(1,128)S(1)}, f32[1,1,1024]{2,1,0:T(1,128)}, u32[]{:S(2)}) copy-start(f32[1,1,1024]{2,1,0:T(1,128)} %param.17) | copy-start | bytes 12292
  59.3 2.6 %collective-permute-start.9 = (f32[5,1,32,256]{3,2,1,0:T(8,128)S(1)}, f32[5,1,32,256]{3,2,1,0:T(8,128)S(1)}, u32[]{:S(2)}, u32[]{:S(2)}) collective-permute-start(f32[5,1,32,256]{3,2,1,0:T(8,128)S(1)} %get-tuple-element.19), channel_id=1, source_target_pairs={{0,16},{1,17},{2,18},{3,19},{4,20},{5,21},{6,22},{7,23},{8,24},{9,... | collective-permute-start | bytes 491528 | tf_op jit(solution)/shard_map/ppermute | solution.py:17
  60.6 3.3 %collective-permute-start.8 = (f32[5,1,32,256]{3,2,1,0:T(8,128)S(1)}, f32[5,1,32,256]{3,2,1,0:T(8,128)S(1)}, u32[]{:S(2)}, u32[]{:S(2)}) collective-permute-start(f32[5,1,32,256]{3,2,1,0:T(8,128)S(1)} %get-tuple-element.20), channel_id=1, source_target_pairs={{16,0},{17,1},{18,2},{19,3},{20,4},{21,5},{22,6},{23,7},{24,8},{25... | collective-permute-start | bytes 491528 | tf_op jit(solution)/shard_map/ppermute | solution.py:18
  64.0 7.1 %collective-permute-start.11 = (f32[5,18,1,256]{3,2,1,0:T(1,128)S(1)}, f32[5,18,1,256]{3,2,1,0:T(1,128)S(1)}, u32[]{:S(2)}, u32[]{:S(2)}) collective-permute-start(f32[5,18,1,256]{3,2,1,0:T(1,128)S(1)} %get-tuple-element.12), channel_id=1, source_target_pairs={{0,1},{1,2},{2,3},{3,4},{4,5},{5,6},{6,7},{7,8},{8,9},{9,10},{10,1... | collective-permute-start | bytes 276488 | tf_op jit(solution)/shard_map/ppermute | solution.py:17
  68.9 7.5 %collective-permute-start.10 = (f32[5,18,1,256]{3,2,1,0:T(1,128)S(1)}, f32[5,18,1,256]{3,2,1,0:T(1,128)S(1)}, u32[]{:S(2)}, u32[]{:S(2)}) collective-permute-start(f32[5,18,1,256]{3,2,1,0:T(1,128)S(1)} %get-tuple-element.13), channel_id=1, source_target_pairs={{1,0},{2,1},{3,2},{4,3},{5,4},{6,5},{7,6},{8,7},{9,8},{10,9},{11,1... | collective-permute-start | bytes 276488 | tf_op jit(solution)/shard_map/ppermute | solution.py:18
  84.6 4.6 %copy-start.4 = (f32[5,16,32,256]{3,2,1,0:T(8,128)S(1)}, f32[5,16,32,256]{3,2,1,0:T(8,128)}, u32[]{:S(2)}) copy-start(f32[5,16,32,256]{3,2,1,0:T(8,128)} %param.10) | copy-start | bytes 7864324
  84.6 4.6 %copy-start.9 = (f32[16,32,256]{2,1,0:T(8,128)S(1)}, f32[16,32,256]{2,1,0:T(8,128)}, u32[]{:S(2)}) copy-start(f32[16,32,256]{2,1,0:T(8,128)} %get-tuple-element.2) | copy-start | bytes 1572868
  89.2 1.8 copy-start.8
  98.7 41.4 %copy-start.11 = (f32[8,1024]{1,0:T(8,128)S(1)}, f32[8,1024]{1,0:T(8,128)}, u32[]{:S(2)}) copy-start(f32[8,1024]{1,0:T(8,128)} %fusion.42) | copy-start | bytes 98308
  98.7 41.4 %copy-start.15 = (s32[1,1,1024]{2,1,0:T(1,128)S(1)}, s32[1,1,1024]{2,1,0:T(1,128)}, u32[]{:S(2)}) copy-start(s32[1,1,1024]{2,1,0:T(1,128)} %param.15) | copy-start | bytes 12292
where the time goes:
time: 188 us; the launch traced here: 187 us
  local copies, waits for them, and re-layouts  56 us (30%)
  other arithmetic  45.7 us (24%)
  blocking collectives  45.3 us (24%)
  starting transfers between devices  29.4 us (16%)
  waiting for transfers between devices  7.78 us (4%)
    psum x1, blocking collectives, shards(): summed = lax.psum(partial_grad, ('east', 'north'))  45.3 us
    concatenate x1, local copies, waits for them, and re-layouts, relax(): return jnp.concatenate([velocity, pressure[None], eddy_new[None]], axis=0)  30.3 us
    ppermute x6, starting transfers between devices, extended(): before = lax.ppermute(last, axis, up)  21.7 us
    concatenate x5, other arithmetic, extended(): shard = jnp.concatenate([before, shard, after], axis=dim)  15.8 us
    gather x1, local copies, waits for them, and re-layouts, shards(): values = flat_state[:, cells]  10.5 us
    ppermute x6, starting transfers between devices, extended(): after = lax.ppermute(leading, axis, down)  7.73 us
    ppermute x6, waiting for transfers between devices, extended(): after = lax.ppermute(leading, axis, down)  7.31 us
    gather x1, local copies, waits for them, and re-layouts, shards(): upstream = base_flow[0].reshape(-1)[cells]  6.15 us
  transfers between devices with their start and end apart: 12, of which 3 were waited for; matrix products, arithmetic and copies ran while one was open for 11% of the time, Pallas kernels for 0%

commit v1 on v0

v1 whole, which is shorter than its diff:
```python
import functools

import jax
import jax.numpy as jnp
from jax import lax
from jax.experimental import pallas as pl
from jax.experimental.pallas import tpu as pltpu
from jax.sharding import PartitionSpec as P

SECT = 8
TURB_DEV = 12
COMPS = 4
LANES = 128
SUB = 8
PACK = 14
EDGE = 6
VMEM = pltpu.VMEM
F32 = jnp.float32


def whole(space=VMEM):
    return pl.BlockSpec(memory_space=space)


def in_vmem(x):
    return pltpu.with_memory_space_constraint(x, VMEM)


def params(mib):
    return pltpu.CompilerParams(vmem_limit_bytes=mib << 20)


def cost(flops, size):
    return pl.CostEstimate(flops=flops, bytes_accessed=size, transcendentals=0)


def face_kernel(at, start, flow, eddy, out, sems):
    e = at[0]
    copies = [
        pltpu.make_async_copy(start.at[:, e], out.at[0:5], sems.at[0]),
        pltpu.make_async_copy(flow.at[:, e], out.at[5:8], sems.at[1]),
        pltpu.make_async_copy(eddy.at[e], out.at[8], sems.at[2]),
    ]
    for c in copies:
        c.start()
    for c in copies:
        c.wait()


def east_face(at, start, flow, eddy):
    _, _, cn, cz = start.shape
    return pl.pallas_call(
        face_kernel,
        out_shape=jax.ShapeDtypeStruct((9, cn, cz), F32),
        in_specs=[whole(pltpu.SMEM), whole(pl.ANY), whole(pl.ANY), whole(pl.ANY)],
        out_specs=whole(pl.ANY),
        scratch_shapes=[pltpu.SemaphoreType.DMA((3,))],
        cost_estimate=cost(0, 18 * cn * cz * 4),
    )(at.reshape(1), start, flow, eddy)


def swap_faces(low, high, size):
    if size == 2:
        got = lax.ppermute(low, "east", [(0, 1), (1, 0)])
        return got, got
    up = [(i, i + 1) for i in range(size - 1)]
    down = [(i + 1, i) for i in range(size - 1)]
    return lax.ppermute(high, "east", up), lax.ppermute(low, "east", down)


class Shifts:
    def __init__(self, rows, cols):
        self.rows, self.cols = rows, cols
        r = lax.broadcasted_iota(jnp.int32, (rows, cols), 0)
        z = lax.broadcasted_iota(jnp.int32, (rows, cols), 1)
        self.not_top, self.not_bottom = r < rows - 1, r > 0
        self.not_high, self.not_low = z < cols - 1, z > 0

    def north(self, x):
        return (
            jnp.where(self.not_top, pltpu.roll(x, self.rows - 1, 0), 0.0),
            jnp.where(self.not_bottom, pltpu.roll(x, 1, 0), 0.0),
        )

    def level(self, x):
        return (
            jnp.where(self.not_high, pltpu.roll(x, self.cols - 1, 1), 0.0),
            jnp.where(self.not_low, pltpu.roll(x, 1, 1), 0.0),
        )


def sweep(sh, mid, nxt, prv, src, flow, visc, curv):
    u = [flow(k) for k in range(3)]
    w = visc()
    inv_v = 1.0 / (6.0 * w + 1.0)
    out = [None] * 5
    q_next, q_prev = nxt(3), prv(3)
    q = mid(3)
    qn, qs = sh.north(q)
    qu, qd = sh.level(q)
    grad = [q_next - q_prev, qn - qs, qu - qd]
    q_sum = (q_next + q_prev) + (qn + qs) + (qu + qd)
    div = None
    bend = None
    for c in range(3):
        v = mid(c)
        a, b = nxt(c), prv(c)
        n, s = sh.north(v)
        h, l = sh.level(v)
        total = (a + b) + (n + s) + (h + l)
        slope = [a - b, n - s, h - l]
        convect = u[0] * slope[0] + u[1] * slope[1] + u[2] * slope[2]
        out[c] = (src(c) + w * total + 0.5 * (convect - grad[c])) * inv_v
        div = slope[c] if div is None else div + slope[c]
        term = v * curv(c)
        bend = term if bend is None else bend + term
    out[3] = (src(3) + q_sum - 0.5 * div) * (1.0 / 7.0)
    m = mid(4)
    n, s = sh.north(m)
    h, l = sh.level(m)
    m_sum = (nxt(4) + prv(4)) + (n + s) + (h + l)
    out[4] = (src(4) + w * m_sum + 0.25 * bend) / (6.0 * w + 2.0)
    return out


def curvature(sh, u, a, b):
    n, s = sh.north(u)
    h, l = sh.level(u)
    return (a + b) + (n + s) + (h + l) - 6.0 * u


def over_slabs(count, body):
    body(0, True, False)

    @pl.loop(1, count - 1)
    def _(e):
        body(e, False, False)

    body(count - 1, False, True)


def first_kernel(ce, cn, cz, flags, start, source, flow, eddy, facep, facen, swept, curv, pdown, pup, cdown, cup):
    sh = Shifts(cn, cz)
    has_prev, has_next = flags[0], flags[1]

    def body(e, first, last):
        def before(ref, f, face_at):
            if first:
                return facep[face_at] * has_prev
            return ref[f, e - 1]

        def after(ref, f, face_at):
            if last:
                return facen[face_at] * has_next
            return ref[f, e + 1]

        for c in range(3):
            curv[c, e] = curvature(sh, flow[c, e], after(flow, c, 5 + c), before(flow, c, 5 + c))
        out = sweep(
            sh,
            lambda f: start[f, e],
            lambda f: after(start, f, f),
            lambda f: before(start, f, f),
            lambda f: source[f, e],
            lambda k: flow[k, e],
            lambda: 1.0 + eddy[e],
            lambda c: curv[c, e],
        )
        for f in range(5):
            swept[f, e] = out[f]

        for pack, coef, row, behind in ((pdown, cdown, 0, 1), (pup, cup, cn - 1, cn - 2)):
            def put(ref, at, line):
                ref[pl.ds(at * ce + e, 1), :] = line

            for f in range(5):
                put(pack, f, start[f, e, row : row + 1, :])
                put(pack, 9 + f, out[f][row : row + 1, :])
            for k in range(3):
                put(pack, 5 + k, flow[k, e, row : row + 1, :])
                put(coef, k, curv[k, e, row : row + 1, :])
            put(pack, 8, eddy[e, row : row + 1, :])
            put(coef, 3, flow[1, e, behind : behind + 1, :])
            put(coef, 4, eddy[e, behind : behind + 1, :])
            put(coef, 5, flow[0, e, behind : behind + 1, :])

    for pack, row in ((pdown, 0), (pup, cn - 1)):
        for f in range(8):
            pack[PACK * ce + f : PACK * ce + f + 1, :] = facep[f, row : row + 1, :] * has_prev
            pack[PACK * ce + 8 + f : PACK * ce + 9 + f, :] = facen[f, row : row + 1, :] * has_next
    over_slabs(ce, body)


def first_sweep(flags, start, source, flow, eddy, facep, facen):
    _, ce, cn, cz = start.shape
    pack = jax.ShapeDtypeStruct((PACK * ce + 16, cz), F32)
    coef = jax.ShapeDtypeStruct((EDGE * ce, cz), F32)
    return pl.pallas_call(
        functools.partial(first_kernel, ce, cn, cz),
        out_shape=(
            VMEM(start.shape, F32),
            VMEM(flow.shape, F32),
            pack,
            pack,
            coef,
            coef,
        ),
        in_specs=[whole(pltpu.SMEM)] + [whole()] * 6,
        out_specs=(whole(),) * 6,
        compiler_params=params(48),
        cost_estimate=cost(120 * start.size // 5, 20 << 20),
    )(flags, in_vmem(start), in_vmem(source), in_vmem(flow), in_vmem(eddy), facep, facen)


def rotor_terms(cells, row_of, high, low, turbine, sector, weight, count, blocks, acc):
    chunks = cells.shape[0]
    rows, width = high.shape
    cz = width // COMPS
    shift = cz.bit_length() - 1
    cell = cells[...]
    tur = turbine[...]
    owner = lax.shift_right_logical(tur * 5462, 16)
    key = owner * SECT + sector[...]
    slot = lax.broadcasted_iota(jnp.int32, cell.shape, 0) * LANES + lax.broadcasted_iota(jnp.int32, cell.shape, 1)
    live = jnp.where(slot < count, weight[...], 0.0)
    row = row_of(lax.shift_right_logical(cell, shift)).astype(F32).T
    level = jnp.bitwise_and(cell, cz - 1).astype(F32).T
    local = (tur - owner * TURB_DEV).astype(F32).T
    live = live.T
    lane_row = lax.broadcasted_iota(jnp.int32, (LANES, rows), 1).astype(F32)
    lane_level = lax.broadcasted_iota(jnp.int32, (LANES, cz), 1).astype(F32)
    lane = lax.broadcasted_iota(jnp.int32, (LANES, LANES), 1)
    lane_comp = lax.shift_right_logical(lane * 5462, 16)
    lane_tur = (lane - lane_comp * TURB_DEV).astype(F32)
    lane_key = lax.broadcasted_iota(jnp.int32, (blocks * SECT, LANES), 0)
    for k in range(chunks):

        @pl.when(k * LANES < count)
        def _(k=k):
            pick = (row[:, k : k + 1] == lane_row).astype(jnp.bfloat16)
            got = jnp.dot(pick, high[...], preferred_element_type=F32)
            got = got + jnp.dot(pick, low[...], preferred_element_type=F32)
            here = level[:, k : k + 1] == lane_level
            spread = jnp.zeros((LANES, LANES), F32)
            for c in range(COMPS):
                part = jnp.where(here, got[:, c * cz : (c + 1) * cz], 0.0)
                val = jnp.sum(part, axis=1, keepdims=True) * live[:, k : k + 1]
                spread = jnp.where(lane_comp == c, val, spread)
            spread = jnp.where(local[:, k : k + 1] == lane_tur, spread, 0.0)
            to = (lane_key == key[k : k + 1, :]).astype(F32)
            acc[...] += jnp.dot(to, spread, precision=lax.Precision.HIGHEST, preferred_element_type=F32)


def split(x):
    high = x.astype(jnp.bfloat16)
    return high, (x - high.astype(F32)).astype(jnp.bfloat16)


def second_kernel(
    ce, cn, cz, blocks,
    flags, count, swept, curv, source, flow, eddy, facep, facen, cells, turbine, sector, weight,
    final, edge_low, edge_high, grad,
    held, high, low, sems,
):
    sh = Shifts(cn, cz)
    has_prev, has_next = flags[0], flags[1]

    def body(e, first, last):
        def before(f):
            if first:
                return facep[f] * has_prev
            return swept[f, e - 1]

        def after(f):
            if last:
                return facen[f] * has_next
            return swept[f, e + 1]

        out = sweep(
            sh,
            lambda f: swept[f, e],
            after,
            before,
            lambda f: source[f, e],
            lambda k: flow[k, e],
            lambda: 1.0 + eddy[e],
            lambda c: curv[c, e],
        )
        u = flow[0, e]
        force = u * jnp.abs(u)
        at = pl.ds(pl.multiple_of(e * cn, cn), cn)
        for f in range(5):
            held[f, e] = out[f]
            edge_low[f, e] = out[f][0:SUB]
            edge_high[f, e] = out[f][cn - SUB : cn]
        for c in range(COMPS):
            hi, lo = split(out[c if c < 3 else 4] * force)
            high[at, c * cz : (c + 1) * cz] = hi
            low[at, c * cz : (c + 1) * cz] = lo

    over_slabs(ce, body)
    copy = pltpu.make_async_copy(held, final, sems.at[0])
    copy.start()
    grad[...] = jnp.zeros_like(grad)
    rotor_terms(cells, lambda r: r, high, low, turbine, sector, weight, count[0], blocks, grad)
    copy.wait()


def second_sweep(flags, count, swept, curv, source, flow, eddy, facep, facen, lists, blocks):
    _, ce, cn, cz = swept.shape
    edge = VMEM((5, ce, SUB, cz), F32)
    return pl.pallas_call(
        functools.partial(second_kernel, ce, cn, cz, blocks),
        out_shape=(
            jax.ShapeDtypeStruct(swept.shape, F32),
            edge,
            edge,
            jax.ShapeDtypeStruct((blocks * SECT, LANES), F32),
        ),
        in_specs=[whole(pltpu.SMEM)] * 2 + [whole()] * 11,
        out_specs=(whole(pl.ANY), whole(), whole(), whole()),
        scratch_shapes=[
            VMEM(swept.shape, F32),
            VMEM((ce * cn, COMPS * cz), jnp.bfloat16),
            VMEM((ce * cn, COMPS * cz), jnp.bfloat16),
            pltpu.SemaphoreType.DMA((1,)),
        ],
        compiler_params=params(48),
        cost_estimate=cost(140 * swept.size // 5, 20 << 20),
    )(flags, count, in_vmem(swept), in_vmem(curv), in_vmem(source), in_vmem(flow), in_vmem(eddy), facep, facen, *lists)


def one_way(sign, w, u1, f, s, inv_v, inv_m, bend=None):
    down = (w + (0.5 * sign) * u1) * inv_v
    out = [down * f[c] for c in range(3)]
    out[1] = out[1] - (0.5 * sign) * f[3] * inv_v
    out.append((f[3] - (0.5 * sign) * f[1]) * (1.0 / 7.0))
    m = w * f[4]
    if bend is not None:
        m = m + 0.25 * bend
    out.append(m * inv_m)
    return out


def edge_kernel(
    ce, cn, cz, blocks, copies_out,
    flags, count, facep, facen, own_low, own_high, coef_low, coef_high, got_prev, got_next,
    edge_low, edge_high, cells, turbine, sector, weight, grad, final_in,
    final, chunks,
    low_out, high_out, high, low, acc, sems,
):
    z = lax.broadcasted_iota(jnp.int32, (ce, cz), 1)
    r = lax.broadcasted_iota(jnp.int32, (ce, cz), 0)
    sub = lax.broadcasted_iota(jnp.int32, (SUB, cz), 0)
    sides = (
        (-1.0, 0, own_low, coef_low, got_prev, flags[2], edge_low, low_out, 0),
        (1.0, cn - 1, own_high, coef_high, got_next, flags[3], edge_high, high_out, cn - SUB),
    )
    waits = []
    for at_side, (sign, row, own, coef, got, exists, edge, out_ref, place) in enumerate(sides):
        def plane(ref, f):
            return ref[f * ce : (f + 1) * ce, :]

        v0 = [plane(own, f) for f in range(5)]
        u = [plane(own, 5 + k) for k in range(3)]
        w = 1.0 + plane(own, 8)
        p1 = [plane(own, 9 + f) for f in range(5)]
        xv = [plane(got, f) for f in range(5)]
        xu = [plane(got, 5 + k) for k in range(3)]
        xw = 1.0 + plane(got, 8)
        xp = [plane(got, 9 + f) for f in range(5)]
        curv = [plane(coef, k) for k in range(3)]
        inv_v, inv_m = 1.0 / (6.0 * w + 1.0), 1.0 / (6.0 * w + 2.0)
        bend = v0[0] * xu[0] + v0[1] * xu[1] + v0[2] * xu[2]
        delta = one_way(sign, w, u[1], xv, None, inv_v, inv_m, bend)
        xinv_v, xinv_m = 1.0 / (6.0 * xw + 1.0), 1.0 / (6.0 * xw + 2.0)
        xbend = xv[0] * u[0] + xv[1] * u[1] + xv[2] * u[2]
        back = one_way(-sign, xw, xu[1], v0, None, xinv_v, xinv_m, xbend)
        x1 = [(xp[f] + back[f]) * exists for f in range(5)]
        ends = []
        for face, has, first in ((facep, flags[0], 0), (facen, flags[1], 8)):
            fv = [face[f, row : row + 1, :] * has for f in range(5)]
            fu = face[6, row : row + 1, :] * has
            fw = 1.0 + face[8, row : row + 1, :] * has
            base = PACK * ce + first
            hv = [got[base + f : base + f + 1, :] for f in range(5)]
            hu = [got[base + 5 + k : base + 6 + k, :] for k in range(3)]
            fb = fv[0] * hu[0] + fv[1] * hu[1] + fv[2] * hu[2]
            line = one_way(sign, fw, fu, hv, None, 1.0 / (6.0 * fw + 1.0), 1.0 / (6.0 * fw + 2.0), fb)
            ends.append([x * has for x in line])
        total, slope0, slope2 = [], [], []
        for f in range(5):
            d = delta[f]
            after = jnp.where(r < ce - 1, pltpu.roll(d, ce - 1, 0), ends[1][f])
            before = jnp.where(r > 0, pltpu.roll(d, 1, 0), ends[0][f])
            up = jnp.where(z < cz - 1, pltpu.roll(d, cz - 1, 1), 0.0)
            down = jnp.where(z > 0, pltpu.roll(d, 1, 1), 0.0)
            total.append((after + before) + (up + down))
            slope0.append(after - before)
            slope2.append(up - down)
        full = [p1[c] + delta[c] for c in range(3)]
        bend = full[0] * xu[0] + full[1] * xu[1] + full[2] * xu[2]
        bend = bend + delta[0] * curv[0] + delta[1] * curv[1] + delta[2] * curv[2]
        add = one_way(sign, w, u[1], x1, None, inv_v, inv_m, bend)
        press = (slope0[3], None, slope2[3])
        for c in range(3):
            more = w * total[c] + 0.5 * (u[0] * slope0[c] + u[2] * slope2[c])
            if press[c] is not None:
                more = more - 0.5 * press[c]
            add[c] = add[c] + more * inv_v
        add[3] = add[3] + (total[3] - 0.5 * (slope0[0] + slope2[2])) * (1.0 / 7.0)
        add[4] = add[4] + w * total[4] * inv_m
        ru1, rw, ru0 = plane(coef, 3), 1.0 + plane(coef, 4), plane(coef, 5)
        rinv_v, rinv_m = 1.0 / (6.0 * rw + 1.0), 1.0 / (6.0 * rw + 2.0)
        behind = one_way(sign, rw, ru1, delta, None, rinv_v, rinv_m)
        near, far = (0, 1) if at_side == 0 else (SUB - 1, SUB - 2)
        for f in range(5):
            for e in range(ce):
                rows = jnp.where(
                    sub == near, add[f][e : e + 1, :], jnp.where(sub == far, behind[f][e : e + 1, :], 0.0)
                )
                out_ref[f, e] = edge[f, e] + rows
        copy = pltpu.make_async_copy(out_ref, final.at[:, :, pl.ds(place, SUB), :], sems.at[at_side])
        copy.start()
        waits.append(copy)
        for source_row, u0, values in ((0, u[0], add), (1, ru0, behind)):
            force = u0 * jnp.abs(u0)
            at = (2 * at_side + source_row) * ce
            for c in range(COMPS):
                hi, lo = split(values[c if c < 3 else 4] * force)
                high[at : at + ce, c * cz : (c + 1) * cz] = hi
                low[at : at + ce, c * cz : (c + 1) * cz] = lo

    shift = cn.bit_length() - 1

    def row_of(line):
        n = jnp.bitwise_and(line, cn - 1)
        e = lax.shift_right_logical(line, shift)
        slot = jnp.where(n == 0, 0, jnp.where(n == 1, 1, jnp.where(n == cn - 1, 2, jnp.where(n == cn - 2, 3, -ce))))
        return slot * ce + e

    acc[...] = grad[...]
    rotor_terms(cells, row_of, high, low, turbine, sector, weight, count[0], blocks, acc)
    for east in range(copies_out):
        chunks[east] = acc[...]
    for copy in waits:
        copy.wait()


def edges(flags, count, faces, packs, coefs, gots, tiles, lists, grad, final, blocks, size):
    _, ce, cn, cz = final.shape
    args = (flags, count, *faces, *packs, *coefs, *gots, *tiles, *lists, grad, final)
    tile = VMEM((5, ce, SUB, cz), F32)
    part = VMEM((4 * ce, COMPS * cz), jnp.bfloat16)
    return pl.pallas_call(
        functools.partial(edge_kernel, ce, cn, cz, blocks, size),
        out_shape=(
            jax.ShapeDtypeStruct(final.shape, F32),
            jax.ShapeDtypeStruct((size, blocks * SECT, LANES), F32),
        ),
        in_specs=[whole(pltpu.SMEM)] * 2 + [whole()] * (len(args) - 3) + [whole(pl.ANY)],
        out_specs=(whole(pl.ANY), whole()),
        scratch_shapes=[
            tile,
            tile,
            part,
            part,
            VMEM((blocks * SECT, LANES), F32),
            pltpu.SemaphoreType.DMA((2,)),
        ],
        input_output_aliases={len(args) - 1: 0},
        compiler_params=params(32),
        cost_estimate=cost(1 << 24, 4 << 20),
    )(*args)


def sum_kernel(parts, out):
    total = jnp.sum(parts[...], axis=0)
    for c in range(COMPS):
        out[c] = total[:, c * TURB_DEV : (c + 1) * TURB_DEV]


def sum_parts(parts):
    return pl.pallas_call(
        sum_kernel,
        out_shape=jax.ShapeDtypeStruct((COMPS, SECT, TURB_DEV), F32),
        in_specs=[whole()],
        out_specs=whole(),
        cost_estimate=cost(parts.size, parts.size * 4),
    )(parts)


def shards(
    adjoint_start,
    adjoint_source,
    base_flow,
    eddy_visc,
    rotor_count,
    rotor_cell,
    rotor_turbine,
    rotor_sector,
    rotor_weight,
):
    _, ce, cn, cz = adjoint_start.shape
    n_east, n_north = lax.axis_size("east"), lax.axis_size("north")
    east, north = lax.axis_index("east"), lax.axis_index("north")
    flags = jnp.stack([east > 0, east < n_east - 1, north > 0, north < n_north - 1]).astype(F32)
    count = rotor_count.reshape(1)
    slots = rotor_cell.shape[-1]
    lists = [x.reshape(slots // LANES, LANES) for x in (rotor_cell, rotor_turbine, rotor_sector, rotor_weight)]

    facing = jnp.where(east == 0, ce - 1, 0).astype(jnp.int32)
    if n_east == 2:
        low = high = east_face(facing, adjoint_start, base_flow, eddy_visc)
    else:
        low, high = (
            east_face(jnp.asarray(e, jnp.int32), adjoint_start, base_flow, eddy_visc) for e in (0, ce - 1)
        )
    faces = swap_faces(low, high, n_east)
    swept, curv, pack_low, pack_high, coef_low, coef_high = first_sweep(
        flags, adjoint_start, adjoint_source, base_flow, eddy_visc, *faces
    )
    up = [(i, i + 1) for i in range(n_north - 1)]
    down = [(i + 1, i) for i in range(n_north - 1)]
    got_prev = lax.ppermute(pack_high, "north", up)
    got_next = lax.ppermute(pack_low, "north", down)
    if n_east == 2:
        low = high = lax.dynamic_index_in_dim(swept, facing, 1, keepdims=False)
    else:
        low, high = swept[:, 0], swept[:, ce - 1]
    faces_swept = swap_faces(low, high, n_east)
    final, edge_low, edge_high, grad = second_sweep(
        flags, count, swept, curv, adjoint_source, base_flow, eddy_visc, *faces_swept, lists, n_north
    )
    final, chunks = edges(
        flags, count, faces, (pack_low, pack_high), (coef_low, coef_high), (got_prev, got_next),
        (edge_low, edge_high), lists, grad, final, n_north, n_east,
    )
    chunks = chunks.reshape(n_east * n_north, SECT, LANES)
    parts = lax.all_to_all(chunks, ("east", "north"), 0, 0, tiled=True)
    return (final, sum_parts(parts))


def solution(mesh):
    placed = (
        P(None, "east", "north", None),
        P(None, "east", "north", None),
        P(None, "east", "north", None),
        P("east", "north", None),
        P("east", "north"),
        P("east", "north", None),
        P("east", "north", None),
        P("east", "north", None),
        P("east", "north", None),
    )
    return jax.shard_map(
        shards,
        mesh=mesh,
        in_specs=placed,
        out_specs=(P(None, "east", "north", None), P(None, None, "north")),
        check_vma=False,
    )
```

time: 188 us -> 77.8 us (0.41)
  local copies, waits for them, and re-layouts: 56 us -> 10.7 us
  other arithmetic: 45.7 us -> 0.67 us
  Pallas kernels: 0 us -> 28.6 us
  starting transfers between devices: 29.4 us -> 7.21 us
  blocking collectives: 45.3 us -> 27.5 us
  waiting for transfers between devices: 7.78 us -> 1.49 us
    psum x1 -> x0, blocking collectives: 45.3 us -> none  [shards(): summed = lax.psum(partial_grad, ('east', 'north'))]
    concatenate x2 -> x0, local copies, waits for them, and re-layouts: 30.3 us -> none  [the longest x1 30.3 us: relax(): return jnp.concatenate([velocity, pressure[None], eddy_new[None]], axis=0)]
    pallas_call x0 -> x5, Pallas kernels: none -> 28.6 us  [the longest x1 10.1 us: east_face(): pl.pallas_call(face_kernel, out_shape=jax.ShapeDtypeStruct((9, cn, cz), F...]
    all_to_all x0 -> x1, blocking collectives: none -> 27.5 us  [shards(): parts = lax.all_to_all(chunks, ('east', 'north'), 0, 0, tiled=True)]
    concatenate x9 -> x0, other arithmetic: 22.8 us -> none  [the longest x5 15.8 us: extended(): shard = jnp.concatenate([before, shard, after], axis=dim)]
    ppermute x12 -> x4, starting transfers between devices: 29.4 us -> 7.21 us  [the longest x1 5.41 us: shards(): got_prev = lax.ppermute(pack_high, 'north', up)]
    gather x2 -> x0, local copies, waits for them, and re-layouts: 16.6 us -> none  [the longest x1 10.5 us: shards(): values = flat_state[:, cells]]
    unnamed x37 -> x40, local copies, waits for them, and re-layouts: 3.57 us -> 10.7 us
  transfers between devices with their start and end apart: 12 -> 4, of which waited for: 3 -> 2; matrix products, arithmetic and copies ran while one was open for 11% -> 1% of each run, Pallas kernels for 0% -> 10%
where the time goes in v1:
time: 77.8 us; the launch traced here: 77.7 us
  Pallas kernels  28.6 us (37%)
  blocking collectives  27.5 us (35%)
  local copies, waits for them, and re-layouts  10.7 us (14%)
  starting transfers between devices  7.21 us (9%)
  between operations  1.53 us (2%)
  waiting for transfers between devices  1.49 us (2%)
    all_to_all x1, blocking collectives, shards(): parts = lax.all_to_all(chunks, ('east', 'north'), 0, 0, tiled=True)  27.5 us
    unnamed x40, local copies, waits for them, and re-layouts  10.7 us
    pallas_call x1, Pallas kernels, east_face(): pl.pallas_call(face_kernel, out_shape=jax.ShapeDtypeStruct((9, cn, cz), F...  10.1 us
    pallas_call x1, Pallas kernels, second_sweep(): pl.pallas_call(functools.partial(second_kernel, ce, cn, cz, blocks), out_...  7.67 us
    pallas_call x1, Pallas kernels, first_sweep(): pl.pallas_call(functools.partial(first_kernel, ce, cn, cz), out_shape=(VM...  6.08 us
    ppermute x1, starting transfers between devices, shards(): got_prev = lax.ppermute(pack_high, 'north', up)  5.41 us
    pallas_call x1, Pallas kernels, edges(): pl.pallas_call(functools.partial(edge_kernel, ce, cn, cz, blocks, size),...  3.14 us
    pallas_call x1, Pallas kernels, sum_parts(): pl.pallas_call(sum_kernel, out_shape=jax.ShapeDtypeStruct((COMPS, SECT, T...  1.61 us
  transfers between devices with their start and end apart: 4, of which 2 were waited for; matrix products, arithmetic and copies ran while one was open for 1% of the time, Pallas kernels for 10%

profile of v1, /device:TPU:0, one launch (start us, length us, event | category | flops | bytes accessed | tf_op | source)
XLA Modules:
  0.0 77.7 jit_solution(3330591444007620839)
XLA Ops:
  0.7 10.1 %shard_map.104 = f32[9,32,256]{2,1,0:T(8,128)} custom-call(s32[1]{0:T(128)} %bitcast.5.at, f32[5,16,32,256]{3,2,1,0:T(8,128)} %start.3, f32[3,16,32,256]{3,2,1,0:T(8,128)} %flow.5, f32[16,32,256]{2,1,0:T(8,128)} %eddy.5), custom_call_target="tpu_custom_call" | custom-call | bytes 589824 | tf_op jit(solution)/shard_map/pallas_call | solution.py:52
  10.7 0.5 collective-permute-start
  11.3 0.7 add_convert_fusion.flags
  11.9 0.7 collective-permute-done.facep.facen
  12.7 0.7 copy-done.4
  13.4 1.7 %copy-done.1 = f32[5,16,32,256]{3,2,1,0:T(8,128)S(1)} copy-done((f32[5,16,32,256]{3,2,1,0:T(8,128)S(1)}, f32[5,16,32,256]{3,2,1,0:T(8,128)}, u32[]{:S(2)}) %copy-start.1) | copy-done | bytes 2621464
  15.1 1.7 %copy-done.3 = f32[5,16,32,256]{3,2,1,0:T(8,128)S(1)} copy-done((f32[5,16,32,256]{3,2,1,0:T(8,128)S(1)}, f32[5,16,32,256]{3,2,1,0:T(8,128)}, u32[]{:S(2)}) %copy-start.3) | copy-done | bytes 2621464
  16.9 6.1 %shard_map.105 = (f32[5,16,32,256]{3,2,1,0:T(8,128)S(1)}, f32[3,16,32,256]{3,2,1,0:T(8,128)S(1)}, f32[240,256]{1,0:T(8,128)}, f32[240,256]{1,0:T(8,128)}, f32[96,256]{1,0:T(8,128)}, /*index=5*/f32[96,256]{1,0:T(8,128)}) custom-call(f32[4]{0:T(128)} %add_convert_fusion.flags, f32[5,16,32,256]{3,2,1,0:T(8,128)S(1)} %copy-done.3, ...), custom_call_target="tpu_custom_call" | custom-call | flops 15728640 | bytes 20971520 | tf_op jit(solution)/shard_map/pallas_call | solution.py:198
  23.0 1.3 %collective-permute-start.2 = (f32[240,256]{1,0:T(8,128)}, f32[240,256]{1,0:T(8,128)S(1)}, u32[]{:S(2)}, u32[]{:S(2)}) collective-permute-start(f32[240,256]{1,0:T(8,128)} %get-tuple-element.14.own_low), channel_id=1, source_target_pairs={{1,0},{2,1},{3,2},{4,3},{5,4},{6,5},{7,6},{8,7},{9,8},{10,9},{11,1... | collective-permute-start | bytes 737288 | tf_op jit(solution)/shard_map/ppermute | solution.py:526
  24.2 5.4 %collective-permute-start.1 = (f32[240,256]{1,0:T(8,128)}, f32[240,256]{1,0:T(8,128)S(1)}, u32[]{:S(2)}, u32[]{:S(2)}) collective-permute-start(f32[240,256]{1,0:T(8,128)} %get-tuple-element.15.own_high), channel_id=1, source_target_pairs={{0,1},{1,2},{2,3},{3,4},{4,5},{5,6},{6,7},{7,8},{8,9},{9,10},{10,1... | collective-permute-start | bytes 737288 | tf_op jit(solution)/shard_map/ppermute | solution.py:525
  29.7 0.0 copy-start.7
  29.7 1.5 %copy-done.7 = f32[5,16,32,256]{3,2,1,0:T(8,128)} copy-done((f32[5,16,32,256]{3,2,1,0:T(8,128)}, f32[5,16,32,256]{3,2,1,0:T(8,128)S(1)}, u32[]{:S(2)}) %copy-start.7) | copy-done | bytes 2621464
  31.2 0.0 collective-permute-start.3
  31.8 0.7 collective-permute-done.3.facep.facen
  32.6 0.7 copy-done.19
  33.2 1.7 %copy-done.2 = f32[5,16,32,256]{3,2,1,0:T(8,128)S(1)} copy-done((f32[5,16,32,256]{3,2,1,0:T(8,128)S(1)}, f32[5,16,32,256]{3,2,1,0:T(8,128)}, u32[]{:S(2)}) %copy-start.2) | copy-done | bytes 2621464
  35.0 1.7 %copy-done.8 = f32[5,16,32,256]{3,2,1,0:T(8,128)S(1)} copy-done((f32[5,16,32,256]{3,2,1,0:T(8,128)S(1)}, f32[5,16,32,256]{3,2,1,0:T(8,128)}, u32[]{:S(2)}) %copy-start.8) | copy-done | bytes 2621464
  36.7 0.0 copy-start.12
  36.8 0.0 copy-start.14
  36.8 0.0 copy-start.15
  36.8 0.0 copy-start.16
  36.8 0.0 copy-start.17
  36.8 7.7 %shard_map.106 = (f32[5,16,32,256]{3,2,1,0:T(8,128)}, f32[5,16,8,256]{3,2,1,0:T(8,128)S(1)}, f32[5,16,8,256]{3,2,1,0:T(8,128)S(1)}, f32[128,128]{1,0:T(8,128)}) custom-call(f32[4]{0:T(128)} %add_convert_fusion.flags, s32[1]{0:T(128)} %bitcast.13.count, f32[5,16,32,256]{3,2,1,0:T(8,128)S(1)} %copy-done.8, f32[3,16,32,256]{3,2,1,0:T(8,128)S(1)} %get-tuple-element.19.curv, ...), custom_call_target="tpu_custom_call" | custom-call | flops 18350080 | bytes 20971520 | tf_op jit(solution)/shard_map/pallas_call | solution.py:312
  44.5 0.0 collective-permute-done.2.got_next
  44.5 0.0 collective-permute-done.1.got_prev
  44.5 0.0 copy-done.5
  44.5 0.0 copy-done.9
  44.5 0.0 copy-done.10
  44.6 0.8 %copy-done.13 = f32[128,128]{1,0:T(8,128)S(1)} copy-done((f32[128,128]{1,0:T(8,128)S(1)}, f32[128,128]{1,0:T(8,128)}, u32[]{:S(2)}) %copy-start.13) | copy-done | bytes 65560
  45.5 3.1 %shard_map.107 = (f32[5,16,32,256]{3,2,1,0:T(8,128)}, f32[2,128,128]{2,1,0:T(8,128)S(1)}) custom-call(f32[4]{0:T(128)S(1)} %copy-done.18, s32[1]{0:T(128)} %bitcast.14.count, f32[9,32,256]{2,1,0:T(8,128)S(1)} %copy-done.5, f32[9,32,256]{2,1,0:T(8,128)S(1)} %copy-done.5, f32[240,256]{1,0:T(8,128)S(1)} %copy-done.9, ...), custom_call_target="tpu_custom_call", output_to_operand_aliasing={{0}: (17, {})} | custom-call | flops 16777216 | bytes 4194304 | tf_op jit(solution)/shard_map/pallas_call | solution.py:455
  48.6 27.5 %all_to_all.5.parts = f32[32,8,128]{2,1,0:T(8,128)} all-to-all(f32[32,8,128]{2,1,0:T(8,128)S(1)} %bitcast.15), channel_id=1, replica_groups=mesh['east'=2,'north'=16] {'east','north'}, dimensions={0} | all-to-all | bytes 262144 | tf_op jit(solution)/shard_map/all_to_all | solution.py:540
  76.1 1.6 %shard_map.108 = f32[4,8,12]{2,1,0:T(8,128)} custom-call(f32[32,8,128]{2,1,0:T(8,128)} %all_to_all.5.parts), custom_call_target="tpu_custom_call" | custom-call | flops 32768 | bytes 131072 | tf_op jit(solution)/shard_map/pallas_call | solution.py:484
  (24 shorter events, 0.1 us)
Async XLA Ops:
  0.6 12.8 %copy-start.6 = (f32[16,32,256]{2,1,0:T(8,128)S(1)}, f32[16,32,256]{2,1,0:T(8,128)}, u32[]{:S(2)}) copy-start(f32[16,32,256]{2,1,0:T(8,128)} %eddy.5) | copy-start | bytes 1572868
  0.6 12.7 %copy-start = (f32[3,16,32,256]{3,2,1,0:T(8,128)S(1)}, f32[3,16,32,256]{3,2,1,0:T(8,128)}, u32[]{:S(2)}) copy-start(f32[3,16,32,256]{3,2,1,0:T(8,128)} %flow.5) | copy-start | bytes 4718596
  10.7 1.9 %collective-permute-start = (f32[9,32,256]{2,1,0:T(8,128)}, f32[9,32,256]{2,1,0:T(8,128)S(1)}, u32[]{:S(2)}, u32[]{:S(2)}) collective-permute-start(f32[9,32,256]{2,1,0:T(8,128)} %shard_map.104), channel_id=1, source_target_pairs={{0,16},{16,0},{1,17},{17,1},{2,18},{18,2},{3,19},{19,3},{4,20},{20... | collective-permute-start | bytes 884744 | tf_op jit(solution)/shard_map/ppermute | solution.py:64
  12.7 0.7 copy-start.4
  13.4 1.7 %copy-start.1 = (f32[5,16,32,256]{3,2,1,0:T(8,128)S(1)}, f32[5,16,32,256]{3,2,1,0:T(8,128)}, u32[]{:S(2)}) copy-start(f32[5,16,32,256]{3,2,1,0:T(8,128)} %source.3) | copy-start | bytes 7864324
  15.1 1.7 %copy-start.3 = (f32[5,16,32,256]{3,2,1,0:T(8,128)S(1)}, f32[5,16,32,256]{3,2,1,0:T(8,128)}, u32[]{:S(2)}) copy-start(f32[5,16,32,256]{3,2,1,0:T(8,128)} %start.3) | copy-start | bytes 7864324
  23.0 21.5 %collective-permute-start.2 = (f32[240,256]{1,0:T(8,128)}, f32[240,256]{1,0:T(8,128)S(1)}, u32[]{:S(2)}, u32[]{:S(2)}) collective-permute-start(f32[240,256]{1,0:T(8,128)} %get-tuple-element.14.own_low), channel_id=1, source_target_pairs={{1,0},{2,1},{3,2},{4,3},{5,4},{6,5},{7,6},{8,7},{9,8},{10,9},{11,1... | collective-permute-start | bytes 737288 | tf_op jit(solution)/shard_map/ppermute | solution.py:526
  24.2 20.3 %collective-permute-start.1 = (f32[240,256]{1,0:T(8,128)}, f32[240,256]{1,0:T(8,128)S(1)}, u32[]{:S(2)}, u32[]{:S(2)}) collective-permute-start(f32[240,256]{1,0:T(8,128)} %get-tuple-element.15.own_high), channel_id=1, source_target_pairs={{0,1},{1,2},{2,3},{3,4},{4,5},{5,6},{6,7},{7,8},{8,9},{9,10},{10,1... | collective-permute-start | bytes 737288 | tf_op jit(solution)/shard_map/ppermute | solution.py:525
  29.7 1.5 %copy-start.7 = (f32[5,16,32,256]{3,2,1,0:T(8,128)}, f32[5,16,32,256]{3,2,1,0:T(8,128)S(1)}, u32[]{:S(2)}) copy-start(f32[5,16,32,256]{3,2,1,0:T(8,128)S(1)} %get-tuple-element.18.swept) | copy-start | bytes 7864324
  31.2 1.4 %collective-permute-start.3 = (f32[5,32,256]{2,1,0:T(8,128)S(1)}, f32[5,32,256]{2,1,0:T(8,128)S(1)}, u32[]{:S(2)}, u32[]{:S(2)}) collective-permute-start(f32[5,32,256]{2,1,0:T(8,128)S(1)} %dynamic-slice_bitcast_fusion), channel_id=1, source_target_pairs={{0,16},{16,0},{1,17},{17,1},{2,18},{18,2},{3,19},{19,3},{4,20},{20... | collective-permute-start | bytes 491528 | tf_op jit(solution)/shard_map/ppermute | solution.py:64
  32.6 0.7 copy-start.19
  33.2 1.7 %copy-start.2 = (f32[5,16,32,256]{3,2,1,0:T(8,128)S(1)}, f32[5,16,32,256]{3,2,1,0:T(8,128)}, u32[]{:S(2)}) copy-start(f32[5,16,32,256]{3,2,1,0:T(8,128)} %source.3) | copy-start | bytes 7864324
  35.0 1.7 %copy-start.8 = (f32[5,16,32,256]{3,2,1,0:T(8,128)S(1)}, f32[5,16,32,256]{3,2,1,0:T(8,128)}, u32[]{:S(2)}) copy-start(f32[5,16,32,256]{3,2,1,0:T(8,128)} %copy-done.7) | copy-start | bytes 7864324
  36.7 7.8 %copy-start.5 = (f32[9,32,256]{2,1,0:T(8,128)S(1)}, f32[9,32,256]{2,1,0:T(8,128)}, u32[]{:S(2)}) copy-start(f32[9,32,256]{2,1,0:T(8,128)} %copy-done.4) | copy-start | bytes 884740
  36.7 7.8 %copy-start.9 = (f32[240,256]{1,0:T(8,128)S(1)}, f32[240,256]{1,0:T(8,128)}, u32[]{:S(2)}) copy-start(f32[240,256]{1,0:T(8,128)} %get-tuple-element.14.own_low) | copy-start | bytes 737284
  36.7 7.8 %copy-start.10 = (f32[240,256]{1,0:T(8,128)S(1)}, f32[240,256]{1,0:T(8,128)}, u32[]{:S(2)}) copy-start(f32[240,256]{1,0:T(8,128)} %get-tuple-element.15.own_high) | copy-start | bytes 737284
  36.7 7.8 %copy-start.11 = (f32[96,256]{1,0:T(8,128)S(1)}, f32[96,256]{1,0:T(8,128)}, u32[]{:S(2)}) copy-start(f32[96,256]{1,0:T(8,128)} %get-tuple-element.16.coef_low) | copy-start | bytes 294916
  36.7 7.8 %copy-start.12 = (f32[96,256]{1,0:T(8,128)S(1)}, f32[96,256]{1,0:T(8,128)}, u32[]{:S(2)}) copy-start(f32[96,256]{1,0:T(8,128)} %get-tuple-element.17.coef_high) | copy-start | bytes 294916
  36.8 7.8 %copy-start.14 = (s32[1,1,1024]{2,1,0:T(1,128)S(1)}, s32[1,1,1024]{2,1,0:T(1,128)}, u32[]{:S(2)}) copy-start(s32[1,1,1024]{2,1,0:T(1,128)} %param.14) | copy-start | bytes 12292
  36.8 7.8 %copy-start.15 = (s32[1,1,1024]{2,1,0:T(1,128)S(1)}, s32[1,1,1024]{2,1,0:T(1,128)}, u32[]{:S(2)}) copy-start(s32[1,1,1024]{2,1,0:T(1,128)} %param.15) | copy-start | bytes 12292
  36.8 7.8 %copy-start.16 = (s32[1,1,1024]{2,1,0:T(1,128)S(1)}, s32[1,1,1024]{2,1,0:T(1,128)}, u32[]{:S(2)}) copy-start(s32[1,1,1024]{2,1,0:T(1,128)} %param.16) | copy-start | bytes 12292
  36.8 7.8 %copy-start.17 = (f32[1,1,1024]{2,1,0:T(1,128)S(1)}, f32[1,1,1024]{2,1,0:T(1,128)}, u32[]{:S(2)}) copy-start(f32[1,1,1024]{2,1,0:T(1,128)} %param.17) | copy-start | bytes 12292
  36.8 7.8 %copy-start.18 = (f32[4]{0:T(128)S(1)}, f32[4]{0:T(128)}, u32[]{:S(2)}) copy-start(f32[4]{0:T(128)} %add_convert_fusion.flags) | copy-start | bytes 52
  44.6 0.8 %copy-start.13 = (f32[128,128]{1,0:T(8,128)S(1)}, f32[128,128]{1,0:T(8,128)}, u32[]{:S(2)}) copy-start(f32[128,128]{1,0:T(8,128)} %get-tuple-element.22.grad) | copy-start | bytes 196612

commit v2 on v0

v2 whole, which is shorter than its diff:
```python
import functools

import jax
import jax.numpy as jnp
from jax import lax
from jax.experimental import pallas as pl
from jax.experimental.pallas import tpu as pltpu
from jax.sharding import PartitionSpec as P

SECT = 8
TURB_DEV = 12
COMPS = 4
LANES = 128
SUB = 8
PAD = 8
PACK = 14
FACE = 22
EDGE = 9
ITEM = 8
BLOCK = 256
VMEM = pltpu.VMEM
F32 = jnp.float32
BF16 = jnp.bfloat16


def whole(space=VMEM):
    return pl.BlockSpec(memory_space=space)


def shape(*dims):
    return jax.ShapeDtypeStruct(dims, F32)


def params(mib):
    return pltpu.CompilerParams(vmem_limit_bytes=mib << 20)


def cost(flops, size):
    return pl.CostEstimate(flops=flops, bytes_accessed=size, transcendentals=0)


class Copies:
    def __init__(self, sems):
        self.sems, self.used = sems, 0

    def take(self, *pairs):
        first = self.used
        self.used += len(pairs)
        return first, pairs

    def made(self, taken):
        first, pairs = taken
        return [pltpu.make_async_copy(s, d, self.sems.at[first + k]) for k, (s, d) in enumerate(pairs)]

    def start(self, taken):
        for c in self.made(taken):
            c.start()

    def wait(self, taken):
        for c in self.made(taken):
            c.wait()


def one_way(k, sign, w, u, f, inv_v, inv_m, bend=None):
    pull = (w + (0.5 * sign) * u) * inv_v
    out = [pull * f[c] for c in range(3)]
    out[k] = out[k] - (0.5 * sign) * f[3] * inv_v
    out.append((f[3] - (0.5 * sign) * f[k]) * (1.0 / 7.0))
    m = w * f[4]
    if bend is not None:
        m = m + 0.25 * bend
    out.append(m * inv_m)
    return out


def inverses(w):
    return 1.0 / (6.0 * w + 1.0), 1.0 / (6.0 * w + 2.0)


def dot3(a, b):
    return a[0] * b[0] + a[1] * b[1] + a[2] * b[2]


def plane_shifts(rows, cols):
    r = lax.broadcasted_iota(jnp.int32, (rows, cols), 0)
    z = lax.broadcasted_iota(jnp.int32, (rows, cols), 1)

    def east(x, before=0.0, after=0.0):
        return (
            jnp.where(r < rows - 1, pltpu.roll(x, rows - 1, 0), after),
            jnp.where(r > 0, pltpu.roll(x, 1, 0), before),
        )

    def level(x):
        return (
            jnp.where(z < cols - 1, pltpu.roll(x, cols - 1, 1), 0.0),
            jnp.where(z > 0, pltpu.roll(x, 1, 1), 0.0),
        )

    return east, level


def ends_kernel(cn, n_faces, at, start, flow, *refs):
    outs, tiles_v, tiles_u, sems = refs[:n_faces], *refs[n_faces:]
    copies = Copies(sems)
    taken = []
    for i in range(n_faces):
        e = at[2 * i]
        pairs = []
        for side, first in enumerate((0, cn - SUB)):
            pairs.append((start.at[:, e, pl.ds(first, SUB)], tiles_v.at[i, side]))
            pairs.append((flow.at[:, e, pl.ds(first, SUB)], tiles_u.at[i, side]))
        taken.append(copies.take(*pairs))
        copies.start(taken[-1])
    for i, out in enumerate(outs):
        copies.wait(taken[i])
        for side, row in enumerate((0, SUB - 1)):
            for f in range(8):
                tile = tiles_v[i, side, f] if f < 5 else tiles_u[i, side, f - 5]
                out[side * 8 + f : side * 8 + f + 1, :] = tile[row : row + 1]


def row_ends(at, start, flow, n_faces):
    _, ce, cn, cz = start.shape
    return pl.pallas_call(
        functools.partial(ends_kernel, cn, n_faces),
        out_shape=[shape(16, cz)] * n_faces,
        in_specs=[whole(pltpu.SMEM)] + [whole(pltpu.HBM)] * 2,
        out_specs=[whole()] * n_faces,
        scratch_shapes=[
            VMEM((n_faces, 2, 5, SUB, cz), F32),
            VMEM((n_faces, 2, 3, SUB, cz), F32),
            pltpu.SemaphoreType.DMA((4 * n_faces,)),
        ],
        compiler_params=params(60),
        cost_estimate=cost(0, 1 << 16),
    )(at, start, flow)


def pack_kernel(ce, cn, cz, n_faces, at, flags, endp, endn, start, source, flow, eddy, *refs):
    packs, refs = refs[:2], refs[2:]
    faces, refs = refs[:n_faces], refs[n_faces:]
    tiles_v, tiles_u, tiles_s, tiles_e, sems = refs
    has = [flags[k].astype(F32) for k in range(2)]
    copies = Copies(sems)
    sides = ((0, 0, 1, -1.0), (cn - SUB, SUB - 1, SUB - 2, 1.0))
    needed = []
    for side, (first, _, _, _) in enumerate(sides):
        pairs = []
        for h in range(2):
            cut = (pl.ds(first, SUB), pl.ds(h * LANES, LANES))
            pairs += [
                (start.at[(slice(None), slice(None)) + cut], tiles_v.at[side, :, :, h]),
                (flow.at[(slice(None), slice(None)) + cut], tiles_u.at[side, :, :, h]),
                (eddy.at[(slice(None),) + cut], tiles_e.at[side, 0, :, h]),
                (source.at[(slice(None), slice(None)) + cut], tiles_s.at[side, :, :, h]),
            ]
        needed.append(copies.take(*pairs))
        copies.start(needed[-1])
    later = []
    for i in range(n_faces):
        near, far, face = at[2 * i], at[2 * i + 1], faces[i]
        taken = copies.take(
            (start.at[:, near], face.at[0:5]),
            (flow.at[:, near], face.at[5:8]),
            (eddy.at[near], face.at[8]),
            (source.at[:, near], face.at[9:14]),
            (start.at[:, far], face.at[14:19]),
            (flow.at[:, far], face.at[19:22]),
        )
        copies.start(taken)
        later.append(taken)
    east, level = plane_shifts(ce, cz)

    def line(ref, side, f, row):
        flat = ref.reshape(2, ref.shape[1], ce * 2 * SUB, LANES)
        return jnp.concatenate([flat[side, f, pl.ds(h * SUB + row, ce, stride=2 * SUB), :] for h in range(2)], axis=1)

    for side, (_, row, behind, sign) in enumerate(sides):
        copies.wait(needed[side])
        pack = packs[side]
        v = [line(tiles_v, side, f, row) for f in range(5)]
        u = [line(tiles_u, side, k, row) for k in range(3)]
        eddy_row = line(tiles_e, side, 0, row)
        inner = [line(tiles_v, side, f, behind) for f in range(5)]
        inner_u = [line(tiles_u, side, k, behind) for k in range(3)]
        src = [line(tiles_s, side, f, row) for f in range(5)]
        for f, x in enumerate(v + u + [eddy_row]):
            pack[f * ce : (f + 1) * ce, :] = x
        w = 1.0 + eddy_row
        inv_v, inv_m = inverses(w)
        before = [endp[side * 8 + f : side * 8 + f + 1, :] * has[0] for f in range(8)]
        after = [endn[side * 8 + f : side * 8 + f + 1, :] * has[1] for f in range(8)]
        for f in range(8):
            pack[PACK * ce + f : PACK * ce + f + 1, :] = before[f]
            pack[PACK * ce + 8 + f : PACK * ce + 9 + f, :] = after[f]
        total, slope0, slope2 = [], [], []
        for f in range(5):
            a, b = east(v[f], before[f], after[f])
            h, l = level(v[f])
            total.append((a + b) + (h + l))
            slope0.append(a - b)
            slope2.append(h - l)
        curv = []
        for k in range(3):
            a, b = east(u[k], before[5 + k], after[5 + k])
            h, l = level(u[k])
            curv.append((a + b) + (h + l) + inner_u[k] - 6.0 * u[k])
        out = one_way(1, -sign, w, u[1], inner, inv_v, inv_m, dot3(v, curv))
        press = (slope0[3], None, slope2[3])
        for c in range(3):
            more = src[c] + w * total[c] + 0.5 * (u[0] * slope0[c] + u[2] * slope2[c])
            if press[c] is not None:
                more = more - 0.5 * press[c]
            out[c] = out[c] + more * inv_v
        out[3] = out[3] + (src[3] + total[3] - 0.5 * (slope0[0] + slope2[2])) * (1.0 / 7.0)
        out[4] = out[4] + (src[4] + w * total[4]) * inv_m
        for f in range(5):
            pack[(9 + f) * ce : (10 + f) * ce, :] = out[f]
    for taken in later:
        copies.wait(taken)


def pack(at, flags, ends, start, source, flow, eddy, n_faces):
    _, ce, cn, cz = start.shape
    out = [shape(PACK * ce + 16, cz)] * 2 + [shape(FACE, cn, cz)] * n_faces
    got = pl.pallas_call(
        functools.partial(pack_kernel, ce, cn, cz, n_faces),
        out_shape=out,
        in_specs=[whole(pltpu.SMEM)] * 2 + [whole()] * 2 + [whole(pltpu.HBM)] * 4,
        out_specs=[whole()] * len(out),
        scratch_shapes=[
            VMEM((2, 5, ce, 2, SUB, LANES), F32),
            VMEM((2, 3, ce, 2, SUB, LANES), F32),
            VMEM((2, 5, ce, 2, SUB, LANES), F32),
            VMEM((2, 1, ce, 2, SUB, LANES), F32),
            pltpu.SemaphoreType.DMA((16 + 6 * n_faces,)),
        ],
        compiler_params=params(60),
        cost_estimate=cost(1 << 22, 4 << 20),
    )(at, flags, *ends, start, source, flow, eddy)
    return got[:2], got[2:]


def split(x):
    high = x.astype(BF16)
    return high, (x - high.astype(F32)).astype(BF16)


def owner_of(turbine):
    return lax.shift_right_logical(turbine * 5462, 16)


def columns(x, first, size):
    return jnp.concatenate([x[:, k : k + 1] for k in range(first // LANES, (first + size) // LANES)], axis=0)


def lines(x, first, size):
    return jnp.concatenate([x[k : k + 1, :] for k in range(first // LANES, (first + size) // LANES)], axis=1)


def rotor_terms(row, level, turbine, weight, key, table, blocks, acc):
    size = row.shape[0]
    rows, width = table.shape[0] // 2, table.shape[1]
    cz = width // COMPS
    lane_row = lax.broadcasted_iota(jnp.int32, (size, rows), 1).astype(F32)
    pick = jnp.where(row == lane_row, 1.0, 0.0).astype(BF16)
    got = jnp.dot(jnp.concatenate([pick, pick], axis=1), table[...], preferred_element_type=F32)
    here = level == lax.broadcasted_iota(jnp.int32, (size, cz), 1).astype(F32)
    lane = lax.broadcasted_iota(jnp.int32, (size, LANES), 1)
    lane_comp = owner_of(lane)
    lane_tur = (lane - lane_comp * TURB_DEV).astype(F32)
    spread = jnp.zeros((size, LANES), F32)
    for c in range(COMPS):
        part = jnp.where(here, got[:, c * cz : (c + 1) * cz], 0.0)
        spread = jnp.where(lane_comp == c, jnp.sum(part, axis=1, keepdims=True), spread)
    spread = jnp.where(turbine == lane_tur, spread * weight, 0.0)
    lane_key = lax.broadcasted_iota(jnp.int32, (blocks * SECT, size), 0).astype(F32)
    to = jnp.where(lane_key == key, 1.0, 0.0).astype(BF16)
    high = spread.astype(BF16)
    rest = spread - high.astype(F32)
    mid, low = split(rest)
    parts = jnp.dot(to, jnp.concatenate([high, mid, low], axis=1), preferred_element_type=F32)
    acc[...] += parts[:, :LANES] + parts[:, LANES : 2 * LANES] + parts[:, 2 * LANES :]


def halves(ref, f, i, cn, move=0):
    return [ref[f, i, h, pl.ds(PAD + move, cn), :] for h in range(2)]


def level_shifts(x, first, last):
    up = [pltpu.roll(x[h], LANES - 1, 1) for h in range(2)]
    down = [pltpu.roll(x[h], 1, 1) for h in range(2)]
    return (
        [jnp.where(last, up[1], up[0]), jnp.where(last, 0.0, up[1])],
        [jnp.where(first, 0.0, down[0]), jnp.where(first, down[0], down[1])],
    )


def slab_sweep(ref, i, cn, first, last, src, flow, visc, curv):
    two = range(2)
    w = visc
    inv = [inverses(w[h]) for h in two]
    w2 = [2.0 * w[h] for h in two]

    def sides(f):
        mid = halves(ref, f, i, cn)
        a, b = halves(ref, f, i + 1, cn), halves(ref, f, i - 1, cn)
        n, s = halves(ref, f, i, cn, 1), halves(ref, f, i, cn, -1)
        up, down = level_shifts(mid, first, last)
        return mid, a, b, n, s, up, down

    _, a, b, n, s, up, down = sides(3)
    grad = [[x[h] - y[h] for h in two] for x, y in ((a, b), (n, s), (up, down))]
    q_sum = [(a[h] + b[h]) + (n[h] + s[h]) + (up[h] + down[h]) for h in two]
    out, div, bend = [], [0.0, 0.0], [0.0, 0.0]
    for c in range(3):
        mid, a, b, n, s, up, down = sides(c)
        res = []
        for h in two:
            total = (a[h] + b[h]) + (n[h] + s[h]) + (up[h] + down[h])
            slope = [a[h] - b[h], n[h] - s[h], up[h] - down[h]]
            carried = flow[0][h] * slope[0] + flow[1][h] * slope[1] + flow[2][h] * slope[2]
            res.append((src(c)[h] + 0.5 * (w2[h] * total + (carried - grad[c][h]))) * inv[h][0])
            div[h] = div[h] + slope[c]
            bend[h] = bend[h] + mid[h] * curv[c][h]
        out.append(res)
    out.append([(src(3)[h] + q_sum[h] - 0.5 * div[h]) * (1.0 / 7.0) for h in two])
    _, a, b, n, s, up, down = sides(4)
    res = []
    for h in two:
        total = (a[h] + b[h]) + (n[h] + s[h]) + (up[h] + down[h])
        res.append((src(4)[h] + w[h] * total + 0.25 * bend[h]) * inv[h][1])
    out.append(res)
    return out


def sweeps_kernel(
    ce, cn, cz, blocks,
    flags, count, start, source, flow, eddy, facep, facen, cells, turbine, sector, weight,
    final, edge_low, edge_high, coef_low, coef_high, grad, items, n_items,
    v0, u, src, ed, v1, curv, held, table, sems,
):
    copies = Copies(sems)
    two = range(2)
    has = (flags[0] > 0, flags[1] > 0)
    inner = pl.ds(PAD, cn)

    def part(h):
        return pl.ds(h * LANES, LANES)

    def halo(face, near, far, slab):
        pairs = []
        for h in two:
            pairs += [
                (face.at[0:5, :, part(h)], v0.at[:, near, h, inner]),
                (face.at[5:8, :, part(h)], u.at[:, near, h, inner]),
                (face.at[8, :, part(h)], ed.at[slab, h]),
                (face.at[9:14, :, part(h)], src.at[:, slab, h]),
                (face.at[14:19, :, part(h)], v0.at[:, far, h, inner]),
                (face.at[19:22, :, part(h)], u.at[:, far, h, inner]),
            ]
        return pairs

    ends = ((facep, 1, 0, 0), (facen, ce + 2, ce + 3, ce + 1))
    halos = []
    for exists, (face, near, far, slab) in zip(has, ends):
        taken = copies.take(*halo(face, near, far, slab))
        halos.append(taken)

        @pl.when(exists)
        def _():
            copies.start(taken)

    step = 4
    groups = []
    for g in range(0, ce, step):
        span, own, own2 = pl.ds(g, step), pl.ds(g + 1, step), pl.ds(g + 2, step)
        pairs = []
        for h in two:
            pairs += [
                (start.at[:, span, :, part(h)], v0.at[:, own2, h, inner]),
                (flow.at[:, span, :, part(h)], u.at[:, own2, h, inner]),
                (eddy.at[span, :, part(h)], ed.at[own, h]),
                (source.at[:, span, :, part(h)], src.at[:, own, h]),
            ]
        groups.append(copies.take(*pairs))
        copies.start(groups[-1])

    blank = jnp.zeros((PAD, LANES), F32)
    for ref, fields in ((v0, 5), (u, 3), (v1, 5)):

        @pl.loop(0, ref.shape[1])
        def _(i):
            for f in range(fields):
                for h in two:
                    ref[f, i, h, 0:PAD, :] = blank
                    ref[f, i, h, PAD + cn : PAD + cn + PAD, :] = blank

    for exists, (_, near, _, _) in zip(has, ends):

        @pl.when(jnp.logical_not(exists))
        def _():
            for ref, fields in ((v0, 5), (u, 3)):
                for f in range(fields):
                    for h in two:
                        ref[f, near, h, inner, :] = jnp.zeros((cn, LANES), F32)

    lane = lax.broadcasted_iota(jnp.int32, (cn, LANES), 1)
    first, last = lane == 0, lane == LANES - 1

    for exists, taken in zip(has, halos):

        @pl.when(exists)
        def _():
            copies.wait(taken)

    copies.wait(groups[0])
    copies.wait(groups[1])

    @pl.loop(0, ce + 2)
    def _(i):
        for g in range(2, len(groups)):

            @pl.when(i == 1 + step * (g - 1))
            def _():
                copies.wait(groups[g])

        real = jnp.logical_and(
            jnp.logical_or(i > 0, has[0]), jnp.logical_or(i < ce + 1, has[1])
        )

        @pl.when(real)
        def _():
            mid = i + 1
            flows = [halves(u, k, mid, cn) for k in range(3)]
            bends = []
            for k in range(3):
                a, b = halves(u, k, mid + 1, cn), halves(u, k, mid - 1, cn)
                n, s = halves(u, k, mid, cn, 1), halves(u, k, mid, cn, -1)
                up, down = level_shifts(flows[k], first, last)
                res = [(a[h] + b[h]) + (n[h] + s[h]) + (up[h] + down[h]) - 6.0 * flows[k][h] for h in two]
                for h in two:
                    curv[k, i, h] = res[h]
                bends.append(res)
            out = slab_sweep(
                v0, mid, cn, first, last,
                lambda f: [src[f, i, h] for h in two],
                flows, [1.0 + ed[i, h] for h in two], bends,
            )
            for f in range(5):
                for h in two:
                    v1[f, i, h, inner, :] = out[f][h]

        @pl.when(jnp.logical_not(real))
        def _():
            for f in range(5):
                for h in two:
                    v1[f, i, h, inner, :] = jnp.zeros((cn, LANES), F32)

    @pl.loop(0, ce)
    def _(e):
        i = e + 1
        flows = [halves(u, k, i + 1, cn) for k in range(3)]
        bends = [[curv[k, i, h] for h in two] for k in range(3)]
        out = slab_sweep(
            v1, i, cn, first, last,
            lambda f: [src[f, i, h] for h in two],
            flows, [1.0 + ed[i, h] for h in two], bends,
        )
        def put(coef, k, line):
            coef[pl.ds(k * ce + e, 1), :] = jnp.concatenate(line, axis=1)

        at = pl.ds(pl.multiple_of(e * cn, cn), cn)
        below = pl.ds(pl.multiple_of((ce + e) * cn, cn), cn)
        for h in two:
            force = flows[0][h] * jnp.abs(flows[0][h])
            for f in range(5):
                held[f, e, :, part(h)] = out[f][h]
                edge_low[f, e, :, part(h)] = out[f][h][0:SUB]
                edge_high[f, e, :, part(h)] = out[f][h][cn - SUB : cn]
            for c in range(COMPS):
                hi, lo = split(out[c if c < 3 else 4][h] * force)
                wide = pl.ds(c * cz + h * LANES, LANES)
                table[at, wide] = hi
                table[below, wide] = lo
        for coef, row, behind in ((coef_low, 0, 1), (coef_high, cn - 1, cn - 2)):
            for k in range(3):
                put(coef, k, [bends[k][h][row : row + 1] for h in two])
                put(coef, 6 + k, [v1[k, i, h, PAD + row : PAD + row + 1, :] for h in two])
            put(coef, 3, [flows[1][h][behind : behind + 1] for h in two])
            put(coef, 4, [ed[i, h, behind : behind + 1, :] for h in two])
            put(coef, 5, [flows[0][h][behind : behind + 1] for h in two])

    done = copies.take((held, final))
    copies.start(done)

    live = count[0]
    cell, tur = cells[...], turbine[...]
    owner = owner_of(tur)
    key = (owner * SECT + sector[...]).astype(F32)
    local = (tur - owner * TURB_DEV).astype(F32)
    chunks = cell.shape[0]
    slot = lax.broadcasted_iota(jnp.int32, cell.shape, 0) * LANES + lax.broadcasted_iota(jnp.int32, cell.shape, 1)
    load = jnp.where(slot < live, weight[...], 0.0)
    line = lax.shift_right_logical(cell, cz.bit_length() - 1)
    level = jnp.bitwise_and(cell, cz - 1).astype(F32)
    north = jnp.bitwise_and(line, cn - 1)
    east = lax.shift_right_logical(line, cn.bit_length() - 1)
    place = jnp.where(north == 0, 0, jnp.where(north == 1, 1, jnp.where(north == cn - 1, 2, 3)))
    is_edge = jnp.logical_or(north <= 1, north >= cn - 2)
    chosen = jnp.where(jnp.logical_and(is_edge, slot < live), 1.0, 0.0)
    edge_row = (place * ce + east).astype(F32)

    lower = lax.broadcasted_iota(jnp.int32, (LANES, LANES), 0) < lax.broadcasted_iota(jnp.int32, (LANES, LANES), 1)
    rank = jnp.dot(chosen.astype(BF16), jnp.where(lower, 1.0, 0.0).astype(BF16), preferred_element_type=F32)
    sums = jnp.sum(chosen, axis=1, keepdims=True)
    so_far = jnp.zeros((1, 1), F32)
    starts = []
    for k in range(chunks):
        starts.append(so_far)
        so_far = so_far + sums[k : k + 1]
    rank = jnp.where(chosen > 0.0, rank + jnp.concatenate(starts, axis=0), -1.0)
    total = jnp.sum(chosen).astype(jnp.int32)
    n_items[0] = total
    load_high = load.astype(BF16).astype(F32)
    load_rest = load - load_high
    load_mid = load_rest.astype(BF16).astype(F32)
    load_low = load_rest - load_mid
    blank = jnp.zeros((1, LANES), F32)
    rows = [
        jnp.concatenate([x[k : k + 1] for x in (edge_row, level, key, local, load_high, load_mid, load_low)] + [blank])
        for k in range(chunks)
    ]
    to = lax.broadcasted_iota(jnp.int32, (LANES, LANES), 0).astype(F32)
    items[...] = jnp.zeros_like(items)
    for q in range(chunks):

        @pl.when(q * LANES < total)
        def _():
            where = jnp.concatenate(
                [jnp.where(rank[k : k + 1] - float(q * LANES) == to, 1.0, 0.0) for k in range(chunks)], axis=1
            ).astype(BF16)
            entries = jnp.concatenate(rows, axis=1).astype(BF16)
            items[q] = lax.dot_general(entries, where, (((1,), (1,)), ((), ())), preferred_element_type=F32)

    row_t, level_t, local_t, load_t = line.astype(F32).T, level.T, local.T, load.T
    grad[...] = jnp.zeros_like(grad)
    size = min(BLOCK, chunks * LANES)
    for base in range(0, chunks * LANES, size):

        @pl.when(base < live)
        def _():
            cols = [columns(x, base, size) for x in (row_t, level_t, local_t, load_t)]
            rotor_terms(*cols, lines(key, base, size), table, blocks, grad)

    copies.wait(done)


def sweeps(flags, count, start, source, flow, eddy, faces, lists, blocks):
    _, ce, cn, cz = start.shape
    chunks = lists[0].shape[0]
    edge = shape(5, ce, SUB, cz)
    return pl.pallas_call(
        functools.partial(sweeps_kernel, ce, cn, cz, blocks),
        out_shape=(
            shape(*start.shape),
            edge,
            edge,
            shape(EDGE * ce, cz),
            shape(EDGE * ce, cz),
            shape(blocks * SECT, LANES),
            shape(chunks, ITEM, LANES),
            jax.ShapeDtypeStruct((1,), jnp.int32),
        ),
        in_specs=[whole(pltpu.SMEM)] * 2 + [whole(pltpu.HBM)] * 6 + [whole()] * 4,
        out_specs=(whole(pltpu.HBM),) + (whole(),) * 6 + (whole(pltpu.SMEM),),
        scratch_shapes=[
            VMEM((5, ce + 4, 2, PAD + cn + PAD, LANES), F32),
            VMEM((3, ce + 4, 2, PAD + cn + PAD, LANES), F32),
            VMEM((5, ce + 2, 2, cn, LANES), F32),
            VMEM((ce + 2, 2, cn, LANES), F32),
            VMEM((5, ce + 2, 2, PAD + cn + PAD, LANES), F32),
            VMEM((3, ce + 2, 2, cn, LANES), F32),
            VMEM(start.shape, F32),
            VMEM((2 * ce * cn, COMPS * cz), BF16),
            pltpu.SemaphoreType.DMA((24 + 8 * (ce // 4) + 1,)),
        ],
        compiler_params=params(48),
        cost_estimate=cost(300 * start.size // 5, 10 << 20),
    )(flags, count, start, source, flow, eddy, *faces, *lists)


def edge_kernel(
    ce, cn, cz, blocks, copies_out,
    flags, n_items, facep, facen, own_low, own_high, coef_low, coef_high, got_prev, got_next,
    edge_low, edge_high, items, grad, final_in,
    final, chunks,
    low_out, high_out, table, acc, sems,
):
    east, level = plane_shifts(ce, cz)
    sub = lax.broadcasted_iota(jnp.int32, (SUB, cz), 0)
    has = [flags[k].astype(F32) for k in range(4)]
    sides = (
        (-1.0, 0, own_low, coef_low, got_prev, edge_low, low_out, 0),
        (1.0, cn - 1, own_high, coef_high, got_next, edge_high, high_out, cn - SUB),
    )
    waits = []
    for side, (sign, row, own, coef, got, edge, out_ref, place) in enumerate(sides):

        def plane(ref, f):
            return ref[f * ce : (f + 1) * ce, :]

        v0 = [plane(own, f) for f in range(5)]
        u = [plane(own, 5 + k) for k in range(3)]
        w = 1.0 + plane(own, 8)
        xv = [plane(got, f) for f in range(5)]
        xu = [plane(got, 5 + k) for k in range(3)]
        xw = 1.0 + plane(got, 8)
        xp = [plane(got, 9 + f) for f in range(5)]
        curv = [plane(coef, k) for k in range(3)]
        inv_v, inv_m = inverses(w)
        delta = one_way(1, sign, w, u[1], xv, inv_v, inv_m, dot3(v0, xu))
        back = one_way(1, -sign, xw, xu[1], v0, *inverses(xw), dot3(xv, u))
        x1 = [xp[f] + back[f] for f in range(5)]
        ends = []
        for far, face in enumerate((facep, facen)):
            hv = [got[PACK * ce + 8 * far + f : PACK * ce + 8 * far + f + 1, :] for f in range(8)]
            fv = [face[f, row : row + 1, :] * has[far] for f in range(5)]
            fu = face[6, row : row + 1, :] * has[far]
            fw = 1.0 + face[8, row : row + 1, :] * has[far]
            ends.append(one_way(1, sign, fw, fu, hv, *inverses(fw), dot3(fv, hv[5:])))
        x1 = [x * has[2 + side] for x in x1]
        total, slope0, slope2 = [], [], []
        for f in range(5):
            a, b = east(delta[f], ends[0][f], ends[1][f])
            h, l = level(delta[f])
            total.append((a + b) + (h + l))
            slope0.append(a - b)
            slope2.append(h - l)
        full = [plane(coef, 6 + c) + delta[c] for c in range(3)]
        add = one_way(1, sign, w, u[1], x1, inv_v, inv_m, dot3(full, xu) + dot3(delta, curv))
        press = (slope0[3], None, slope2[3])
        for c in range(3):
            more = w * total[c] + 0.5 * (u[0] * slope0[c] + u[2] * slope2[c])
            if press[c] is not None:
                more = more - 0.5 * press[c]
            add[c] = add[c] + more * inv_v
        add[3] = add[3] + (total[3] - 0.5 * (slope0[0] + slope2[2])) * (1.0 / 7.0)
        add[4] = add[4] + w * total[4] * inv_m
        ru1, rw, ru0 = plane(coef, 3), 1.0 + plane(coef, 4), plane(coef, 5)
        behind = one_way(1, sign, rw, ru1, delta, *inverses(rw))
        near, far = (0, 1) if side == 0 else (SUB - 1, SUB - 2)
        for f in range(5):
            for e in range(ce):
                rows = jnp.where(
                    sub == near, add[f][e : e + 1, :], jnp.where(sub == far, behind[f][e : e + 1, :], 0.0)
                )
                out_ref[f, e] = edge[f, e] + rows
        copy = pltpu.make_async_copy(out_ref, final.at[:, :, pl.ds(place, SUB), :], sems.at[side])
        copy.start()
        waits.append(copy)
        for behind_row, u0, values in ((0, u[0], add), (1, ru0, behind)):
            force = u0 * jnp.abs(u0)
            at = (2 * side + behind_row) * ce
            for c in range(COMPS):
                hi, lo = split(values[c if c < 3 else 4] * force)
                table[at : at + ce, c * cz : (c + 1) * cz] = hi
                table[4 * ce + at : 5 * ce + at, c * cz : (c + 1) * cz] = lo

    acc[...] = grad[...]
    live = n_items[0]
    count = items.shape[0]
    per = min(BLOCK // LANES, count)
    for base in range(0, count, per):

        @pl.when(base * LANES < live)
        def _():
            lists = [items[base + k] for k in range(per)]
            turned = [x.T for x in lists]

            def col(j):
                return jnp.concatenate([x[:, j : j + 1] for x in turned], axis=0)

            key = jnp.concatenate([x[2:3] for x in lists], axis=1)
            rotor_terms(col(0), col(1), col(3), col(4) + col(5) + col(6), key, table, blocks, acc)

    for copy in range(copies_out):
        chunks[copy] = acc[...]
    for copy in waits:
        copy.wait()


def edges(flags, n_items, faces, packs, coefs, gots, tiles, items, grad, final, blocks, size):
    _, ce, cn, cz = final.shape
    args = (flags, n_items, *faces, *packs, *coefs, *gots, *tiles, items, grad, final)
    tile = VMEM((5, ce, SUB, cz), F32)
    return pl.pallas_call(
        functools.partial(edge_kernel, ce, cn, cz, blocks, size),
        out_shape=(shape(*final.shape), shape(size, blocks * SECT, LANES)),
        in_specs=[whole(pltpu.SMEM)] * 2 + [whole()] * (len(args) - 3) + [whole(pltpu.HBM)],
        out_specs=(whole(pltpu.HBM), whole()),
        scratch_shapes=[
            tile,
            tile,
            VMEM((8 * ce, COMPS * cz), BF16),
            VMEM((blocks * SECT, LANES), F32),
            pltpu.SemaphoreType.DMA((2,)),
        ],
        input_output_aliases={len(args) - 1: 0},
        compiler_params=params(32),
        cost_estimate=cost(1 << 24, 4 << 20),
    )(*args)


def sum_kernel(parts, out):
    total = jnp.sum(parts[...], axis=0)
    for c in range(COMPS):
        out[c] = total[:, c * TURB_DEV : (c + 1) * TURB_DEV]


def sum_parts(parts):
    return pl.pallas_call(
        sum_kernel,
        out_shape=shape(COMPS, SECT, TURB_DEV),
        in_specs=[whole()],
        out_specs=whole(),
        cost_estimate=cost(parts.size, parts.size * 4),
    )(parts)


def beside(x, size):
    if size == 2:
        got = lax.ppermute(x[0], "east", [(0, 1), (1, 0)])
        return got, got
    up = [(i, i + 1) for i in range(size - 1)]
    down = [(i + 1, i) for i in range(size - 1)]
    return lax.ppermute(x[1], "east", up), lax.ppermute(x[0], "east", down)


def north_ways(x, size):
    up = [(i, i + 1) for i in range(size - 1)]
    down = [(i + 1, i) for i in range(size - 1)]
    return lax.ppermute(x[1], "north", up), lax.ppermute(x[0], "north", down)


def shards(
    adjoint_start,
    adjoint_source,
    base_flow,
    eddy_visc,
    rotor_count,
    rotor_cell,
    rotor_turbine,
    rotor_sector,
    rotor_weight,
):
    _, ce, cn, cz = adjoint_start.shape
    n_east, n_north = lax.axis_size("east"), lax.axis_size("north")
    east, north = lax.axis_index("east"), lax.axis_index("north")
    flags = jnp.stack([east > 0, east < n_east - 1, north > 0, north < n_north - 1]).astype(jnp.int32)
    count = rotor_count.reshape(1)
    slots = rotor_cell.shape[-1]
    lists = [x.reshape(slots // LANES, LANES) for x in (rotor_cell, rotor_turbine, rotor_sector, rotor_weight)]

    if n_east == 2:
        at = jnp.stack([(1 - east) * (ce - 1), (1 - east) * (ce - 1) + 2 * east - 1])
    else:
        at = jnp.array([0, 1, ce - 1, ce - 2])
    at, n_faces = at.astype(jnp.int32), 1 if n_east == 2 else 2
    ends = beside(row_ends(at, adjoint_start, base_flow, n_faces), n_east)
    packs, own = pack(at, flags, ends, adjoint_start, adjoint_source, base_flow, eddy_visc, n_faces)
    gots = north_ways(packs, n_north)
    faces = beside(own, n_east)
    final, low, high, coef_low, coef_high, grad, items, n_items = sweeps(
        flags, count, adjoint_start, adjoint_source, base_flow, eddy_visc, faces, lists, n_north
    )
    final, chunks = edges(
        flags, n_items, faces, packs, (coef_low, coef_high), gots, (low, high), items, grad, final,
        n_north, n_east,
    )
    chunks = chunks.reshape(n_east * n_north, SECT, LANES)
    parts = lax.all_to_all(chunks, ("east", "north"), 0, 0, tiled=True)
    return (final, sum_parts(parts))


def solution(mesh):
    placed = (
        P(None, "east", "north", None),
        P(None, "east", "north", None),
        P(None, "east", "north", None),
        P("east", "north", None),
        P("east", "north"),
        P("east", "north", None),
        P("east", "north", None),
        P("east", "north", None),
        P("east", "north", None),
    )
    return jax.shard_map(
        shards,
        mesh=mesh,
        in_specs=placed,
        out_specs=(P(None, "east", "north", None), P(None, None, "north")),
        check_vma=False,
    )
```

time: 188 us -> 51.2 us (0.27)
  local copies, waits for them, and re-layouts: 56 us -> 0.65 us
  other arithmetic: 45.7 us -> 1.21 us
  blocking collectives: 45.3 us -> 12.9 us
  Pallas kernels: 0 us -> 26.6 us
  starting transfers between devices: 29.4 us -> 7.41 us
  waiting for transfers between devices: 7.78 us -> 0.36 us
    psum x1 -> x0, blocking collectives: 45.3 us -> none  [shards(): summed = lax.psum(partial_grad, ('east', 'north'))]
    concatenate x2 -> x0, local copies, waits for them, and re-layouts: 30.3 us -> none  [the longest x1 30.3 us: relax(): return jnp.concatenate([velocity, pressure[None], eddy_new[None]], axis=0)]
    pallas_call x0 -> x5, Pallas kernels: none -> 26.6 us  [the longest x1 15.8 us: sweeps(): pl.pallas_call(functools.partial(sweeps_kernel, ce, cn, cz, blocks), out_...]
    concatenate x9 -> x0, other arithmetic: 22.8 us -> none  [the longest x5 15.8 us: extended(): shard = jnp.concatenate([before, shard, after], axis=dim)]
    ppermute x12 -> x4, starting transfers between devices: 29.4 us -> 7.41 us  [the longest x2 6.48 us: north_ways(): return (lax.ppermute(x[1], 'north', up), lax.ppermute(x[0], 'north', down))]
    gather x2 -> x0, local copies, waits for them, and re-layouts: 16.6 us -> none  [the longest x1 10.5 us: shards(): values = flat_state[:, cells]]
    all_to_all x0 -> x1, blocking collectives: none -> 12.9 us  [shards(): parts = lax.all_to_all(chunks, ('east', 'north'), 0, 0, tiled=True)]
    ppermute x12 -> x4, waiting for transfers between devices: 7.78 us -> 0.36 us  [the longest x2 0.35 us: beside(): got = lax.ppermute(x[0], 'east', [(0, 1), (1, 0)])]
  transfers between devices with their start and end apart: 12 -> 4, of which waited for: 3 -> 1; matrix products, arithmetic and copies ran while one was open for 11% -> 1% of each run, Pallas kernels for 0% -> 31%
where the time goes in v2:
time: 51.2 us; the launch traced here: 50.6 us
  Pallas kernels  26.6 us (52%)
  blocking collectives  12.9 us (25%)
  starting transfers between devices  7.41 us (14%)
  between operations  1.48 us (3%)
  other arithmetic  1.21 us (2%)
  local copies, waits for them, and re-layouts  0.65 us (1%)
    pallas_call x1, Pallas kernels, sweeps(): pl.pallas_call(functools.partial(sweeps_kernel, ce, cn, cz, blocks), out_...  15.8 us
    all_to_all x1, blocking collectives, shards(): parts = lax.all_to_all(chunks, ('east', 'north'), 0, 0, tiled=True)  12.9 us
    ppermute x2, starting transfers between devices, north_ways(): return (lax.ppermute(x[1], 'north', up), lax.ppermute(x[0], 'north', down))  6.48 us
    pallas_call x1, Pallas kernels, pack(): pl.pallas_call(functools.partial(pack_kernel, ce, cn, cz, n_faces), out_s...  4.3 us
    pallas_call x1, Pallas kernels, edges(): pl.pallas_call(functools.partial(edge_kernel, ce, cn, cz, blocks, size),...  2.67 us
    pallas_call x1, Pallas kernels, row_ends(): pl.pallas_call(functools.partial(ends_kernel, cn, n_faces), out_shape=[sh...  2.13 us
    pallas_call x1, Pallas kernels, sum_parts(): pl.pallas_call(sum_kernel, out_shape=shape(COMPS, SECT, TURB_DEV), in_spe...  1.61 us
  transfers between devices with their start and end apart: 4, of which 1 were waited for; matrix products, arithmetic and copies ran while one was open for 1% of the time, Pallas kernels for 31%

profile of v2, /device:TPU:0, one launch (start us, length us, event | category | flops | bytes accessed | tf_op | source)
XLA Modules:
  0.0 50.6 jit_solution(14402518710738561876)
XLA Ops:
  0.6 0.6 %pad_add_fusion.at = s32[2]{0:T(128)} fusion(s32[1]{0:T(128)} %bitcast.6, s32[1]{0:T(128)} %bitcast.5), kind=kLoop, calls=%fused_computation.1 | loop fusion | flops 2 | bytes 16 | tf_op jit(solution)/shard_map/stack | solution.py:767
  1.2 2.1 %shard_map.104 = f32[16,256]{1,0:T(8,128)} custom-call(s32[2]{0:T(128)} %pad_add_fusion.at, f32[5,16,32,256]{3,2,1,0:T(8,128)} %start.5, f32[3,16,32,256]{3,2,1,0:T(8,128)} %flow.5), custom_call_target="tpu_custom_call" | custom-call | bytes 65536 | tf_op jit(solution)/shard_map/pallas_call | solution.py:125
  3.3 0.5 %collective-permute-start = (f32[16,256]{1,0:T(8,128)}, f32[16,256]{1,0:T(8,128)S(1)}, u32[]{:S(2)}, u32[]{:S(2)}) collective-permute-start(f32[16,256]{1,0:T(8,128)} %shard_map.104), channel_id=1, source_target_pairs={{0,16},{16,0},{1,17},{17,1},{2,18},{18,2},{3,19},{19,3},{4,20},{20... | collective-permute-start | bytes 49160 | tf_op jit(solution)/shard_map/ppermute | solution.py:734
  3.9 0.7 %add_convert_fusion.flags = s32[4]{0:T(128)} fusion(pred[1]{0:T(512)(128)(4,1)} %bitcast.3, pred[1]{0:T(512)(128)(4,1)} %bitcast.2, pred[1]{0:T(512)(128)(4,1)} %bitcast.1, pred[1]{0:T(512)(128)(4,1)} %bitcast), kind=kLoop, calls=%fused_computation | loop fusion | flops 16 | bytes 20 | tf_op jit(solution)/shard_map/convert_element_type | solution.py:761
  4.5 0.0 copy-start
  4.5 0.0 copy-start.6
  4.5 0.0 copy-start.7
  4.5 0.0 copy-start.8
  4.6 0.3 collective-permute-done.endp.endn
  4.9 0.6 %copy-done.9 = f32[16,256]{1,0:T(8,128)} copy-done((f32[16,256]{1,0:T(8,128)}, f32[16,256]{1,0:T(8,128)S(1)}, u32[]{:S(2)}) %copy-start.9) | copy-done | bytes 16408
  5.5 4.3 %shard_map.105 = (f32[240,256]{1,0:T(8,128)}, f32[240,256]{1,0:T(8,128)}, f32[22,32,256]{2,1,0:T(8,128)}) custom-call(s32[2]{0:T(128)} %pad_add_fusion.at, s32[4]{0:T(128)} %add_convert_fusion.flags, f32[16,256]{1,0:T(8,128)} %copy-done.9, f32[16,256]{1,0:T(8,128)} %copy-done.9, f32[5,16,32,256]{3,2,1,0:T(8,128)} %start.5, f32[5,16,32,256]{3,2,1,0:T(8,128)} %source.3, ...), custom_call_target="tpu_custom_call" | custom-call | flops 4194304 | bytes 4194304 | tf_op jit(solution)/shard_map/pallas_call | solution.py:227
  9.8 0.4 collective-permute-start.1
  10.2 1.3 %collective-permute-start.3 = (f32[240,256]{1,0:T(8,128)}, f32[240,256]{1,0:T(8,128)S(1)}, u32[]{:S(2)}, u32[]{:S(2)}) collective-permute-start(f32[240,256]{1,0:T(8,128)} %get-tuple-element.17.own_low), channel_id=1, source_target_pairs={{1,0},{2,1},{3,2},{4,3},{5,4},{6,5},{7,6},{8,7},{9,8},{10,9},{11,1... | collective-permute-start | bytes 737288 | tf_op jit(solution)/shard_map/ppermute | solution.py:744
  11.5 5.2 %collective-permute-start.2 = (f32[240,256]{1,0:T(8,128)}, f32[240,256]{1,0:T(8,128)S(1)}, u32[]{:S(2)}, u32[]{:S(2)}) collective-permute-start(f32[240,256]{1,0:T(8,128)} %get-tuple-element.18.own_high), channel_id=1, source_target_pairs={{0,1},{1,2},{2,3},{3,4},{4,5},{5,6},{6,7},{7,8},{8,9},{9,10},{10,1... | collective-permute-start | bytes 737288 | tf_op jit(solution)/shard_map/ppermute | solution.py:744
  17.4 0.0 collective-permute-done.1.facep.facen
  17.4 0.0 copy-done
  17.4 0.0 copy-done.1
  17.4 0.0 copy-done.4
  17.4 0.0 copy-done.5
  17.4 0.0 copy-done.6
  17.4 0.0 copy-done.7
  17.4 0.0 copy-done.8
  17.4 0.0 copy-start.2
  17.5 0.0 copy-start.3
  17.5 15.8 %shard_map.106 = (f32[5,16,32,256]{3,2,1,0:T(8,128)}, f32[5,16,8,256]{3,2,1,0:T(8,128)S(1)}, f32[5,16,8,256]{3,2,1,0:T(8,128)S(1)}, f32[144,256]{1,0:T(8,128)S(1...) custom-call(s32[4]{0:T(128)S(1)} %copy-done.4, s32[1]{0:T(128)} %bitcast.12.count, ...), custom_call_target="tpu_custom_call" | custom-call | flops 39321600 | bytes 10485760 | tf_op jit(solution)/shard_map/pallas_call | solution.py:564
  33.3 0.0 collective-permute-done.3.got_next
  33.3 0.0 collective-permute-done.2.got_prev
  33.3 0.0 copy-done.2
  33.3 0.0 copy-done.3
  33.4 2.7 %shard_map.107 = (f32[5,16,32,256]{3,2,1,0:T(8,128)}, f32[2,128,128]{2,1,0:T(8,128)S(1)}) custom-call(s32[4]{0:T(128)S(1)} %copy-done.4, s32[1]{0:T(128)} %get-tuple-element.16.n_items, f32[22,32,256]{2,1,0:T(8,128)S(1)} %collective-permute-done.1.facep.facen, ...), custom_call_target="tpu_custom_call", output_to_operand_aliasing={{0}: (14, {})} | custom-call | flops 16777216 | bytes 4194304 | tf_op jit(solution)/shard_map/pallas_call | solution.py:698
  36.0 12.9 %all_to_all.5.parts = f32[32,8,128]{2,1,0:T(8,128)} all-to-all(f32[32,8,128]{2,1,0:T(8,128)S(1)} %bitcast.13), channel_id=1, replica_groups=mesh['east'=2,'north'=16] {'east','north'}, dimensions={0} | all-to-all | bytes 262144 | tf_op jit(solution)/shard_map/all_to_all | solution.py:783
  49.0 1.6 %shard_map.108 = f32[4,8,12]{2,1,0:T(8,128)} custom-call(f32[32,8,128]{2,1,0:T(8,128)} %all_to_all.5.parts), custom_call_target="tpu_custom_call" | custom-call | flops 32768 | bytes 131072 | tf_op jit(solution)/shard_map/pallas_call | solution.py:723
  (4 shorter events, 0.0 us)
Async XLA Ops:
  3.3 1.6 %collective-permute-start = (f32[16,256]{1,0:T(8,128)}, f32[16,256]{1,0:T(8,128)S(1)}, u32[]{:S(2)}, u32[]{:S(2)}) collective-permute-start(f32[16,256]{1,0:T(8,128)} %shard_map.104), channel_id=1, source_target_pairs={{0,16},{16,0},{1,17},{17,1},{2,18},{18,2},{3,19},{19,3},{4,20},{20... | collective-permute-start | bytes 49160 | tf_op jit(solution)/shard_map/ppermute | solution.py:734
  4.5 12.9 %copy-start = (f32[3,16,32,256]{3,2,1,0:T(8,128)S(1)}, f32[3,16,32,256]{3,2,1,0:T(8,128)}, u32[]{:S(2)}) copy-start(f32[3,16,32,256]{3,2,1,0:T(8,128)} %flow.5) | copy-start | bytes 4718596
  4.5 12.9 %copy-start.1 = (f32[16,32,256]{2,1,0:T(8,128)S(1)}, f32[16,32,256]{2,1,0:T(8,128)}, u32[]{:S(2)}) copy-start(f32[16,32,256]{2,1,0:T(8,128)} %eddy.3) | copy-start | bytes 1572868
  4.5 12.9 %copy-start.4 = (s32[4]{0:T(128)S(1)}, s32[4]{0:T(128)}, u32[]{:S(2)}) copy-start(s32[4]{0:T(128)} %add_convert_fusion.flags) | copy-start | bytes 52
  4.5 12.9 %copy-start.5 = (s32[1,1,1024]{2,1,0:T(1,128)S(1)}, s32[1,1,1024]{2,1,0:T(1,128)}, u32[]{:S(2)}) copy-start(s32[1,1,1024]{2,1,0:T(1,128)} %param.14) | copy-start | bytes 12292
  4.5 12.9 %copy-start.6 = (s32[1,1,1024]{2,1,0:T(1,128)S(1)}, s32[1,1,1024]{2,1,0:T(1,128)}, u32[]{:S(2)}) copy-start(s32[1,1,1024]{2,1,0:T(1,128)} %param.15) | copy-start | bytes 12292
  4.5 12.9 %copy-start.7 = (s32[1,1,1024]{2,1,0:T(1,128)S(1)}, s32[1,1,1024]{2,1,0:T(1,128)}, u32[]{:S(2)}) copy-start(s32[1,1,1024]{2,1,0:T(1,128)} %param.16) | copy-start | bytes 12292
  4.5 12.9 %copy-start.8 = (f32[1,1,1024]{2,1,0:T(1,128)S(1)}, f32[1,1,1024]{2,1,0:T(1,128)}, u32[]{:S(2)}) copy-start(f32[1,1,1024]{2,1,0:T(1,128)} %param.17) | copy-start | bytes 12292
  4.9 0.6 %copy-start.9 = (f32[16,256]{1,0:T(8,128)}, f32[16,256]{1,0:T(8,128)S(1)}, u32[]{:S(2)}) copy-start(f32[16,256]{1,0:T(8,128)S(1)} %collective-permute-done.endp.endn) | copy-start | bytes 49156
  9.8 7.6 %collective-permute-start.1 = (f32[22,32,256]{2,1,0:T(8,128)}, f32[22,32,256]{2,1,0:T(8,128)S(1)}, u32[]{:S(2)}, u32[]{:S(2)}) collective-permute-start(f32[22,32,256]{2,1,0:T(8,128)} %get-tuple-element.15), channel_id=1, source_target_pairs={{0,16},{16,0},{1,17},{17,1},{2,18},{18,2},{3,19},{19,3},{4,20},{20... | collective-permute-start | bytes 2162696 | tf_op jit(solution)/shard_map/ppermute | solution.py:734
  10.2 23.1 %collective-permute-start.3 = (f32[240,256]{1,0:T(8,128)}, f32[240,256]{1,0:T(8,128)S(1)}, u32[]{:S(2)}, u32[]{:S(2)}) collective-permute-start(f32[240,256]{1,0:T(8,128)} %get-tuple-element.17.own_low), channel_id=1, source_target_pairs={{1,0},{2,1},{3,2},{4,3},{5,4},{6,5},{7,6},{8,7},{9,8},{10,9},{11,1... | collective-permute-start | bytes 737288 | tf_op jit(solution)/shard_map/ppermute | solution.py:744
  11.5 21.8 %collective-permute-start.2 = (f32[240,256]{1,0:T(8,128)}, f32[240,256]{1,0:T(8,128)S(1)}, u32[]{:S(2)}, u32[]{:S(2)}) collective-permute-start(f32[240,256]{1,0:T(8,128)} %get-tuple-element.18.own_high), channel_id=1, source_target_pairs={{0,1},{1,2},{2,3},{3,4},{4,5},{5,6},{6,7},{7,8},{8,9},{9,10},{10,1... | collective-permute-start | bytes 737288 | tf_op jit(solution)/shard_map/ppermute | solution.py:744
  17.4 15.9 %copy-start.2 = (f32[240,256]{1,0:T(8,128)S(1)}, f32[240,256]{1,0:T(8,128)}, u32[]{:S(2)}) copy-start(f32[240,256]{1,0:T(8,128)} %get-tuple-element.17.own_low) | copy-start | bytes 737284
  17.5 15.9 %copy-start.3 = (f32[240,256]{1,0:T(8,128)S(1)}, f32[240,256]{1,0:T(8,128)}, u32[]{:S(2)}) copy-start(f32[240,256]{1,0:T(8,128)} %get-tuple-element.18.own_high) | copy-start | bytes 737284

commit v3 on v2

--- a/solution.py
+++ b/solution.py
@@ -17,7 +17,7 @@
 FACE = 22
 EDGE = 9
 ITEM = 8
-BLOCK = 256
+STEP = 2
 VMEM = pltpu.VMEM
 F32 = jnp.float32
 BF16 = jnp.bfloat16
@@ -59,6 +59,22 @@
     def wait(self, taken):
         for c in self.made(taken):
             c.wait()
+
+
+def neighbours():
+    e, n = lax.axis_index("east"), lax.axis_index("north")
+    last_e, last_n = lax.axis_size("east") - 1, lax.axis_size("north") - 1
+    return [
+        jnp.where(e > 0, 1, 0), jnp.where(e < last_e, 1, 0),
+        jnp.where(n > 0, 1, 0), jnp.where(n < last_n, 1, 0),
+    ]
+
+
+def facing(ce):
+    if lax.axis_size("east") == 2:
+        e = lax.axis_index("east")
+        return [((1 - e) * (ce - 1), (1 - e) * (ce - 1) + 2 * e - 1)]
+    return [(0, 1), (ce - 1, ce - 2)]
 
 
 def one_way(k, sign, w, u, f, inv_v, inv_m, bend=None):
@@ -100,12 +116,11 @@
     return east, level
 
 
-def ends_kernel(cn, n_faces, at, start, flow, *refs):
+def ends_kernel(ce, cn, n_faces, start, flow, *refs):
     outs, tiles_v, tiles_u, sems = refs[:n_faces], *refs[n_faces:]
     copies = Copies(sems)
     taken = []
-    for i in range(n_faces):
-        e = at[2 * i]
+    for i, (e, _) in enumerate(facing(ce)):
         pairs = []
         for side, first in enumerate((0, cn - SUB)):
             pairs.append((start.at[:, e, pl.ds(first, SUB)], tiles_v.at[i, side]))
@@ -120,12 +135,12 @@
                 out[side * 8 + f : side * 8 + f + 1, :] = tile[row : row + 1]
 
 
-def row_ends(at, start, flow, n_faces):
+def row_ends(start, flow, n_faces):
     _, ce, cn, cz = start.shape
     return pl.pallas_call(
-        functools.partial(ends_kernel, cn, n_faces),
+        functools.partial(ends_kernel, ce, cn, n_faces),
         out_shape=[shape(16, cz)] * n_faces,
-        in_specs=[whole(pltpu.SMEM)] + [whole(pltpu.HBM)] * 2,
+        in_specs=[whole(pltpu.HBM)] * 2,
         out_specs=[whole()] * n_faces,
         scratch_shapes=[
             VMEM((n_faces, 2, 5, SUB, cz), F32),
@@ -134,14 +149,14 @@
         ],
         compiler_params=params(60),
         cost_estimate=cost(0, 1 << 16),
-    )(at, start, flow)
-
-
-def pack_kernel(ce, cn, cz, n_faces, at, flags, endp, endn, start, source, flow, eddy, *refs):
+    )(start, flow)
+
+
+def pack_kernel(ce, cn, cz, n_faces, endp, endn, start, source, flow, eddy, *refs):
     packs, refs = refs[:2], refs[2:]
     faces, refs = refs[:n_faces], refs[n_faces:]
     tiles_v, tiles_u, tiles_s, tiles_e, sems = refs
-    has = [flags[k].astype(F32) for k in range(2)]
+    has = [x.astype(F32) for x in neighbours()[:2]]
     copies = Copies(sems)
     sides = ((0, 0, 1, -1.0), (cn - SUB, SUB - 1, SUB - 2, 1.0))
     needed = []
@@ -158,8 +173,7 @@
         needed.append(copies.take(*pairs))
         copies.start(needed[-1])
     later = []
-    for i in range(n_faces):
-        near, far, face = at[2 * i], at[2 * i + 1], faces[i]
+    for (near, far), face in zip(facing(ce), faces):
         taken = copies.take(
             (start.at[:, near], face.at[0:5]),
             (flow.at[:, near], face.at[5:8]),
@@ -221,13 +235,13 @@
         copies.wait(taken)
 
 
-def pack(at, flags, ends, start, source, flow, eddy, n_faces):
+def pack(ends, start, source, flow, eddy, n_faces):
     _, ce, cn, cz = start.shape
     out = [shape(PACK * ce + 16, cz)] * 2 + [shape(FACE, cn, cz)] * n_faces
     got = pl.pallas_call(
         functools.partial(pack_kernel, ce, cn, cz, n_faces),
         out_shape=out,
-        in_specs=[whole(pltpu.SMEM)] * 2 + [whole()] * 2 + [whole(pltpu.HBM)] * 4,
+        in_specs=[whole()] * 2 + [whole(pltpu.HBM)] * 4,
         out_specs=[whole()] * len(out),
         scratch_shapes=[
             VMEM((2, 5, ce, 2, SUB, LANES), F32),
@@ -238,7 +252,7 @@
         ],
         compiler_params=params(60),
         cost_estimate=cost(1 << 22, 4 << 20),
-    )(at, flags, *ends, start, source, flow, eddy)
+    )(*ends, start, source, flow, eddy)
     return got[:2], got[2:]
 
 
@@ -257,6 +271,11 @@
 
 def lines(x, first, size):
     return jnp.concatenate([x[k : k + 1, :] for k in range(first // LANES, (first + size) // LANES)], axis=1)
+
+
+def steps_of(chunks):
+    sizes = [0] + [x for x in (LANES, 2 * LANES) if x < chunks * LANES] + [chunks * LANES]
+    return list(zip(sizes[:-1], sizes[1:]))
 
 
 def rotor_terms(row, level, turbine, weight, key, table, blocks, acc):
@@ -337,13 +356,13 @@
 
 def sweeps_kernel(
     ce, cn, cz, blocks,
-    flags, count, start, source, flow, eddy, facep, facen, cells, turbine, sector, weight,
+    count, start, source, flow, eddy, facep, facen, cells, turbine, sector, weight,
     final, edge_low, edge_high, coef_low, coef_high, grad, items, n_items,
     v0, u, src, ed, v1, curv, held, table, sems,
 ):
     copies = Copies(sems)
     two = range(2)
-    has = (flags[0] > 0, flags[1] > 0)
+    has = [x > 0 for x in neighbours()[:2]]
     inner = pl.ds(PAD, cn)
 
     def part(h):
@@ -363,19 +382,10 @@
         return pairs
 
     ends = ((facep, 1, 0, 0), (facen, ce + 2, ce + 3, ce + 1))
-    halos = []
-    for exists, (face, near, far, slab) in zip(has, ends):
-        taken = copies.take(*halo(face, near, far, slab))
-        halos.append(taken)
-
-        @pl.when(exists)
-        def _():
-            copies.start(taken)
-
-    step = 4
-    groups = []
-    for g in range(0, ce, step):
-        span, own, own2 = pl.ds(g, step), pl.ds(g + 1, step), pl.ds(g + 2, step)
+    halos = [copies.take(*halo(*x)) for x in ends]
+
+    def group(g):
+        span, own, own2 = pl.ds(g, STEP), pl.ds(g + 1, STEP), pl.ds(g + 2, STEP)
         pairs = []
         for h in two:
             pairs += [
@@ -384,8 +394,19 @@
                 (eddy.at[span, :, part(h)], ed.at[own, h]),
                 (source.at[:, span, :, part(h)], src.at[:, own, h]),
             ]
-        groups.append(copies.take(*pairs))
-        copies.start(groups[-1])
+        return pairs
+
+    groups = [copies.take(*group(g)) for g in range(0, ce, STEP)]
+    per = len(groups[0][1])
+    copies.start(groups[0])
+    for exists, taken in zip(has, halos):
+
+        @pl.when(exists)
+        def _():
+            copies.start(taken)
+
+    for taken in groups[1:]:
+        copies.start(taken)
 
     blank = jnp.zeros((PAD, LANES), F32)
     for ref, fields in ((v0, 5), (u, 3), (v1, 5)):
@@ -408,92 +429,6 @@
 
     lane = lax.broadcasted_iota(jnp.int32, (cn, LANES), 1)
     first, last = lane == 0, lane == LANES - 1
-
-    for exists, taken in zip(has, halos):
-
-        @pl.when(exists)
-        def _():
-            copies.wait(taken)
-
-    copies.wait(groups[0])
-    copies.wait(groups[1])
-
-    @pl.loop(0, ce + 2)
-    def _(i):
-        for g in range(2, len(groups)):
-
-            @pl.when(i == 1 + step * (g - 1))
-            def _():
-                copies.wait(groups[g])
-
-        real = jnp.logical_and(
-            jnp.logical_or(i > 0, has[0]), jnp.logical_or(i < ce + 1, has[1])
-        )
-
-        @pl.when(real)
-        def _():
-            mid = i + 1
-            flows = [halves(u, k, mid, cn) for k in range(3)]
-            bends = []
-            for k in range(3):
-                a, b = halves(u, k, mid + 1, cn), halves(u, k, mid - 1, cn)
-                n, s = halves(u, k, mid, cn, 1), halves(u, k, mid, cn, -1)
-                up, down = level_shifts(flows[k], first, last)
-                res = [(a[h] + b[h]) + (n[h] + s[h]) + (up[h] + down[h]) - 6.0 * flows[k][h] for h in two]
-                for h in two:
-                    curv[k, i, h] = res[h]
-                bends.append(res)
-            out = slab_sweep(
-                v0, mid, cn, first, last,
-                lambda f: [src[f, i, h] for h in two],
-                flows, [1.0 + ed[i, h] for h in two], bends,
-            )
-            for f in range(5):
-                for h in two:
-                    v1[f, i, h, inner, :] = out[f][h]
-
-        @pl.when(jnp.logical_not(real))
-        def _():
-            for f in range(5):
-                for h in two:
-                    v1[f, i, h, inner, :] = jnp.zeros((cn, LANES), F32)
-
-    @pl.loop(0, ce)
-    def _(e):
-        i = e + 1
-        flows = [halves(u, k, i + 1, cn) for k in range(3)]
-        bends = [[curv[k, i, h] for h in two] for k in range(3)]
-        out = slab_sweep(
-            v1, i, cn, first, last,
-            lambda f: [src[f, i, h] for h in two],
-            flows, [1.0 + ed[i, h] for h in two], bends,
-        )
-        def put(coef, k, line):
-            coef[pl.ds(k * ce + e, 1), :] = jnp.concatenate(line, axis=1)
-
-        at = pl.ds(pl.multiple_of(e * cn, cn), cn)
-        below = pl.ds(pl.multiple_of((ce + e) * cn, cn), cn)
-        for h in two:
-            force = flows[0][h] * jnp.abs(flows[0][h])
-            for f in range(5):
-                held[f, e, :, part(h)] = out[f][h]
-                edge_low[f, e, :, part(h)] = out[f][h][0:SUB]
-                edge_high[f, e, :, part(h)] = out[f][h][cn - SUB : cn]
-            for c in range(COMPS):
-                hi, lo = split(out[c if c < 3 else 4][h] * force)
-                wide = pl.ds(c * cz + h * LANES, LANES)
-                table[at, wide] = hi
-                table[below, wide] = lo
-        for coef, row, behind in ((coef_low, 0, 1), (coef_high, cn - 1, cn - 2)):
-            for k in range(3):
-                put(coef, k, [bends[k][h][row : row + 1] for h in two])
-                put(coef, 6 + k, [v1[k, i, h, PAD + row : PAD + row + 1, :] for h in two])
-            put(coef, 3, [flows[1][h][behind : behind + 1] for h in two])
-            put(coef, 4, [ed[i, h, behind : behind + 1, :] for h in two])
-            put(coef, 5, [flows[0][h][behind : behind + 1] for h in two])
-
-    done = copies.take((held, final))
-    copies.start(done)
 
     live = count[0]
     cell, tur = cells[...], turbine[...]
@@ -544,20 +479,110 @@
             entries = jnp.concatenate(rows, axis=1).astype(BF16)
             items[q] = lax.dot_general(entries, where, (((1,), (1,)), ((), ())), preferred_element_type=F32)
 
+    @pl.when(has[0])
+    def _():
+        copies.wait(halos[0])
+
+    @pl.loop(0, ce + 2)
+    def _(i):
+        @pl.when(jnp.logical_and(i < ce, lax.rem(i, STEP) == 0))
+        def _():
+            copies.wait((groups[0][0] + lax.div(i, STEP) * per, group(i)))
+
+        @pl.when(jnp.logical_and(i == ce, has[1]))
+        def _():
+            copies.wait(halos[1])
+
+        real = jnp.logical_and(
+            jnp.logical_or(i > 0, has[0]), jnp.logical_or(i < ce + 1, has[1])
+        )
+
+        @pl.when(real)
+        def _():
+            mid = i + 1
+            flows = [halves(u, k, mid, cn) for k in range(3)]
+            bends = []
+            for k in range(3):
+                a, b = halves(u, k, mid + 1, cn), halves(u, k, mid - 1, cn)
+                n, s = halves(u, k, mid, cn, 1), halves(u, k, mid, cn, -1)
+                up, down = level_shifts(flows[k], first, last)
+                res = [(a[h] + b[h]) + (n[h] + s[h]) + (up[h] + down[h]) - 6.0 * flows[k][h] for h in two]
+                for h in two:
+                    curv[k, i, h] = res[h]
+                bends.append(res)
+            out = slab_sweep(
+                v0, mid, cn, first, last,
+                lambda f: [src[f, i, h] for h in two],
+                flows, [1.0 + ed[i, h] for h in two], bends,
+            )
+            for f in range(5):
+                for h in two:
+                    v1[f, i, h, inner, :] = out[f][h]
+
+        @pl.when(jnp.logical_not(real))
+        def _():
+            for f in range(5):
+                for h in two:
+                    v1[f, i, h, inner, :] = jnp.zeros((cn, LANES), F32)
+
+    def leave(e):
+        return [(held.at[:, pl.ds(e, STEP)], final.at[:, pl.ds(e, STEP)])]
+
+    outs = [copies.take(*leave(e)) for e in range(0, ce, STEP)]
+
+    @pl.loop(0, ce)
+    def _(e):
+        i = e + 1
+        flows = [halves(u, k, i + 1, cn) for k in range(3)]
+        bends = [[curv[k, i, h] for h in two] for k in range(3)]
+        out = slab_sweep(
+            v1, i, cn, first, last,
+            lambda f: [src[f, i, h] for h in two],
+            flows, [1.0 + ed[i, h] for h in two], bends,
+        )
+        def put(coef, k, line):
+            coef[pl.ds(k * ce + e, 1), :] = jnp.concatenate(line, axis=1)
+
+        at = pl.ds(pl.multiple_of(e * cn, cn), cn)
+        below = pl.ds(pl.multiple_of((ce + e) * cn, cn), cn)
+        for h in two:
+            force = flows[0][h] * jnp.abs(flows[0][h])
+            for f in range(5):
+                held[f, e, :, part(h)] = out[f][h]
+                edge_low[f, e, :, part(h)] = out[f][h][0:SUB]
+                edge_high[f, e, :, part(h)] = out[f][h][cn - SUB : cn]
+            for c in range(COMPS):
+                hi, lo = split(out[c if c < 3 else 4][h] * force)
+                wide = pl.ds(c * cz + h * LANES, LANES)
+                table[at, wide] = hi
+                table[below, wide] = lo
+        for coef, row, behind in ((coef_low, 0, 1), (coef_high, cn - 1, cn - 2)):
+            for k in range(3):
+                put(coef, k, [bends[k][h][row : row + 1] for h in two])
+                put(coef, 6 + k, [v1[k, i, h, PAD + row : PAD + row + 1, :] for h in two])
+            put(coef, 3, [flows[1][h][behind : behind + 1] for h in two])
+            put(coef, 4, [ed[i, h, behind : behind + 1, :] for h in two])
+            put(coef, 5, [flows[0][h][behind : behind + 1] for h in two])
+
+        @pl.when(lax.rem(e, STEP) == STEP - 1)
+        def _():
+            copies.start((outs[0][0] + lax.div(e, STEP), leave(e - (STEP - 1))))
+
+
     row_t, level_t, local_t, load_t = line.astype(F32).T, level.T, local.T, load.T
     grad[...] = jnp.zeros_like(grad)
-    size = min(BLOCK, chunks * LANES)
-    for base in range(0, chunks * LANES, size):
-
-        @pl.when(base < live)
-        def _():
-            cols = [columns(x, base, size) for x in (row_t, level_t, local_t, load_t)]
-            rotor_terms(*cols, lines(key, base, size), table, blocks, grad)
-
-    copies.wait(done)
-
-
-def sweeps(flags, count, start, source, flow, eddy, faces, lists, blocks):
+    for least, size in steps_of(chunks):
+
+        @pl.when(jnp.logical_and(live > least, live <= size))
+        def _():
+            cols = [columns(x, 0, size) for x in (row_t, level_t, local_t, load_t)]
+            rotor_terms(*cols, lines(key, 0, size), table, blocks, grad)
+
+    for taken in outs:
+        copies.wait(taken)
+
+
+def sweeps(count, start, source, flow, eddy, faces, lists, blocks):
     _, ce, cn, cz = start.shape
     chunks = lists[0].shape[0]
     edge = shape(5, ce, SUB, cz)
@@ -573,7 +598,7 @@
             shape(chunks, ITEM, LANES),
             jax.ShapeDtypeStruct((1,), jnp.int32),
         ),
-        in_specs=[whole(pltpu.SMEM)] * 2 + [whole(pltpu.HBM)] * 6 + [whole()] * 4,
+        in_specs=[whole(pltpu.SMEM)] + [whole(pltpu.HBM)] * 6 + [whole()] * 4,
         out_specs=(whole(pltpu.HBM),) + (whole(),) * 6 + (whole(pltpu.SMEM),),
         scratch_shapes=[
             VMEM((5, ce + 4, 2, PAD + cn + PAD, LANES), F32),
@@ -584,23 +609,23 @@
             VMEM((3, ce + 2, 2, cn, LANES), F32),
             VMEM(start.shape, F32),
             VMEM((2 * ce * cn, COMPS * cz), BF16),
-            pltpu.SemaphoreType.DMA((24 + 8 * (ce // 4) + 1,)),
+            pltpu.SemaphoreType.DMA((24 + 9 * (ce // STEP),)),
         ],
         compiler_params=params(48),
         cost_estimate=cost(300 * start.size // 5, 10 << 20),
-    )(flags, count, start, source, flow, eddy, *faces, *lists)
+    )(count, start, source, flow, eddy, *faces, *lists)
 
 
 def edge_kernel(
     ce, cn, cz, blocks, copies_out,
-    flags, n_items, facep, facen, own_low, own_high, coef_low, coef_high, got_prev, got_next,
+    n_items, facep, facen, own_low, own_high, coef_low, coef_high, got_prev, got_next,
     edge_low, edge_high, items, grad, final_in,
     final, chunks,
     low_out, high_out, table, acc, sems,
 ):
     east, level = plane_shifts(ce, cz)
     sub = lax.broadcasted_iota(jnp.int32, (SUB, cz), 0)
-    has = [flags[k].astype(F32) for k in range(4)]
+    has = [x.astype(F32) for x in neighbours()]
     sides = (
         (-1.0, 0, own_low, coef_low, got_prev, edge_low, low_out, 0),
         (1.0, cn - 1, own_high, coef_high, got_next, edge_high, high_out, cn - SUB),
@@ -670,13 +695,11 @@
 
     acc[...] = grad[...]
     live = n_items[0]
-    count = items.shape[0]
-    per = min(BLOCK // LANES, count)
-    for base in range(0, count, per):
-
-        @pl.when(base * LANES < live)
-        def _():
-            lists = [items[base + k] for k in range(per)]
+    for least, size in steps_of(items.shape[0]):
+
+        @pl.when(jnp.logical_and(live > least, live <= size))
+        def _():
+            lists = [items[k] for k in range(size // LANES)]
             turned = [x.T for x in lists]
 
             def col(j):
@@ -691,14 +714,14 @@
         copy.wait()
 
 
-def edges(flags, n_items, faces, packs, coefs, gots, tiles, items, grad, final, blocks, size):
+def edges(n_items, faces, packs, coefs, gots, tiles, items, grad, final, blocks, size):
     _, ce, cn, cz = final.shape
-    args = (flags, n_items, *faces, *packs, *coefs, *gots, *tiles, items, grad, final)
+    args = (n_items, *faces, *packs, *coefs, *gots, *tiles, items, grad, final)
     tile = VMEM((5, ce, SUB, cz), F32)
     return pl.pallas_call(
         functools.partial(edge_kernel, ce, cn, cz, blocks, size),
         out_shape=(shape(*final.shape), shape(size, blocks * SECT, LANES)),
-        in_specs=[whole(pltpu.SMEM)] * 2 + [whole()] * (len(args) - 3) + [whole(pltpu.HBM)],
+        in_specs=[whole(pltpu.SMEM)] + [whole()] * (len(args) - 2) + [whole(pltpu.HBM)],
         out_specs=(whole(pltpu.HBM), whole()),
         scratch_shapes=[
             tile,
@@ -725,6 +748,7 @@
         out_shape=shape(COMPS, SECT, TURB_DEV),
         in_specs=[whole()],
         out_specs=whole(),
+        compiler_params=params(4),
         cost_estimate=cost(parts.size, parts.size * 4),
     )(parts)
 
@@ -757,26 +781,20 @@
 ):
     _, ce, cn, cz = adjoint_start.shape
     n_east, n_north = lax.axis_size("east"), lax.axis_size("north")
-    east, north = lax.axis_index("east"), lax.axis_index("north")
-    flags = jnp.stack([east > 0, east < n_east - 1, north > 0, north < n_north - 1]).astype(jnp.int32)
     count = rotor_count.reshape(1)
     slots = rotor_cell.shape[-1]
     lists = [x.reshape(slots // LANES, LANES) for x in (rotor_cell, rotor_turbine, rotor_sector, rotor_weight)]
 
-    if n_east == 2:
-        at = jnp.stack([(1 - east) * (ce - 1), (1 - east) * (ce - 1) + 2 * east - 1])
-    else:
-        at = jnp.array([0, 1, ce - 1, ce - 2])
-    at, n_faces = at.astype(jnp.int32), 1 if n_east == 2 else 2
-    ends = beside(row_ends(at, adjoint_start, base_flow, n_faces), n_east)
-    packs, own = pack(at, flags, ends, adjoint_start, adjoint_source, base_flow, eddy_visc, n_faces)
+    n_faces = 1 if n_east == 2 else 2
+    ends = beside(row_ends(adjoint_start, base_flow, n_faces), n_east)
+    packs, own = pack(ends, adjoint_start, adjoint_source, base_flow, eddy_visc, n_faces)
     gots = north_ways(packs, n_north)
     faces = beside(own, n_east)
     final, low, high, coef_low, coef_high, grad, items, n_items = sweeps(
-        flags, count, adjoint_start, adjoint_source, base_flow, eddy_visc, faces, lists, n_north
+        count, adjoint_start, adjoint_source, base_flow, eddy_visc, faces, lists, n_north
     )
     final, chunks = edges(
-        flags, n_items, faces, packs, (coef_low, coef_high), gots, (low, high), items, grad, final,
+        n_items, faces, packs, (coef_low, coef_high), gots, (low, high), items, grad, final,
         n_north, n_east,
     )
     chunks = chunks.reshape(n_east * n_north, SECT, LANES)

time: 51.2 us -> 46.7 us (0.912)
  Pallas kernels: 26.6 us -> 20.1 us
  blocking collectives: 12.9 us -> 15.1 us
  other arithmetic: 1.21 us -> 0 us
  waiting for transfers between devices: 0.36 us -> 1.06 us
    pallas_call x1, Pallas kernels: 15.8 us -> 11.5 us  [sweeps(): pl.pallas_call(functools.partial(sweeps_kernel, ce, cn, cz, blocks), out_...]
    all_to_all x1, blocking collectives: 12.9 us -> 15.1 us  [shards(): parts = lax.all_to_all(chunks, ('east', 'north'), 0, 0, tiled=True)]
    pallas_call x1, Pallas kernels: 1.61 us -> 0.71 us  [sum_parts(): pl.pallas_call(sum_kernel, out_shape=shape(COMPS, SECT, TURB_DEV), in_spe...]
    ppermute x2, waiting for transfers between devices: 0.35 us -> 1.05 us  [beside(): got = lax.ppermute(x[0], 'east', [(0, 1), (1, 0)])]
    pallas_call x1, Pallas kernels: 2.13 us -> 1.48 us  [row_ends(): pl.pallas_call(functools.partial(ends_kernel, ce, cn, n_faces), out_shape...]
    convert_element_type x1 -> x0, other arithmetic: 0.65 us -> none  [shards(): jnp.stack([east > 0, east < n_east - 1, north > 0, north < n_north - 1])]
    another operation x1 -> x0, other arithmetic: 0.56 us -> none  [shards(): jnp.stack([(1 - east) * (ce - 1), (1 - east) * (ce - 1) + 2 * east - 1])]
    pallas_call x1, Pallas kernels: 2.67 us -> 2.16 us  [edges(): pl.pallas_call(functools.partial(edge_kernel, ce, cn, cz, blocks, size),...]
  transfers between devices with their start and end apart: 4 -> 4, of which waited for: 1 -> 1; matrix products, arithmetic and copies ran while one was open for 1% -> 0% of each run, Pallas kernels for 31% -> 25%
where the time goes in v3:
time: 46.7 us; the launch traced here: 45.8 us
  Pallas kernels  20.1 us (43%)
  blocking collectives  15.1 us (32%)
  starting transfers between devices  7.41 us (16%)
  between operations  1.48 us (3%)
  waiting for transfers between devices  1.06 us (2%)
  local copies, waits for them, and re-layouts  0.65 us (1%)
    all_to_all x1, blocking collectives, shards(): parts = lax.all_to_all(chunks, ('east', 'north'), 0, 0, tiled=True)  15.1 us
    pallas_call x1, Pallas kernels, sweeps(): pl.pallas_call(functools.partial(sweeps_kernel, ce, cn, cz, blocks), out_...  11.5 us
    ppermute x2, starting transfers between devices, north_ways(): return (lax.ppermute(x[1], 'north', up), lax.ppermute(x[0], 'north', down))  6.48 us
    pallas_call x1, Pallas kernels, pack(): pl.pallas_call(functools.partial(pack_kernel, ce, cn, cz, n_faces), out_s...  4.28 us
    pallas_call x1, Pallas kernels, edges(): pl.pallas_call(functools.partial(edge_kernel, ce, cn, cz, blocks, size),...  2.16 us
    pallas_call x1, Pallas kernels, row_ends(): pl.pallas_call(functools.partial(ends_kernel, ce, cn, n_faces), out_shape...  1.48 us
    ppermute x2, waiting for transfers between devices, beside(): got = lax.ppermute(x[0], 'east', [(0, 1), (1, 0)])  1.05 us
  transfers between devices with their start and end apart: 4, of which 1 were waited for; matrix products, arithmetic and copies ran while one was open for 0% of the time, Pallas kernels for 25%

profile of v3, /device:TPU:0, one launch (start us, length us, event | category | flops | bytes accessed | tf_op | source)
XLA Modules:
  0.0 45.8 jit_solution(1199530832099501444)
XLA Ops:
  0.6 1.5 %shard_map.104 = f32[16,256]{1,0:T(8,128)} custom-call(f32[5,16,32,256]{3,2,1,0:T(8,128)} %start.5, f32[3,16,32,256]{3,2,1,0:T(8,128)} %flow.5), custom_call_target="tpu_custom_call" | custom-call | bytes 65536 | tf_op jit(solution)/shard_map/pallas_call | solution.py:140
  2.1 0.0 copy-start
  2.1 0.0 copy-start.1
  2.1 0.0 copy-start.4
  2.2 0.0 copy-start.5
  2.2 0.0 copy-start.6
  2.2 0.0 copy-start.7
  2.2 0.5 %collective-permute-start = (f32[16,256]{1,0:T(8,128)}, f32[16,256]{1,0:T(8,128)S(1)}, u32[]{:S(2)}, u32[]{:S(2)}) collective-permute-start(f32[16,256]{1,0:T(8,128)} %shard_map.104), channel_id=1, source_target_pairs={{0,16},{16,0},{1,17},{17,1},{2,18},{18,2},{3,19},{19,3},{4,20},{20... | collective-permute-start | bytes 49160 | tf_op jit(solution)/shard_map/ppermute | solution.py:758
  2.7 1.0 %collective-permute-done.endp.endn = f32[16,256]{1,0:T(8,128)S(1)} collective-permute-done((f32[16,256]{1,0:T(8,128)}, f32[16,256]{1,0:T(8,128)S(1)}, u32[]{:S(2)}, u32[]{:S(2)}) %collective-permute-start) | collective-permute-done | bytes 16416 | tf_op jit(solution)/shard_map/ppermute | solution.py:758
  3.8 0.0 copy-start.8
  3.8 0.6 %copy-done.8 = f32[16,256]{1,0:T(8,128)} copy-done((f32[16,256]{1,0:T(8,128)}, f32[16,256]{1,0:T(8,128)S(1)}, u32[]{:S(2)}) %copy-start.8) | copy-done | bytes 16408
  4.4 4.3 %shard_map.105 = (f32[240,256]{1,0:T(8,128)}, f32[240,256]{1,0:T(8,128)}, f32[22,32,256]{2,1,0:T(8,128)}) custom-call(f32[16,256]{1,0:T(8,128)} %copy-done.8, f32[16,256]{1,0:T(8,128)} %copy-done.8, f32[5,16,32,256]{3,2,1,0:T(8,128)} %start.5, f32[5,16,32,256]{3,2,1,0:T(8,128)} %source.3, f32[3,16,32,256]{3,2,1,0:T(8,128)} %flow.5, f32[16,32,256]{2,1,0:T(8,128)} %eddy.3), custom_call_target="tpu_custom_call" | custom-call | flops 4194304 | bytes 4194304 | tf_op jit(solution)/shard_map/pallas_call | solution.py:241
  8.7 0.4 collective-permute-start.1
  9.1 1.3 %collective-permute-start.3 = (f32[240,256]{1,0:T(8,128)}, f32[240,256]{1,0:T(8,128)S(1)}, u32[]{:S(2)}, u32[]{:S(2)}) collective-permute-start(f32[240,256]{1,0:T(8,128)} %get-tuple-element.17.own_low), channel_id=1, source_target_pairs={{1,0},{2,1},{3,2},{4,3},{5,4},{6,5},{7,6},{8,7},{9,8},{10,9},{11,1... | collective-permute-start | bytes 737288 | tf_op jit(solution)/shard_map/ppermute | solution.py:768
  10.4 5.2 %collective-permute-start.2 = (f32[240,256]{1,0:T(8,128)}, f32[240,256]{1,0:T(8,128)S(1)}, u32[]{:S(2)}, u32[]{:S(2)}) collective-permute-start(f32[240,256]{1,0:T(8,128)} %get-tuple-element.18.own_high), channel_id=1, source_target_pairs={{0,1},{1,2},{2,3},{3,4},{4,5},{5,6},{6,7},{7,8},{8,9},{9,10},{10,1... | collective-permute-start | bytes 737288 | tf_op jit(solution)/shard_map/ppermute | solution.py:768
  16.2 0.0 collective-permute-done.1.facep.facen
  16.2 0.0 copy-done
  16.2 0.0 copy-done.1
  16.2 0.0 copy-done.4
  16.2 0.0 copy-done.5
  16.3 0.0 copy-done.6
  16.3 0.0 copy-done.7
  16.3 0.0 copy-start.2
  16.3 0.0 copy-start.3
  16.3 11.5 %shard_map.106 = (f32[5,16,32,256]{3,2,1,0:T(8,128)}, f32[5,16,8,256]{3,2,1,0:T(8,128)S(1)}, f32[5,16,8,256]{3,2,1,0:T(8,128)S(1)}, f32[144,256]{1,0:T(8,128)S(1...) custom-call(s32[1]{0:T(128)} %bitcast.6.count, ...), custom_call_target="tpu_custom_call" | custom-call | flops 39321600 | bytes 10485760 | tf_op jit(solution)/shard_map/pallas_call | solution.py:589
  27.8 0.0 collective-permute-done.3.got_next
  27.8 0.0 collective-permute-done.2.got_prev
  27.8 0.0 copy-done.2
  27.9 0.0 copy-done.3
  27.9 2.2 %shard_map.107 = (f32[5,16,32,256]{3,2,1,0:T(8,128)}, f32[2,128,128]{2,1,0:T(8,128)S(1)}) custom-call(s32[1]{0:T(128)} %get-tuple-element.16.n_items, f32[22,32,256]{2,1,0:T(8,128)S(1)} %collective-permute-done.1.facep.facen, f32[22,32,256]{2,1,0:T(8,128)S(1)} %collective-permute-done.1.facep.facen, ...), custom_call_target="tpu_custom_call", output_to_operand_aliasing={{0}: (13, {})} | custom-call | flops 16777216 | bytes 4194304 | tf_op jit(solution)/shard_map/pallas_call | solution.py:721
  30.0 15.1 %all_to_all.5.parts = f32[32,8,128]{2,1,0:T(8,128)S(1)} all-to-all(f32[32,8,128]{2,1,0:T(8,128)S(1)} %bitcast.7), channel_id=1, replica_groups=mesh['east'=2,'north'=16] {'east','north'}, dimensions={0} | all-to-all | bytes 262144 | tf_op jit(solution)/shard_map/all_to_all | solution.py:801
  45.1 0.7 %shard_map.108 = f32[4,8,12]{2,1,0:T(8,128)} custom-call(f32[32,8,128]{2,1,0:T(8,128)S(1)} %all_to_all.5.parts), custom_call_target="tpu_custom_call" | custom-call | flops 32768 | bytes 131072 | tf_op jit(solution)/shard_map/pallas_call | solution.py:746
Async XLA Ops:
  2.1 14.1 %copy-start = (f32[3,16,32,256]{3,2,1,0:T(8,128)S(1)}, f32[3,16,32,256]{3,2,1,0:T(8,128)}, u32[]{:S(2)}) copy-start(f32[3,16,32,256]{3,2,1,0:T(8,128)} %flow.5) | copy-start | bytes 4718596
  2.1 14.1 %copy-start.1 = (f32[16,32,256]{2,1,0:T(8,128)S(1)}, f32[16,32,256]{2,1,0:T(8,128)}, u32[]{:S(2)}) copy-start(f32[16,32,256]{2,1,0:T(8,128)} %eddy.3) | copy-start | bytes 1572868
  2.1 14.1 %copy-start.4 = (s32[1,1,1024]{2,1,0:T(1,128)S(1)}, s32[1,1,1024]{2,1,0:T(1,128)}, u32[]{:S(2)}) copy-start(s32[1,1,1024]{2,1,0:T(1,128)} %param.14) | copy-start | bytes 12292
  2.2 14.1 %copy-start.5 = (s32[1,1,1024]{2,1,0:T(1,128)S(1)}, s32[1,1,1024]{2,1,0:T(1,128)}, u32[]{:S(2)}) copy-start(s32[1,1,1024]{2,1,0:T(1,128)} %param.15) | copy-start | bytes 12292
  2.2 14.1 %copy-start.6 = (s32[1,1,1024]{2,1,0:T(1,128)S(1)}, s32[1,1,1024]{2,1,0:T(1,128)}, u32[]{:S(2)}) copy-start(s32[1,1,1024]{2,1,0:T(1,128)} %param.16) | copy-start | bytes 12292
  2.2 14.1 %copy-start.7 = (f32[1,1,1024]{2,1,0:T(1,128)S(1)}, f32[1,1,1024]{2,1,0:T(1,128)}, u32[]{:S(2)}) copy-start(f32[1,1,1024]{2,1,0:T(1,128)} %param.17) | copy-start | bytes 12292
  2.2 1.6 %collective-permute-start = (f32[16,256]{1,0:T(8,128)}, f32[16,256]{1,0:T(8,128)S(1)}, u32[]{:S(2)}, u32[]{:S(2)}) collective-permute-start(f32[16,256]{1,0:T(8,128)} %shard_map.104), channel_id=1, source_target_pairs={{0,16},{16,0},{1,17},{17,1},{2,18},{18,2},{3,19},{19,3},{4,20},{20... | collective-permute-start | bytes 49160 | tf_op jit(solution)/shard_map/ppermute | solution.py:758
  3.8 0.6 %copy-start.8 = (f32[16,256]{1,0:T(8,128)}, f32[16,256]{1,0:T(8,128)S(1)}, u32[]{:S(2)}) copy-start(f32[16,256]{1,0:T(8,128)S(1)} %collective-permute-done.endp.endn) | copy-start | bytes 49156
  8.7 7.6 %collective-permute-start.1 = (f32[22,32,256]{2,1,0:T(8,128)}, f32[22,32,256]{2,1,0:T(8,128)S(1)}, u32[]{:S(2)}, u32[]{:S(2)}) collective-permute-start(f32[22,32,256]{2,1,0:T(8,128)} %get-tuple-element.15), channel_id=1, source_target_pairs={{0,16},{16,0},{1,17},{17,1},{2,18},{18,2},{3,19},{19,3},{4,20},{20... | collective-permute-start | bytes 2162696 | tf_op jit(solution)/shard_map/ppermute | solution.py:758
  9.1 18.8 %collective-permute-start.3 = (f32[240,256]{1,0:T(8,128)}, f32[240,256]{1,0:T(8,128)S(1)}, u32[]{:S(2)}, u32[]{:S(2)}) collective-permute-start(f32[240,256]{1,0:T(8,128)} %get-tuple-element.17.own_low), channel_id=1, source_target_pairs={{1,0},{2,1},{3,2},{4,3},{5,4},{6,5},{7,6},{8,7},{9,8},{10,9},{11,1... | collective-permute-start | bytes 737288 | tf_op jit(solution)/shard_map/ppermute | solution.py:768
  10.4 17.5 %collective-permute-start.2 = (f32[240,256]{1,0:T(8,128)}, f32[240,256]{1,0:T(8,128)S(1)}, u32[]{:S(2)}, u32[]{:S(2)}) collective-permute-start(f32[240,256]{1,0:T(8,128)} %get-tuple-element.18.own_high), channel_id=1, source_target_pairs={{0,1},{1,2},{2,3},{3,4},{4,5},{5,6},{6,7},{7,8},{8,9},{9,10},{10,1... | collective-permute-start | bytes 737288 | tf_op jit(solution)/shard_map/ppermute | solution.py:768
  16.3 11.6 %copy-start.2 = (f32[240,256]{1,0:T(8,128)S(1)}, f32[240,256]{1,0:T(8,128)}, u32[]{:S(2)}) copy-start(f32[240,256]{1,0:T(8,128)} %get-tuple-element.17.own_low) | copy-start | bytes 737284
  16.3 11.6 %copy-start.3 = (f32[240,256]{1,0:T(8,128)S(1)}, f32[240,256]{1,0:T(8,128)}, u32[]{:S(2)}) copy-start(f32[240,256]{1,0:T(8,128)} %get-tuple-element.18.own_high) | copy-start | bytes 737284

commit v4 on v3

--- a/solution.py
+++ b/solution.py
@@ -16,8 +16,11 @@
 PACK = 14
 FACE = 22
 EDGE = 9
+RAW = 23
 ITEM = 8
-STEP = 2
+STEP = 4
+ROWS_1 = 8
+ROWS_2 = 16
 VMEM = pltpu.VMEM
 F32 = jnp.float32
 BF16 = jnp.bfloat16
@@ -278,6 +281,53 @@
     return list(zip(sizes[:-1], sizes[1:]))
 
 
+def entries(live, cells, turbine, sector, weight, cz):
+    cell, tur = cells[...], turbine[...]
+    owner = owner_of(tur)
+    key = (owner * SECT + sector[...]).astype(F32)
+    local = (tur - owner * TURB_DEV).astype(F32)
+    slot = lax.broadcasted_iota(jnp.int32, cell.shape, 0) * LANES + lax.broadcasted_iota(jnp.int32, cell.shape, 1)
+    load = jnp.where(slot < live, weight[...], 0.0)
+    line = lax.shift_right_logical(cell, cz.bit_length() - 1)
+    level = jnp.bitwise_and(cell, cz - 1).astype(F32)
+    return slot, line, level, key, local, load
+
+
+def gather_edge(chosen, edge_row, level, key, local, load, put):
+    chunks = chosen.shape[0]
+    lower = lax.broadcasted_iota(jnp.int32, (LANES, LANES), 0) < lax.broadcasted_iota(jnp.int32, (LANES, LANES), 1)
+    rank = jnp.dot(chosen.astype(BF16), jnp.where(lower, 1.0, 0.0).astype(BF16), preferred_element_type=F32)
+    sums = jnp.sum(chosen, axis=1, keepdims=True)
+    so_far = jnp.zeros((1, 1), F32)
+    starts = []
+    for k in range(chunks):
+        starts.append(so_far)
+        so_far = so_far + sums[k : k + 1]
+    rank = jnp.where(chosen > 0.0, rank + jnp.concatenate(starts, axis=0), -1.0)
+    total = jnp.sum(chosen).astype(jnp.int32)
+    load_high = load.astype(BF16).astype(F32)
+    load_rest = load - load_high
+    load_mid = load_rest.astype(BF16).astype(F32)
+    load_low = load_rest - load_mid
+    blank = jnp.zeros((1, LANES), F32)
+    rows = [
+        jnp.concatenate([x[k : k + 1] for x in (edge_row, level, key, local, load_high, load_mid, load_low)] + [blank])
+        for k in range(chunks)
+    ]
+    to = lax.broadcasted_iota(jnp.int32, (LANES, LANES), 0).astype(F32)
+    for q in range(chunks):
+
+        @pl.when(q * LANES < total)
+        def _():
+            where = jnp.concatenate(
+                [jnp.where(rank[k : k + 1] - float(q * LANES) == to, 1.0, 0.0) for k in range(chunks)], axis=1
+            ).astype(BF16)
+            entries = jnp.concatenate(rows, axis=1).astype(BF16)
+            put(q, lax.dot_general(entries, where, (((1,), (1,)), ((), ())), preferred_element_type=F32))
+
+    return total
+
+
 def rotor_terms(row, level, turbine, weight, key, table, blocks, acc):
     size = row.shape[0]
     rows, width = table.shape[0] // 2, table.shape[1]
@@ -303,8 +353,9 @@
     acc[...] += parts[:, :LANES] + parts[:, LANES : 2 * LANES] + parts[:, 2 * LANES :]
 
 
-def halves(ref, f, i, cn, move=0):
-    return [ref[f, i, h, pl.ds(PAD + move, cn), :] for h in range(2)]
+def halves(ref, f, i, rows, move=0):
+    first, size = rows
+    return [ref[f, i, h, pl.ds(PAD + first + move, size), :] for h in range(2)]
 
 
 def level_shifts(x, first, last):
@@ -316,16 +367,16 @@
     )
 
 
-def slab_sweep(ref, i, cn, first, last, src, flow, visc, curv):
+def slab_sweep(ref, i, rows, first, last, src, flow, visc, curv):
     two = range(2)
     w = visc
     inv = [inverses(w[h]) for h in two]
     w2 = [2.0 * w[h] for h in two]
 
     def sides(f):
-        mid = halves(ref, f, i, cn)
-        a, b = halves(ref, f, i + 1, cn), halves(ref, f, i - 1, cn)
-        n, s = halves(ref, f, i, cn, 1), halves(ref, f, i, cn, -1)
+        mid = halves(ref, f, i, rows)
+        a, b = halves(ref, f, i + 1, rows), halves(ref, f, i - 1, rows)
+        n, s = halves(ref, f, i, rows, 1), halves(ref, f, i, rows, -1)
         up, down = level_shifts(mid, first, last)
         return mid, a, b, n, s, up, down
 
@@ -355,11 +406,13 @@
 
 
 def sweeps_kernel(
-    ce, cn, cz, blocks,
+    ce, cn, cz, blocks, pair,
     count, start, source, flow, eddy, facep, facen, cells, turbine, sector, weight,
-    final, edge_low, edge_high, coef_low, coef_high, grad, items, n_items,
-    v0, u, src, ed, v1, curv, held, table, sems,
+    final, held, grad, *refs,
 ):
+    if not pair:
+        coef_low, coef_high, items, n_items = refs[:4]
+    v0, u, src, ed, v1, curv, table, sems = refs[-8:]
     copies = Copies(sems)
     two = range(2)
     has = [x > 0 for x in neighbours()[:2]]
@@ -374,7 +427,7 @@
             pairs += [
                 (face.at[0:5, :, part(h)], v0.at[:, near, h, inner]),
                 (face.at[5:8, :, part(h)], u.at[:, near, h, inner]),
-                (face.at[8, :, part(h)], ed.at[slab, h]),
+                (face.at[8, :, part(h)], ed.at[0, slab, h]),
                 (face.at[9:14, :, part(h)], src.at[:, slab, h]),
                 (face.at[14:19, :, part(h)], v0.at[:, far, h, inner]),
                 (face.at[19:22, :, part(h)], u.at[:, far, h, inner]),
@@ -391,7 +444,7 @@
             pairs += [
                 (start.at[:, span, :, part(h)], v0.at[:, own2, h, inner]),
                 (flow.at[:, span, :, part(h)], u.at[:, own2, h, inner]),
-                (eddy.at[span, :, part(h)], ed.at[own, h]),
+                (eddy.at[span, :, part(h)], ed.at[0, own, h]),
                 (source.at[:, span, :, part(h)], src.at[:, own, h]),
             ]
         return pairs
@@ -427,57 +480,26 @@
                     for h in two:
                         ref[f, near, h, inner, :] = jnp.zeros((cn, LANES), F32)
 
-    lane = lax.broadcasted_iota(jnp.int32, (cn, LANES), 1)
-    first, last = lane == 0, lane == LANES - 1
+    def ends_of(size):
+        lane = lax.broadcasted_iota(jnp.int32, (size, LANES), 1)
+        return lane == 0, lane == LANES - 1
 
     live = count[0]
-    cell, tur = cells[...], turbine[...]
-    owner = owner_of(tur)
-    key = (owner * SECT + sector[...]).astype(F32)
-    local = (tur - owner * TURB_DEV).astype(F32)
-    chunks = cell.shape[0]
-    slot = lax.broadcasted_iota(jnp.int32, cell.shape, 0) * LANES + lax.broadcasted_iota(jnp.int32, cell.shape, 1)
-    load = jnp.where(slot < live, weight[...], 0.0)
-    line = lax.shift_right_logical(cell, cz.bit_length() - 1)
-    level = jnp.bitwise_and(cell, cz - 1).astype(F32)
-    north = jnp.bitwise_and(line, cn - 1)
-    east = lax.shift_right_logical(line, cn.bit_length() - 1)
-    place = jnp.where(north == 0, 0, jnp.where(north == 1, 1, jnp.where(north == cn - 1, 2, 3)))
-    is_edge = jnp.logical_or(north <= 1, north >= cn - 2)
-    chosen = jnp.where(jnp.logical_and(is_edge, slot < live), 1.0, 0.0)
-    edge_row = (place * ce + east).astype(F32)
-
-    lower = lax.broadcasted_iota(jnp.int32, (LANES, LANES), 0) < lax.broadcasted_iota(jnp.int32, (LANES, LANES), 1)
-    rank = jnp.dot(chosen.astype(BF16), jnp.where(lower, 1.0, 0.0).astype(BF16), preferred_element_type=F32)
-    sums = jnp.sum(chosen, axis=1, keepdims=True)
-    so_far = jnp.zeros((1, 1), F32)
-    starts = []
-    for k in range(chunks):
-        starts.append(so_far)
-        so_far = so_far + sums[k : k + 1]
-    rank = jnp.where(chosen > 0.0, rank + jnp.concatenate(starts, axis=0), -1.0)
-    total = jnp.sum(chosen).astype(jnp.int32)
-    n_items[0] = total
-    load_high = load.astype(BF16).astype(F32)
-    load_rest = load - load_high
-    load_mid = load_rest.astype(BF16).astype(F32)
-    load_low = load_rest - load_mid
-    blank = jnp.zeros((1, LANES), F32)
-    rows = [
-        jnp.concatenate([x[k : k + 1] for x in (edge_row, level, key, local, load_high, load_mid, load_low)] + [blank])
-        for k in range(chunks)
-    ]
-    to = lax.broadcasted_iota(jnp.int32, (LANES, LANES), 0).astype(F32)
-    items[...] = jnp.zeros_like(items)
-    for q in range(chunks):
-
-        @pl.when(q * LANES < total)
-        def _():
-            where = jnp.concatenate(
-                [jnp.where(rank[k : k + 1] - float(q * LANES) == to, 1.0, 0.0) for k in range(chunks)], axis=1
-            ).astype(BF16)
-            entries = jnp.concatenate(rows, axis=1).astype(BF16)
-            items[q] = lax.dot_general(entries, where, (((1,), (1,)), ((), ())), preferred_element_type=F32)
+    slot, line, level, key, local, load = entries(live, cells, turbine, sector, weight, cz)
+    chunks = slot.shape[0]
+    if not pair:
+        north = jnp.bitwise_and(line, cn - 1)
+        east = lax.shift_right_logical(line, cn.bit_length() - 1)
+        place = jnp.where(north == 0, 0, jnp.where(north == 1, 1, jnp.where(north == cn - 1, 2, 3)))
+        is_edge = jnp.logical_or(north <= 1, north >= cn - 2)
+        chosen = jnp.where(jnp.logical_and(is_edge, slot < live), 1.0, 0.0)
+        edge_row = (place * ce + east).astype(F32)
+        items[...] = jnp.zeros_like(items)
+
+        def put(q, x):
+            items[q] = x
+
+        n_items[0] = gather_edge(chosen, edge_row, level, key, local, load, put)
 
     @pl.when(has[0])
     def _():
@@ -500,24 +522,27 @@
         @pl.when(real)
         def _():
             mid = i + 1
-            flows = [halves(u, k, mid, cn) for k in range(3)]
-            bends = []
-            for k in range(3):
-                a, b = halves(u, k, mid + 1, cn), halves(u, k, mid - 1, cn)
-                n, s = halves(u, k, mid, cn, 1), halves(u, k, mid, cn, -1)
-                up, down = level_shifts(flows[k], first, last)
-                res = [(a[h] + b[h]) + (n[h] + s[h]) + (up[h] + down[h]) - 6.0 * flows[k][h] for h in two]
-                for h in two:
-                    curv[k, i, h] = res[h]
-                bends.append(res)
-            out = slab_sweep(
-                v0, mid, cn, first, last,
-                lambda f: [src[f, i, h] for h in two],
-                flows, [1.0 + ed[i, h] for h in two], bends,
-            )
-            for f in range(5):
-                for h in two:
-                    v1[f, i, h, inner, :] = out[f][h]
+            first, last = ends_of(ROWS_1)
+            for r in range(0, cn, ROWS_1):
+                rows, at = (r, ROWS_1), pl.ds(r, ROWS_1)
+                flows = [halves(u, k, mid, rows) for k in range(3)]
+                bends = []
+                for k in range(3):
+                    a, b = halves(u, k, mid + 1, rows), halves(u, k, mid - 1, rows)
+                    n, s = halves(u, k, mid, rows, 1), halves(u, k, mid, rows, -1)
+                    up, down = level_shifts(flows[k], first, last)
+                    res = [(a[h] + b[h]) + (n[h] + s[h]) + (up[h] + down[h]) - 6.0 * flows[k][h] for h in two]
+                    for h in two:
+                        curv[k, i, h, at, :] = res[h]
+                    bends.append(res)
+                out = slab_sweep(
+                    v0, mid, rows, first, last,
+                    lambda f: [src[f, i, h, at, :] for h in two],
+                    flows, [1.0 + ed[0, i, h, at, :] for h in two], bends,
+                )
+                for f in range(5):
+                    for h in two:
+                        v1[f, i, h, pl.ds(PAD + r, ROWS_1), :] = out[f][h]
 
         @pl.when(jnp.logical_not(real))
         def _():
@@ -533,41 +558,48 @@
     @pl.loop(0, ce)
     def _(e):
         i = e + 1
-        flows = [halves(u, k, i + 1, cn) for k in range(3)]
-        bends = [[curv[k, i, h] for h in two] for k in range(3)]
-        out = slab_sweep(
-            v1, i, cn, first, last,
-            lambda f: [src[f, i, h] for h in two],
-            flows, [1.0 + ed[i, h] for h in two], bends,
-        )
-        def put(coef, k, line):
-            coef[pl.ds(k * ce + e, 1), :] = jnp.concatenate(line, axis=1)
-
-        at = pl.ds(pl.multiple_of(e * cn, cn), cn)
-        below = pl.ds(pl.multiple_of((ce + e) * cn, cn), cn)
-        for h in two:
-            force = flows[0][h] * jnp.abs(flows[0][h])
-            for f in range(5):
-                held[f, e, :, part(h)] = out[f][h]
-                edge_low[f, e, :, part(h)] = out[f][h][0:SUB]
-                edge_high[f, e, :, part(h)] = out[f][h][cn - SUB : cn]
-            for c in range(COMPS):
-                hi, lo = split(out[c if c < 3 else 4][h] * force)
-                wide = pl.ds(c * cz + h * LANES, LANES)
-                table[at, wide] = hi
-                table[below, wide] = lo
-        for coef, row, behind in ((coef_low, 0, 1), (coef_high, cn - 1, cn - 2)):
-            for k in range(3):
-                put(coef, k, [bends[k][h][row : row + 1] for h in two])
-                put(coef, 6 + k, [v1[k, i, h, PAD + row : PAD + row + 1, :] for h in two])
-            put(coef, 3, [flows[1][h][behind : behind + 1] for h in two])
-            put(coef, 4, [ed[i, h, behind : behind + 1, :] for h in two])
-            put(coef, 5, [flows[0][h][behind : behind + 1] for h in two])
-
+        first, last = ends_of(ROWS_2)
+
+        for r in range(0, cn, ROWS_2):
+            rows, span = (r, ROWS_2), pl.ds(r, ROWS_2)
+            flows = [halves(u, k, i + 1, rows) for k in range(3)]
+            bends = [[curv[k, i, h, span, :] for h in two] for k in range(3)]
+            out = slab_sweep(
+                v1, i, rows, first, last,
+                lambda f: [src[f, i, h, span, :] for h in two],
+                flows, [1.0 + ed[0, i, h, span, :] for h in two], bends,
+            )
+            at = pl.ds(pl.multiple_of(e * cn + r, ROWS_2), ROWS_2)
+            below = pl.ds(pl.multiple_of((ce + e) * cn + r, ROWS_2), ROWS_2)
+            for h in two:
+                force = flows[0][h] * jnp.abs(flows[0][h])
+                for f in range(5):
+                    held[f, e, span, part(h)] = out[f][h]
+                for c in range(COMPS):
+                    hi, lo = split(out[c if c < 3 else 4][h] * force)
+                    wide = pl.ds(c * cz + h * LANES, LANES)
+                    table[at, wide] = hi
+                    table[below, wide] = lo
         @pl.when(lax.rem(e, STEP) == STEP - 1)
         def _():
             copies.start((outs[0][0] + lax.div(e, STEP), leave(e - (STEP - 1))))
 
+
+    def edge_plane(ref, k, first, tall, row):
+        fields, slabs = ref.shape[:2]
+        flat = ref.reshape(fields, slabs * 2 * tall, LANES)
+        return jnp.concatenate(
+            [flat[k, pl.ds((first * 2 + h) * tall + row, ce, stride=2 * tall), :] for h in two], axis=1
+        )
+
+    tall = PAD + cn + PAD
+    edge_rows = () if pair else ((coef_low, 0, 1), (coef_high, cn - 1, cn - 2))
+    for coef, row, behind in edge_rows:
+        planes = [edge_plane(curv, k, 1, cn, row) for k in range(3)]
+        planes += [edge_plane(u, 1, 2, tall, PAD + behind), edge_plane(ed, 0, 1, cn, behind), edge_plane(u, 0, 2, tall, PAD + behind)]
+        planes += [edge_plane(v1, k, 1, tall, PAD + row) for k in range(3)]
+        for k, x in enumerate(planes):
+            coef[k * ce : (k + 1) * ce, :] = x
 
     row_t, level_t, local_t, load_t = line.astype(F32).T, level.T, local.T, load.T
     grad[...] = jnp.zeros_like(grad)
@@ -582,44 +614,35 @@
         copies.wait(taken)
 
 
-def sweeps(count, start, source, flow, eddy, faces, lists, blocks):
+def sweeps(count, start, source, flow, eddy, faces, lists, blocks, pair):
     _, ce, cn, cz = start.shape
     chunks = lists[0].shape[0]
-    edge = shape(5, ce, SUB, cz)
+    tall = PAD + cn + PAD
+    more = [shape(EDGE * ce, cz)] * 2 + [shape(chunks, ITEM, LANES), jax.ShapeDtypeStruct((1,), jnp.int32)]
     return pl.pallas_call(
-        functools.partial(sweeps_kernel, ce, cn, cz, blocks),
-        out_shape=(
-            shape(*start.shape),
-            edge,
-            edge,
-            shape(EDGE * ce, cz),
-            shape(EDGE * ce, cz),
-            shape(blocks * SECT, LANES),
-            shape(chunks, ITEM, LANES),
-            jax.ShapeDtypeStruct((1,), jnp.int32),
-        ),
+        functools.partial(sweeps_kernel, ce, cn, cz, blocks, pair),
+        out_shape=[shape(*start.shape)] * 2 + [shape(blocks * SECT, LANES)] + ([] if pair else more),
         in_specs=[whole(pltpu.SMEM)] + [whole(pltpu.HBM)] * 6 + [whole()] * 4,
-        out_specs=(whole(pltpu.HBM),) + (whole(),) * 6 + (whole(pltpu.SMEM),),
+        out_specs=[whole(pltpu.HBM), whole(), whole()] + ([] if pair else [whole()] * 3 + [whole(pltpu.SMEM)]),
         scratch_shapes=[
-            VMEM((5, ce + 4, 2, PAD + cn + PAD, LANES), F32),
-            VMEM((3, ce + 4, 2, PAD + cn + PAD, LANES), F32),
+            VMEM((5, ce + 4, 2, tall, LANES), F32),
+            VMEM((3, ce + 4, 2, tall, LANES), F32),
             VMEM((5, ce + 2, 2, cn, LANES), F32),
-            VMEM((ce + 2, 2, cn, LANES), F32),
-            VMEM((5, ce + 2, 2, PAD + cn + PAD, LANES), F32),
+            VMEM((1, ce + 2, 2, cn, LANES), F32),
+            VMEM((5, ce + 2, 2, tall, LANES), F32),
             VMEM((3, ce + 2, 2, cn, LANES), F32),
-            VMEM(start.shape, F32),
             VMEM((2 * ce * cn, COMPS * cz), BF16),
             pltpu.SemaphoreType.DMA((24 + 9 * (ce // STEP),)),
         ],
         compiler_params=params(48),
-        cost_estimate=cost(300 * start.size // 5, 10 << 20),
+        cost_estimate=cost(0, 1 << 10),
     )(count, start, source, flow, eddy, *faces, *lists)
 
 
 def edge_kernel(
     ce, cn, cz, blocks, copies_out,
     n_items, facep, facen, own_low, own_high, coef_low, coef_high, got_prev, got_next,
-    edge_low, edge_high, items, grad, final_in,
+    held, items, grad, final_in,
     final, chunks,
     low_out, high_out, table, acc, sems,
 ):
@@ -627,11 +650,11 @@
     sub = lax.broadcasted_iota(jnp.int32, (SUB, cz), 0)
     has = [x.astype(F32) for x in neighbours()]
     sides = (
-        (-1.0, 0, own_low, coef_low, got_prev, edge_low, low_out, 0),
-        (1.0, cn - 1, own_high, coef_high, got_next, edge_high, high_out, cn - SUB),
+        (-1.0, 0, own_low, coef_low, got_prev, low_out, 0),
+        (1.0, cn - 1, own_high, coef_high, got_next, high_out, cn - SUB),
     )
     waits = []
-    for side, (sign, row, own, coef, got, edge, out_ref, place) in enumerate(sides):
+    for side, (sign, row, own, coef, got, out_ref, place) in enumerate(sides):
 
         def plane(ref, f):
             return ref[f * ce : (f + 1) * ce, :]
@@ -681,7 +704,7 @@
                 rows = jnp.where(
                     sub == near, add[f][e : e + 1, :], jnp.where(sub == far, behind[f][e : e + 1, :], 0.0)
                 )
-                out_ref[f, e] = edge[f, e] + rows
+                out_ref[f, e] = held[f, e, place : place + SUB, :] + rows
         copy = pltpu.make_async_copy(out_ref, final.at[:, :, pl.ds(place, SUB), :], sems.at[side])
         copy.start()
         waits.append(copy)
@@ -714,9 +737,9 @@
         copy.wait()
 
 
-def edges(n_items, faces, packs, coefs, gots, tiles, items, grad, final, blocks, size):
+def edges(n_items, faces, packs, coefs, gots, held, items, grad, final, blocks, size):
     _, ce, cn, cz = final.shape
-    args = (n_items, *faces, *packs, *coefs, *gots, *tiles, items, grad, final)
+    args = (n_items, *faces, *packs, *coefs, *gots, held, items, grad, final)
     tile = VMEM((5, ce, SUB, cz), F32)
     return pl.pallas_call(
         functools.partial(edge_kernel, ce, cn, cz, blocks, size),
@@ -736,6 +759,320 @@
     )(*args)
 
 
+def side(own):
+    e = lax.axis_index("east")
+    return 1 - e if own else e
+
+
+def raw_kernel(ce, cn, cz, own, *refs):
+    count, start, source, flow, eddy, *lists = refs[:9]
+    rows, refs = refs[9], refs[10:]
+    faces, refs = (refs[:1], refs[1:]) if own else ((), refs)
+    tiles_v, tiles_u, tiles_s, tiles_e, cells, turbine, sector, weight, sems = refs
+    copies = Copies(sems)
+    high = side(own)
+    first = pl.multiple_of(high * (cn - SUB), SUB)
+    held = copies.take(*zip(lists, (cells, turbine, sector, weight)))
+    copies.start(held)
+    pairs = []
+    for h in range(2):
+        cut = (pl.ds(first, SUB), pl.ds(h * LANES, LANES))
+        pairs += [
+            (start.at[(slice(None), slice(None)) + cut], tiles_v.at[:, :, h]),
+            (flow.at[(slice(None), slice(None)) + cut], tiles_u.at[:, :, h]),
+            (eddy.at[(slice(None),) + cut], tiles_e.at[0, :, h]),
+            (source.at[(slice(None), slice(None)) + cut], tiles_s.at[:, :, h]),
+        ]
+    needed = copies.take(*pairs)
+    copies.start(needed)
+    later = []
+    for (near, far), face in zip(facing(ce), faces):
+        later.append(
+            copies.take(
+                (start.at[:, near], face.at[0:5]),
+                (flow.at[:, near], face.at[5:8]),
+                (eddy.at[near], face.at[8]),
+                (source.at[:, near], face.at[9:14]),
+                (start.at[:, far], face.at[14:19]),
+                (flow.at[:, far], face.at[19:22]),
+            )
+        )
+        copies.start(later[-1])
+
+    copies.wait(held)
+    live = count[0]
+    slot, line, level, key, local, load = entries(live, cells, turbine, sector, weight, cz)
+    north = jnp.bitwise_and(line, cn - 1)
+    column = lax.shift_right_logical(line, cn.bit_length() - 1) + lax.axis_index("east") * ce
+    edge = high * (cn - 1)
+    behind = edge + 1 - 2 * high
+    chosen = jnp.where(jnp.logical_and(jnp.logical_or(north == edge, north == behind), slot < live), 1.0, 0.0)
+    edge_row = (jnp.where(north == behind, 2 * ce, 0) + column).astype(F32)
+    base = RAW * ce
+    tail = rows.shape[0] - base
+    rows[base:, :] = jnp.zeros((tail, cz), F32)
+
+    def put(q, x):
+        rows[base + q // 2 * ITEM : base + (q // 2 + 1) * ITEM, q % 2 * LANES : (q % 2 + 1) * LANES] = x
+
+    total = gather_edge(chosen, edge_row, level, key, local, load, put)
+    rows[base + tail - ITEM :, :] = jnp.full((ITEM, cz), total.astype(F32))
+
+    def plane(ref, f, low, top):
+        flat = ref.reshape(ref.shape[0], ce * 2 * SUB, LANES)
+        parts = []
+        for h in range(2):
+            x, y = (flat[f, pl.ds(h * SUB + at, ce, stride=2 * SUB), :] for at in (low, top))
+            parts.append(jnp.where(high > 0, y, x))
+        return jnp.concatenate(parts, axis=1)
+
+    copies.wait(needed)
+    planes = [(tiles_v, f, 0) for f in range(5)] + [(tiles_u, k, 0) for k in range(3)] + [(tiles_e, 0, 0)]
+    planes += [(tiles_s, f, 0) for f in range(5)]
+    planes += [(tiles_v, f, 1) for f in range(5)] + [(tiles_u, k, 1) for k in range(3)] + [(tiles_e, 0, 1)]
+    for k, (ref, f, at) in enumerate(planes):
+        rows[k * ce : (k + 1) * ce, :] = plane(ref, f, at, SUB - 1 - at)
+    for taken in later:
+        copies.wait(taken)
+
+
+def raw_rows(own, count, start, source, flow, eddy, lists):
+    _, ce, cn, cz = start.shape
+    chunks = lists[0].shape[0]
+    out = [shape(RAW * ce + (chunks * LANES // cz + 1) * ITEM, cz)] + ([shape(FACE, cn, cz)] if own else [])
+    return pl.pallas_call(
+        functools.partial(raw_kernel, ce, cn, cz, own),
+        out_shape=out,
+        in_specs=[whole(pltpu.SMEM)] + [whole(pltpu.HBM)] * 8,
+        out_specs=[whole()] * len(out),
+        scratch_shapes=[
+            VMEM((5, ce, 2, SUB, LANES), F32),
+            VMEM((3, ce, 2, SUB, LANES), F32),
+            VMEM((5, ce, 2, SUB, LANES), F32),
+            VMEM((1, ce, 2, SUB, LANES), F32),
+            VMEM((chunks, LANES), jnp.int32),
+            VMEM((chunks, LANES), jnp.int32),
+            VMEM((chunks, LANES), jnp.int32),
+            VMEM((chunks, LANES), F32),
+            pltpu.SemaphoreType.DMA((18,)),
+        ],
+        compiler_params=params(59),
+        cost_estimate=cost(0, 1 << 10),
+    )(count, start, source, flow, eddy, *lists)
+
+
+def joined(ce, own, other, k):
+    west = lax.axis_index("east") == 0
+    a, b = own[k * ce : (k + 1) * ce, :], other[k * ce : (k + 1) * ce, :]
+    return jnp.concatenate([jnp.where(west, a, b), jnp.where(west, b, a)], axis=0)
+
+
+def join_kernel(ce, cz, own, other, pack, coef):
+    sign = (2 * side(True) - 1).astype(F32)
+    east, level = plane_shifts(2 * ce, cz)
+    raw = [joined(ce, own, other, k) for k in range(RAW)]
+    v, u, src, inner, inner_u = raw[:5], raw[5:8], raw[9:14], raw[14:19], raw[19:22]
+    w = 1.0 + raw[8]
+    inv_v, inv_m = inverses(w)
+    total, slope0, slope2 = [], [], []
+    for f in range(5):
+        a, b = east(v[f])
+        h, l = level(v[f])
+        total.append((a + b) + (h + l))
+        slope0.append(a - b)
+        slope2.append(h - l)
+    curv = []
+    for k in range(3):
+        a, b = east(u[k])
+        h, l = level(u[k])
+        curv.append((a + b) + (h + l) + inner_u[k] - 6.0 * u[k])
+    out = one_way(1, -sign, w, u[1], inner, inv_v, inv_m, dot3(v, curv))
+    press = (slope0[3], None, slope2[3])
+    for c in range(3):
+        more = src[c] + w * total[c] + 0.5 * (u[0] * slope0[c] + u[2] * slope2[c])
+        if press[c] is not None:
+            more = more - 0.5 * press[c]
+        out[c] = out[c] + more * inv_v
+    out[3] = out[3] + (src[3] + total[3] - 0.5 * (slope0[0] + slope2[2])) * (1.0 / 7.0)
+    out[4] = out[4] + (src[4] + w * total[4]) * inv_m
+    for k, x in enumerate(raw[:9] + out):
+        pack[2 * k * ce : 2 * (k + 1) * ce, :] = x
+    for k, x in enumerate(curv + [inner_u[1], raw[22], inner_u[0]]):
+        coef[2 * k * ce : 2 * (k + 1) * ce, :] = x
+
+
+def join_rows(own, other, ce):
+    cz = own.shape[1]
+    return pl.pallas_call(
+        functools.partial(join_kernel, ce, cz),
+        out_shape=[shape(PACK * 2 * ce, cz), shape(6 * 2 * ce, cz)],
+        in_specs=[whole()] * 2,
+        out_specs=[whole()] * 2,
+        compiler_params=params(16),
+        cost_estimate=cost(0, 1 << 10),
+    )(own, other)
+
+
+def put_rows(ce, cn, high, planes, tile, out_ref):
+    cz = out_ref.shape[3]
+    sub = lax.broadcasted_iota(jnp.int32, (SUB, cz), 0)
+    near, far = high * (SUB - 1), 1 + high * (SUB - 3)
+    place = pl.multiple_of(high * (cn - SUB), SUB)
+    for f in range(5):
+        for e in range(ce):
+            rows = jnp.where(
+                sub == near, planes[f][e : e + 1, :], jnp.where(sub == far, planes[5 + f][e : e + 1, :], 0.0)
+            )
+            out_ref[f, e] = tile(f, e, pl.ds(place, SUB)) + rows
+    return pl.ds(place, SUB)
+
+
+def both_kernel(
+    ce, cn, cz, blocks, copies_out,
+    own, other, pack, coef, got, held, grad, final_in,
+    final, chunks, fix, rest,
+    mine, tile_out, table, acc, sems,
+):
+    wide = 2 * ce
+    high = side(True)
+    sign = (2 * high - 1).astype(F32)
+    north = lax.axis_index("north")
+    exists = jnp.where(high > 0, north < lax.axis_size("north") - 1, north > 0).astype(F32)
+    east, level = plane_shifts(wide, cz)
+
+    def plane(ref, f):
+        return ref[f * wide : (f + 1) * wide, :]
+
+    v0 = [plane(pack, f) for f in range(5)]
+    u = [plane(pack, 5 + k) for k in range(3)]
+    w = 1.0 + plane(pack, 8)
+    xv = [plane(got, f) for f in range(5)]
+    xu = [plane(got, 5 + k) for k in range(3)]
+    xw = 1.0 + plane(got, 8)
+    curv = [plane(coef, k) for k in range(3)]
+    inv_v, inv_m = inverses(w)
+    delta = one_way(1, sign, w, u[1], xv, inv_v, inv_m, dot3(v0, xu))
+    back = one_way(1, -sign, xw, xu[1], v0, *inverses(xw), dot3(xv, u))
+    x1 = [(plane(got, 9 + f) + back[f]) * exists for f in range(5)]
+    total, slope0, slope2 = [], [], []
+    for f in range(5):
+        a, b = east(delta[f])
+        h, l = level(delta[f])
+        total.append((a + b) + (h + l))
+        slope0.append(a - b)
+        slope2.append(h - l)
+    full = [plane(pack, 9 + c) + delta[c] for c in range(3)]
+    add = one_way(1, sign, w, u[1], x1, inv_v, inv_m, dot3(full, xu) + dot3(delta, curv))
+    press = (slope0[3], None, slope2[3])
+    for c in range(3):
+        more = w * total[c] + 0.5 * (u[0] * slope0[c] + u[2] * slope2[c])
+        if press[c] is not None:
+            more = more - 0.5 * press[c]
+        add[c] = add[c] + more * inv_v
+    add[3] = add[3] + (total[3] - 0.5 * (slope0[0] + slope2[2])) * (1.0 / 7.0)
+    add[4] = add[4] + w * total[4] * inv_m
+    ru1, rw, ru0 = plane(coef, 3), 1.0 + plane(coef, 4), plane(coef, 5)
+    behind = one_way(1, sign, rw, ru1, delta, *inverses(rw))
+    west = lax.axis_index("east") == 0
+    for k, x in enumerate(add + behind):
+        mine[k] = jnp.where(west, x[:ce], x[ce:])
+        fix[k * ce : (k + 1) * ce, :] = jnp.where(west, x[ce:], x[:ce])
+    for row, u0, values in ((0, u[0], add), (1, ru0, behind)):
+        force = u0 * jnp.abs(u0)
+        for c in range(COMPS):
+            hi, lo = split(values[c if c < 3 else 4] * force)
+            table[row * wide : (row + 1) * wide, c * cz : (c + 1) * cz] = hi
+            table[(2 + row) * wide : (3 + row) * wide, c * cz : (c + 1) * cz] = lo
+    place = put_rows(ce, cn, high, mine, lambda f, e, at: held[f, e, at, :], tile_out)
+    copy = pltpu.make_async_copy(tile_out, final.at[:, :, place, :], sems.at[0])
+    copy.start()
+    away = pl.ds(pl.multiple_of((1 - high) * (cn - SUB), SUB), SUB)
+    for f in range(5):
+        for e in range(ce):
+            rest[f, e] = held[f, e, away, :]
+
+    acc[...] = grad[...]
+    base = RAW * ce
+    tail = own.shape[0] - base
+    most = (tail - ITEM) // ITEM * (cz // LANES)
+
+    def chunk(ref, q):
+        return ref[base + q // 2 * ITEM : base + (q // 2 + 1) * ITEM, q % 2 * LANES : (q % 2 + 1) * LANES]
+
+    def terms(lists):
+        turned = [x.T for x in lists]
+
+        def col(j):
+            return jnp.concatenate([x[:, j : j + 1] for x in turned], axis=0)
+
+        key = jnp.concatenate([x[2:3] for x in lists], axis=1)
+        rotor_terms(col(0), col(1), col(3), col(4) + col(5) + col(6), key, table, blocks, acc)
+
+    terms([chunk(own, 0), chunk(other, 0)])
+    for ref in (own, other):
+        live = jnp.max(ref[base + tail - ITEM :, :LANES])
+
+        @pl.when(live > float(LANES))
+        def _():
+            terms([chunk(ref, q) for q in range(1, min(2, most))])
+
+        @pl.when(live > 2.0 * LANES)
+        def _():
+            terms([chunk(ref, q) for q in range(2, most)])
+
+    for k in range(copies_out):
+        chunks[k] = acc[...]
+    copy.wait()
+
+
+def both_edges(own, other, pack, coef, got, held, grad, final, blocks, size):
+    _, ce, cn, cz = final.shape
+    args = (own, other, pack, coef, got, held, grad, final)
+    return pl.pallas_call(
+        functools.partial(both_kernel, ce, cn, cz, blocks, size),
+        out_shape=(shape(*final.shape), shape(size, blocks * SECT, LANES), shape(10 * ce, cz), shape(5, ce, SUB, cz)),
+        in_specs=[whole()] * (len(args) - 1) + [whole(pltpu.HBM)],
+        out_specs=(whole(pltpu.HBM), whole(), whole(), whole()),
+        scratch_shapes=[
+            VMEM((10, ce, cz), F32),
+            VMEM((5, ce, SUB, cz), F32),
+            VMEM((8 * ce, COMPS * cz), BF16),
+            VMEM((blocks * SECT, LANES), F32),
+            pltpu.SemaphoreType.DMA((1,)),
+        ],
+        input_output_aliases={len(args) - 1: 0},
+        compiler_params=params(32),
+        cost_estimate=cost(0, 1 << 10),
+    )(*args)
+
+
+def home_kernel(ce, cn, fix, rest, final_in, final, mine, tile_out, sems):
+    for k in range(10):
+        mine[k] = fix[k * ce : (k + 1) * ce, :]
+    place = put_rows(ce, cn, side(False), mine, lambda f, e, at: rest[f, e], tile_out)
+    copy = pltpu.make_async_copy(tile_out, final.at[:, :, place, :], sems.at[0])
+    copy.start()
+    copy.wait()
+
+
+def rows_home(fix, rest, final):
+    _, ce, cn, cz = final.shape
+    return pl.pallas_call(
+        functools.partial(home_kernel, ce, cn),
+        out_shape=shape(*final.shape),
+        in_specs=[whole()] * 2 + [whole(pltpu.HBM)],
+        out_specs=whole(pltpu.HBM),
+        scratch_shapes=[
+            VMEM((10, ce, cz), F32),
+            VMEM((5, ce, SUB, cz), F32),
+            pltpu.SemaphoreType.DMA((1,)),
+        ],
+        input_output_aliases={2: 0},
+        compiler_params=params(16),
+        cost_estimate=cost(0, 1 << 10),
+    )(fix, rest, final)
+
+
 def sum_kernel(parts, out):
     total = jnp.sum(parts[...], axis=0)
     for c in range(COMPS):
@@ -785,20 +1122,37 @@
     slots = rotor_cell.shape[-1]
     lists = [x.reshape(slots // LANES, LANES) for x in (rotor_cell, rotor_turbine, rotor_sector, rotor_weight)]
 
-    n_faces = 1 if n_east == 2 else 2
+    fields = adjoint_start, adjoint_source, base_flow, eddy_visc
+    if n_east == 2:
+        return pair_shards(count, fields, lists, n_north)
+    n_faces = 2
     ends = beside(row_ends(adjoint_start, base_flow, n_faces), n_east)
-    packs, own = pack(ends, adjoint_start, adjoint_source, base_flow, eddy_visc, n_faces)
+    packs, own = pack(ends, *fields, n_faces)
     gots = north_ways(packs, n_north)
     faces = beside(own, n_east)
-    final, low, high, coef_low, coef_high, grad, items, n_items = sweeps(
-        count, adjoint_start, adjoint_source, base_flow, eddy_visc, faces, lists, n_north
-    )
+    final, held, grad, coef_low, coef_high, items, n_items = sweeps(count, *fields, faces, lists, n_north, False)
     final, chunks = edges(
-        n_items, faces, packs, (coef_low, coef_high), gots, (low, high), items, grad, final,
-        n_north, n_east,
+        n_items, faces, packs, (coef_low, coef_high), gots, held, items, grad, final, n_north, n_east
     )
     chunks = chunks.reshape(n_east * n_north, SECT, LANES)
     parts = lax.all_to_all(chunks, ("east", "north"), 0, 0, tiled=True)
+    return (final, sum_parts(parts))
+
+
+def pair_shards(count, fields, lists, n_north):
+    ce = fields[0].shape[1]
+    swap = [(0, 1), (1, 0)]
+    (rows,) = raw_rows(False, count, *fields, lists)
+    other = lax.ppermute(rows, "east", swap)
+    own, face = raw_rows(True, count, *fields, lists)
+    pack_both, coef = join_rows(own, other, ce)
+    ways = [(n, n_north + n + 1) for n in range(n_north - 1)] + [(n_north + n, n - 1) for n in range(1, n_north)]
+    got = lax.ppermute(pack_both, ("east", "north"), ways)
+    faces = (lax.ppermute(face, "east", swap),) * 2
+    final, held, grad = sweeps(count, *fields, faces, lists, n_north, True)
+    final, chunks, fix, rest = both_edges(own, other, pack_both, coef, got, held, grad, final, n_north, 2)
+    parts = lax.all_to_all(chunks.reshape(2 * n_north, SECT, LANES), ("east", "north"), 0, 0, tiled=True)
+    final = rows_home(lax.ppermute(fix, "east", swap), rest, final)
     return (final, sum_parts(parts))
 
 

time: 46.7 us -> 41.8 us (0.90); the launches traced: 45.8 us -> 41.4 us
  blocking collectives: 15.1 us -> 0 us
  waiting for transfers between devices: 1.06 us -> 6.97 us
  starting transfers between devices: 7.41 us -> 11.7 us
    all_to_all x1 -> x0, blocking collectives: 15.1 us -> none  [shards(): parts = lax.all_to_all(chunks, ('east', 'north'), 0, 0, tiled=True)]
    all_to_all x0 -> x1, starting transfers between devices: none -> 6.28 us  [pair_shards(): lax.all_to_all(chunks.reshape(2 * n_north, SECT, LANES), ('east', 'north'...]
    all_to_all x0 -> x1, waiting for transfers between devices: none -> 5.46 us  [pair_shards(): lax.all_to_all(chunks.reshape(2 * n_north, SECT, LANES), ('east', 'north'...]
    ppermute x4, starting transfers between devices: 7.41 us -> 5.45 us  [the longest x1 4.5 us: pair_shards(): got = lax.ppermute(pack_both, ('east', 'north'), ways)]
    unnamed x18 -> x16, local copies, waits for them, and re-layouts: 0.65 us -> 1.04 us
    pallas_call x4 -> x6, Pallas kernels: 19.4 us -> 19.5 us  [the longest x1 10.4 us: sweeps(): pl.pallas_call(functools.partial(sweeps_kernel, ce, cn, cz, blocks, pair)...]
  transfers between devices with their start and end apart: 4 -> 5, of which waited for: 1 -> 3; matrix products, arithmetic and copies ran while one was open for 0% -> 0% of each run, Pallas kernels for 25% -> 36%
where the time goes in v4:
time: 41.8 us; the launch traced here: 41.4 us
  Pallas kernels  20.2 us (48%)
  starting transfers between devices  11.7 us (28%)
  waiting for transfers between devices  6.97 us (17%)
  between operations  1.42 us (3%)
  local copies, waits for them, and re-layouts  1.04 us (2%)
    pallas_call x1, Pallas kernels, sweeps(): pl.pallas_call(functools.partial(sweeps_kernel, ce, cn, cz, blocks, pair)...  10.4 us
    all_to_all x1, starting transfers between devices, pair_shards(): lax.all_to_all(chunks.reshape(2 * n_north, SECT, LANES), ('east', 'north'...  6.28 us
    pallas_call x2, Pallas kernels, raw_rows(): pl.pallas_call(functools.partial(raw_kernel, ce, cn, cz, own), out_shape=...  5.74 us
    all_to_all x1, waiting for transfers between devices, pair_shards(): lax.all_to_all(chunks.reshape(2 * n_north, SECT, LANES), ('east', 'north'...  5.46 us
    ppermute x1, starting transfers between devices, pair_shards(): got = lax.ppermute(pack_both, ('east', 'north'), ways)  4.5 us
    pallas_call x1, Pallas kernels, both_edges(): pl.pallas_call(functools.partial(both_kernel, ce, cn, cz, blocks, size),...  2.1 us
    ppermute x1, waiting for transfers between devices, pair_shards(): final = rows_home(lax.ppermute(fix, 'east', swap), rest, final)  1.14 us
    unnamed x16, local copies, waits for them, and re-layouts  1.04 us
  transfers between devices with their start and end apart: 5, of which 3 were waited for; matrix products, arithmetic and copies ran while one was open for 0% of the time, Pallas kernels for 36%

profile of v4, /device:TPU:0, one launch (start us, length us, event | category | flops | bytes accessed | tf_op | source)
XLA Modules:
  0.0 41.4 jit_solution(502886180059369773)
XLA Ops:
  1.3 2.7 %shard_map.105 = f32[408,256]{1,0:T(8,128)} custom-call(s32[1]{0:T(128)} %bitcast.7.refs_0_, f32[5,16,32,256]{3,2,1,0:T(8,128)} %start.1, f32[5,16,32,256]{3,2,1,0:T(8,128)} %source.1, f32[3,16,32,256]{3,2,1,0:T(8,128)} %flow.1, f32[16,32,256]{2,1,0:T(8,128)} %eddy.1, s32[8,128]{1,0:T(8,128)} %bitcast.9, s32[8,128]{1,0:T(8,128)} %bitcast.12, ...), custom_call_target="tpu_custom_call" | custom-call | bytes 1024 | tf_op jit(solution)/shard_map/pallas_call | solution.py:843
  4.0 0.5 %collective-permute-start = (f32[408,256]{1,0:T(8,128)}, f32[408,256]{1,0:T(8,128)S(1)}, u32[]{:S(2)}, u32[]{:S(2)}) collective-permute-start(f32[408,256]{1,0:T(8,128)} %shard_map.105), channel_id=1, source_target_pairs={{0,16},{16,0},{1,17},{17,1},{2,18},{18,2},{3,19},{19,3},{4,20},{20... | collective-permute-start | bytes 1253384 | tf_op jit(solution)/shard_map/ppermute | solution.py:1146
  4.5 0.0 copy-start.1
  4.5 0.0 copy-start.4
  4.5 0.0 copy-start.5
  4.5 0.0 copy-start.6
  4.5 0.0 copy-start.7
  4.5 3.1 %shard_map.104 = (f32[408,256]{1,0:T(8,128)}, f32[22,32,256]{2,1,0:T(8,128)}) custom-call(s32[1]{0:T(128)} %bitcast.6.refs_0_, f32[5,16,32,256]{3,2,1,0:T(8,128)} %start.1, f32[5,16,32,256]{3,2,1,0:T(8,128)} %source.1, f32[3,16,32,256]{3,2,1,0:T(8,128)} %flow.1, f32[16,32,256]{2,1,0:T(8,128)} %eddy.1, s32[8,128]{1,0:T(8,128)} %bitcast.10, ...), custom_call_target="tpu_custom_call" | custom-call | bytes 1024 | tf_op jit(solution)/shard_map/pallas_call | solution.py:843
  7.6 0.1 collective-permute-start.2
  7.7 0.0 collective-permute-done.other
  7.7 0.0 copy-start.2
  7.7 1.0 %copy-done.2 = f32[408,256]{1,0:T(8,128)S(1)} copy-done((f32[408,256]{1,0:T(8,128)S(1)}, f32[408,256]{1,0:T(8,128)}, u32[]{:S(2)}) %copy-start.2) | copy-done | bytes 417816
  8.7 0.3 shard_map.106
  9.0 4.5 %collective-permute-start.1 = (f32[448,256]{1,0:T(8,128)S(1)}, f32[448,256]{1,0:T(8,128)S(1)}, u32[]{:S(2)}, u32[]{:S(2)}) collective-permute-start(f32[448,256]{1,0:T(8,128)S(1)} %get-tuple-element.14.pack), channel_id=1, source_target_pairs={{0,17},{1,18},{2,19},{3,20},{4,21},{5,22},{6,23},{7,24},{8,25},{9,... | collective-permute-start | bytes 1376264 | tf_op jit(solution)/shard_map/ppermute | solution.py:1150
  13.5 0.0 collective-permute-done.2.facep.facen
  13.5 0.0 copy-done
  13.5 0.0 copy-done.1
  13.5 0.0 copy-done.4
  13.5 0.0 copy-done.5
  13.5 0.0 copy-done.6
  13.6 0.0 copy-done.7
  13.6 0.0 copy-start.3
  13.6 10.4 %shard_map.107 = (f32[5,16,32,256]{3,2,1,0:T(8,128)}, f32[5,16,32,256]{3,2,1,0:T(8,128)S(1)}, f32[128,128]{1,0:T(8,128)S(1)}) custom-call(s32[1]{0:T(128)} %bitcast.8.count, f32[5,16,32,256]{3,2,1,0:T(8,128)} %start.1, f32[5,16,32,256]{3,2,1,0:T(8,128)} %source.1, f32[3,16,32,256]{3,2,1,0:T(8,128)S(1)} %copy-done, f32[16,32,256]{2,1,0:T(8,128)S(1)} %copy-done.1, ...), custom_call_target="tpu_custom_call" | custom-call | bytes 1024 | tf_op jit(solution)/shard_map/pallas_call | solution.py:622
  24.0 0.4 collective-permute-done.1.got
  24.4 0.0 copy-done.3
  24.4 2.1 %shard_map.108 = (f32[5,16,32,256]{3,2,1,0:T(8,128)}, f32[2,128,128]{2,1,0:T(8,128)}, f32[160,256]{1,0:T(8,128)S(1)}, f32[5,16,8,256]{3,2,1,0:T(8,128)S(1)}) custom-call(f32[408,256]{1,0:T(8,128)S(1)} %copy-done.3, f32[408,256]{1,0:T(8,128)S(1)} %collective-permute-done.other, ...), custom_call_target="tpu_custom_call", output_to_operand_aliasing={{0}: (7, {})} | custom-call | bytes 1024 | tf_op jit(solution)/shard_map/pallas_call | solution.py:1031
  26.5 6.3 %all-to-all-start = ((f32[32,8,128]{2,1,0:T(8,128)}), f32[32,8,128]{2,1,0:T(8,128)S(1)}, u32[]{:S(2)}, u32[]{:S(2)}) async-start(f32[32,8,128]{2,1,0:T(8,128)} %bitcast.5), calls=%async_computation | async-start | bytes 262144 | tf_op jit(solution)/shard_map/all_to_all | solution.py:1154
  32.8 0.3 collective-permute-start.3
  33.1 1.1 %collective-permute-done.3.fix = f32[160,256]{1,0:T(8,128)S(1)} collective-permute-done((f32[160,256]{1,0:T(8,128)S(1)}, f32[160,256]{1,0:T(8,128)S(1)}, u32[]{:S(2)}, u32[]{:S(2)}) %collective-permute-start.3) | collective-permute-done | bytes 163872 | tf_op jit(solution)/shard_map/ppermute | solution.py:1155
  34.3 1.0 %shard_map.109 = f32[5,16,32,256]{3,2,1,0:T(8,128)} custom-call(f32[160,256]{1,0:T(8,128)S(1)} %collective-permute-done.3.fix, f32[5,16,8,256]{3,2,1,0:T(8,128)S(1)} %get-tuple-element.21.rest, f32[5,16,32,256]{3,2,1,0:T(8,128)} %get-tuple-element.22.final_in), custom_call_target="tpu_custom_call", output_to_operand_aliasing={{}: (2, {})} | custom-call | bytes 1024 | tf_op jit(solution)/shard_map/pallas_call | solution.py:1060
  35.2 5.5 %all-to-all-done.parts = f32[32,8,128]{2,1,0:T(8,128)S(1)} async-done(((f32[32,8,128]{2,1,0:T(8,128)}), f32[32,8,128]{2,1,0:T(8,128)S(1)}, u32[]{:S(2)}, u32[]{:S(2)}) %all-to-all-start) | async-done | bytes 131104 | tf_op jit(solution)/shard_map/all_to_all | solution.py:1154
  40.7 0.7 %shard_map.110 = f32[4,8,12]{2,1,0:T(8,128)} custom-call(f32[32,8,128]{2,1,0:T(8,128)S(1)} %all-to-all-done.parts), custom_call_target="tpu_custom_call" | custom-call | flops 32768 | bytes 131072 | tf_op jit(solution)/shard_map/pallas_call | solution.py:1083
  (1 shorter events, 0.0 us)
Async XLA Ops:
  4.0 3.7 %collective-permute-start = (f32[408,256]{1,0:T(8,128)}, f32[408,256]{1,0:T(8,128)S(1)}, u32[]{:S(2)}, u32[]{:S(2)}) collective-permute-start(f32[408,256]{1,0:T(8,128)} %shard_map.105), channel_id=1, source_target_pairs={{0,16},{16,0},{1,17},{17,1},{2,18},{18,2},{3,19},{19,3},{4,20},{20... | collective-permute-start | bytes 1253384 | tf_op jit(solution)/shard_map/ppermute | solution.py:1146
  4.5 9.0 %copy-start = (f32[3,16,32,256]{3,2,1,0:T(8,128)S(1)}, f32[3,16,32,256]{3,2,1,0:T(8,128)}, u32[]{:S(2)}) copy-start(f32[3,16,32,256]{3,2,1,0:T(8,128)} %flow.1) | copy-start | bytes 4718596
  4.5 9.0 %copy-start.1 = (f32[16,32,256]{2,1,0:T(8,128)S(1)}, f32[16,32,256]{2,1,0:T(8,128)}, u32[]{:S(2)}) copy-start(f32[16,32,256]{2,1,0:T(8,128)} %eddy.1) | copy-start | bytes 1572868
  4.5 9.0 %copy-start.4 = (s32[1,1,1024]{2,1,0:T(1,128)S(1)}, s32[1,1,1024]{2,1,0:T(1,128)}, u32[]{:S(2)}) copy-start(s32[1,1,1024]{2,1,0:T(1,128)} %param.14) | copy-start | bytes 12292
  4.5 9.0 %copy-start.5 = (s32[1,1,1024]{2,1,0:T(1,128)S(1)}, s32[1,1,1024]{2,1,0:T(1,128)}, u32[]{:S(2)}) copy-start(s32[1,1,1024]{2,1,0:T(1,128)} %param.15) | copy-start | bytes 12292
  4.5 9.0 %copy-start.6 = (s32[1,1,1024]{2,1,0:T(1,128)S(1)}, s32[1,1,1024]{2,1,0:T(1,128)}, u32[]{:S(2)}) copy-start(s32[1,1,1024]{2,1,0:T(1,128)} %param.16) | copy-start | bytes 12292
  4.5 9.0 %copy-start.7 = (f32[1,1,1024]{2,1,0:T(1,128)S(1)}, f32[1,1,1024]{2,1,0:T(1,128)}, u32[]{:S(2)}) copy-start(f32[1,1,1024]{2,1,0:T(1,128)} %param.17) | copy-start | bytes 12292
  7.6 5.9 %collective-permute-start.2 = (f32[22,32,256]{2,1,0:T(8,128)}, f32[22,32,256]{2,1,0:T(8,128)S(1)}, u32[]{:S(2)}, u32[]{:S(2)}) collective-permute-start(f32[22,32,256]{2,1,0:T(8,128)} %get-tuple-element.16), channel_id=1, source_target_pairs={{0,16},{16,0},{1,17},{17,1},{2,18},{18,2},{3,19},{19,3},{4,20},{20... | collective-permute-start | bytes 2162696 | tf_op jit(solution)/shard_map/ppermute | solution.py:1151
  7.7 1.0 %copy-start.2 = (f32[408,256]{1,0:T(8,128)S(1)}, f32[408,256]{1,0:T(8,128)}, u32[]{:S(2)}) copy-start(f32[408,256]{1,0:T(8,128)} %get-tuple-element.13.own) | copy-start | bytes 1253380
  9.0 15.4 %collective-permute-start.1 = (f32[448,256]{1,0:T(8,128)S(1)}, f32[448,256]{1,0:T(8,128)S(1)}, u32[]{:S(2)}, u32[]{:S(2)}) collective-permute-start(f32[448,256]{1,0:T(8,128)S(1)} %get-tuple-element.14.pack), channel_id=1, source_target_pairs={{0,17},{1,18},{2,19},{3,20},{4,21},{5,22},{6,23},{7,24},{8,25},{9,... | collective-permute-start | bytes 1376264 | tf_op jit(solution)/shard_map/ppermute | solution.py:1150
  13.6 10.8 %copy-start.3 = (f32[408,256]{1,0:T(8,128)S(1)}, f32[408,256]{1,0:T(8,128)}, u32[]{:S(2)}) copy-start(f32[408,256]{1,0:T(8,128)} %get-tuple-element.13.own) | copy-start | bytes 1253380
  26.5 14.2 %all-to-all-start = ((f32[32,8,128]{2,1,0:T(8,128)}), f32[32,8,128]{2,1,0:T(8,128)S(1)}, u32[]{:S(2)}, u32[]{:S(2)}) async-start(f32[32,8,128]{2,1,0:T(8,128)} %bitcast.5), calls=%async_computation | async-start | bytes 262144 | tf_op jit(solution)/shard_map/all_to_all | solution.py:1154
  32.8 1.5 %collective-permute-start.3 = (f32[160,256]{1,0:T(8,128)S(1)}, f32[160,256]{1,0:T(8,128)S(1)}, u32[]{:S(2)}, u32[]{:S(2)}) collective-permute-start(f32[160,256]{1,0:T(8,128)S(1)} %get-tuple-element.20), channel_id=1, source_target_pairs={{0,16},{16,0},{1,17},{17,1},{2,18},{18,2},{3,19},{19,3},{4,20},{20... | collective-permute-start | bytes 491528 | tf_op jit(solution)/shard_map/ppermute | solution.py:1155

commit v5 on v4

--- a/solution.py
+++ b/solution.py
@@ -19,6 +19,7 @@
 RAW = 23
 ITEM = 8
 STEP = 4
+OUT_STEP = 4
 ROWS_1 = 8
 ROWS_2 = 16
 VMEM = pltpu.VMEM
@@ -28,6 +29,10 @@
 
 def whole(space=VMEM):
     return pl.BlockSpec(memory_space=space)
+
+
+def in_hbm(*arrays):
+    return [pltpu.with_memory_space_constraint(x, pltpu.HBM) for x in arrays]
 
 
 def shape(*dims):
@@ -92,8 +97,14 @@
     return out
 
 
+def inverse(x):
+    y = pl.reciprocal(x, approx=True)
+    return y * (2.0 - x * y)
+
+
 def inverses(w):
-    return 1.0 / (6.0 * w + 1.0), 1.0 / (6.0 * w + 2.0)
+    six = 6.0 * w
+    return inverse(six + 1.0), inverse(six + 2.0)
 
 
 def dot3(a, b):
@@ -408,11 +419,11 @@
 def sweeps_kernel(
     ce, cn, cz, blocks, pair,
     count, start, source, flow, eddy, facep, facen, cells, turbine, sector, weight,
-    final, held, grad, *refs,
+    final, edge_low, edge_high, grad, *refs,
 ):
     if not pair:
         coef_low, coef_high, items, n_items = refs[:4]
-    v0, u, src, ed, v1, curv, table, sems = refs[-8:]
+    held, v0, u, src, ed, v1, curv, table, sems = refs[-9:]
     copies = Copies(sems)
     two = range(2)
     has = [x > 0 for x in neighbours()[:2]]
@@ -437,8 +448,8 @@
     ends = ((facep, 1, 0, 0), (facen, ce + 2, ce + 3, ce + 1))
     halos = [copies.take(*halo(*x)) for x in ends]
 
-    def group(g):
-        span, own, own2 = pl.ds(g, STEP), pl.ds(g + 1, STEP), pl.ds(g + 2, STEP)
+    def group(g, size):
+        span, own, own2 = pl.ds(g, size), pl.ds(g + 1, size), pl.ds(g + 2, size)
         pairs = []
         for h in two:
             pairs += [
@@ -449,7 +460,7 @@
             ]
         return pairs
 
-    groups = [copies.take(*group(g)) for g in range(0, ce, STEP)]
+    groups = [copies.take(*group(g, STEP)) for g in range(0, ce, STEP)]
     per = len(groups[0][1])
     copies.start(groups[0])
     for exists, taken in zip(has, halos):
@@ -471,20 +482,20 @@
                     ref[f, i, h, 0:PAD, :] = blank
                     ref[f, i, h, PAD + cn : PAD + cn + PAD, :] = blank
 
-    for exists, (_, near, _, _) in zip(has, ends):
+    for exists, (_, near, _, end) in zip(has, ends):
 
         @pl.when(jnp.logical_not(exists))
         def _():
-            for ref, fields in ((v0, 5), (u, 3)):
+            for ref, fields, slab in ((v0, 5, near), (u, 3, near), (v1, 5, end)):
                 for f in range(fields):
                     for h in two:
-                        ref[f, near, h, inner, :] = jnp.zeros((cn, LANES), F32)
+                        ref[f, slab, h, inner, :] = jnp.zeros((cn, LANES), F32)
 
     def ends_of(size):
         lane = lax.broadcasted_iota(jnp.int32, (size, LANES), 1)
         return lane == 0, lane == LANES - 1
 
-    live = count[0]
+    live = count[0, 0]
     slot, line, level, key, local, load = entries(live, cells, turbine, sector, weight, cz)
     chunks = slot.shape[0]
     if not pair:
@@ -505,22 +516,19 @@
     def _():
         copies.wait(halos[0])
 
-    @pl.loop(0, ce + 2)
-    def _(i):
-        @pl.when(jnp.logical_and(i < ce, lax.rem(i, STEP) == 0))
-        def _():
-            copies.wait((groups[0][0] + lax.div(i, STEP) * per, group(i)))
-
-        @pl.when(jnp.logical_and(i == ce, has[1]))
+    low_slab, high_slab = jnp.where(has[0], 0, 1), jnp.where(has[1], ce + 2, ce + 1)
+    steps = ce // STEP
+
+    @pl.loop(0, steps)
+    def _(g):
+        copies.wait((groups[0][0] + g * per, group(g * STEP, STEP)))
+
+        @pl.when(jnp.logical_and(g == steps - 1, has[1]))
         def _():
             copies.wait(halos[1])
 
-        real = jnp.logical_and(
-            jnp.logical_or(i > 0, has[0]), jnp.logical_or(i < ce + 1, has[1])
-        )
-
-        @pl.when(real)
-        def _():
+        @pl.loop(jnp.where(g == 0, low_slab, g * STEP), jnp.where(g == steps - 1, high_slab, (g + 1) * STEP))
+        def _(i):
             mid = i + 1
             first, last = ends_of(ROWS_1)
             for r in range(0, cn, ROWS_1):
@@ -544,46 +552,41 @@
                     for h in two:
                         v1[f, i, h, pl.ds(PAD + r, ROWS_1), :] = out[f][h]
 
-        @pl.when(jnp.logical_not(real))
-        def _():
-            for f in range(5):
+    def leave(e):
+        return [(held.at[:, pl.ds(e, OUT_STEP)], final.at[:, pl.ds(e, OUT_STEP)])]
+
+    outs = [copies.take(*leave(e)) for e in range(0, ce, OUT_STEP)]
+
+    @pl.loop(0, ce // OUT_STEP)
+    def _(g):
+        @pl.loop(0, OUT_STEP)
+        def _(k):
+            e = g * OUT_STEP + k
+            i = e + 1
+            first, last = ends_of(ROWS_2)
+
+            for r in range(0, cn, ROWS_2):
+                rows, span = (r, ROWS_2), pl.ds(r, ROWS_2)
+                flows = [halves(u, k, i + 1, rows) for k in range(3)]
+                bends = [[curv[k, i, h, span, :] for h in two] for k in range(3)]
+                out = slab_sweep(
+                    v1, i, rows, first, last,
+                    lambda f: [src[f, i, h, span, :] for h in two],
+                    flows, [1.0 + ed[0, i, h, span, :] for h in two], bends,
+                )
+                at = pl.ds(pl.multiple_of(e * cn + r, ROWS_2), ROWS_2)
+                below = pl.ds(pl.multiple_of((ce + e) * cn + r, ROWS_2), ROWS_2)
                 for h in two:
-                    v1[f, i, h, inner, :] = jnp.zeros((cn, LANES), F32)
-
-    def leave(e):
-        return [(held.at[:, pl.ds(e, STEP)], final.at[:, pl.ds(e, STEP)])]
-
-    outs = [copies.take(*leave(e)) for e in range(0, ce, STEP)]
-
-    @pl.loop(0, ce)
-    def _(e):
-        i = e + 1
-        first, last = ends_of(ROWS_2)
-
-        for r in range(0, cn, ROWS_2):
-            rows, span = (r, ROWS_2), pl.ds(r, ROWS_2)
-            flows = [halves(u, k, i + 1, rows) for k in range(3)]
-            bends = [[curv[k, i, h, span, :] for h in two] for k in range(3)]
-            out = slab_sweep(
-                v1, i, rows, first, last,
-                lambda f: [src[f, i, h, span, :] for h in two],
-                flows, [1.0 + ed[0, i, h, span, :] for h in two], bends,
-            )
-            at = pl.ds(pl.multiple_of(e * cn + r, ROWS_2), ROWS_2)
-            below = pl.ds(pl.multiple_of((ce + e) * cn + r, ROWS_2), ROWS_2)
-            for h in two:
-                force = flows[0][h] * jnp.abs(flows[0][h])
-                for f in range(5):
-                    held[f, e, span, part(h)] = out[f][h]
-                for c in range(COMPS):
-                    hi, lo = split(out[c if c < 3 else 4][h] * force)
-                    wide = pl.ds(c * cz + h * LANES, LANES)
-                    table[at, wide] = hi
-                    table[below, wide] = lo
-        @pl.when(lax.rem(e, STEP) == STEP - 1)
-        def _():
-            copies.start((outs[0][0] + lax.div(e, STEP), leave(e - (STEP - 1))))
-
+                    force = flows[0][h] * jnp.abs(flows[0][h])
+                    for f in range(5):
+                        held[f, e, span, part(h)] = out[f][h]
+                    for c in range(COMPS):
+                        hi, lo = split(out[c if c < 3 else 4][h] * force)
+                        wide = pl.ds(c * cz + h * LANES, LANES)
+                        table[at, wide] = hi
+                        table[below, wide] = lo
+
+        copies.start((outs[0][0] + g, leave(g * OUT_STEP)))
 
     def edge_plane(ref, k, first, tall, row):
         fields, slabs = ref.shape[:2]
@@ -601,6 +604,9 @@
         for k, x in enumerate(planes):
             coef[k * ce : (k + 1) * ce, :] = x
 
+    tiles = copies.take((held.at[:, :, 0:SUB, :], edge_low), (held.at[:, :, cn - SUB : cn, :], edge_high))
+    copies.start(tiles)
+
     row_t, level_t, local_t, load_t = line.astype(F32).T, level.T, local.T, load.T
     grad[...] = jnp.zeros_like(grad)
     for least, size in steps_of(chunks):
@@ -610,7 +616,7 @@
             cols = [columns(x, 0, size) for x in (row_t, level_t, local_t, load_t)]
             rotor_terms(*cols, lines(key, 0, size), table, blocks, grad)
 
-    for taken in outs:
+    for taken in outs + [tiles]:
         copies.wait(taken)
 
 
@@ -621,10 +627,11 @@
     more = [shape(EDGE * ce, cz)] * 2 + [shape(chunks, ITEM, LANES), jax.ShapeDtypeStruct((1,), jnp.int32)]
     return pl.pallas_call(
         functools.partial(sweeps_kernel, ce, cn, cz, blocks, pair),
-        out_shape=[shape(*start.shape)] * 2 + [shape(blocks * SECT, LANES)] + ([] if pair else more),
+        out_shape=[shape(*start.shape)] + [shape(5, ce, SUB, cz)] * 2 + [shape(blocks * SECT, LANES)] + ([] if pair else more),
         in_specs=[whole(pltpu.SMEM)] + [whole(pltpu.HBM)] * 6 + [whole()] * 4,
-        out_specs=[whole(pltpu.HBM), whole(), whole()] + ([] if pair else [whole()] * 3 + [whole(pltpu.SMEM)]),
+        out_specs=[whole(pltpu.HBM), whole(), whole(), whole()] + ([] if pair else [whole()] * 3 + [whole(pltpu.SMEM)]),
         scratch_shapes=[
+            VMEM(start.shape, F32),
             VMEM((5, ce + 4, 2, tall, LANES), F32),
             VMEM((3, ce + 4, 2, tall, LANES), F32),
             VMEM((5, ce + 2, 2, cn, LANES), F32),
@@ -632,17 +639,17 @@
             VMEM((5, ce + 2, 2, tall, LANES), F32),
             VMEM((3, ce + 2, 2, cn, LANES), F32),
             VMEM((2 * ce * cn, COMPS * cz), BF16),
-            pltpu.SemaphoreType.DMA((24 + 9 * (ce // STEP),)),
+            pltpu.SemaphoreType.DMA((26 + 8 * (ce // STEP) + ce // OUT_STEP,)),
         ],
         compiler_params=params(48),
         cost_estimate=cost(0, 1 << 10),
-    )(count, start, source, flow, eddy, *faces, *lists)
+    )(count, *in_hbm(start, source, flow, eddy), *faces, *lists)
 
 
 def edge_kernel(
     ce, cn, cz, blocks, copies_out,
     n_items, facep, facen, own_low, own_high, coef_low, coef_high, got_prev, got_next,
-    held, items, grad, final_in,
+    edge_low, edge_high, items, grad, final_in,
     final, chunks,
     low_out, high_out, table, acc, sems,
 ):
@@ -650,11 +657,11 @@
     sub = lax.broadcasted_iota(jnp.int32, (SUB, cz), 0)
     has = [x.astype(F32) for x in neighbours()]
     sides = (
-        (-1.0, 0, own_low, coef_low, got_prev, low_out, 0),
-        (1.0, cn - 1, own_high, coef_high, got_next, high_out, cn - SUB),
+        (-1.0, 0, own_low, coef_low, got_prev, edge_low, low_out, 0),
+        (1.0, cn - 1, own_high, coef_high, got_next, edge_high, high_out, cn - SUB),
     )
     waits = []
-    for side, (sign, row, own, coef, got, out_ref, place) in enumerate(sides):
+    for side, (sign, row, own, coef, got, edge, out_ref, place) in enumerate(sides):
 
         def plane(ref, f):
             return ref[f * ce : (f + 1) * ce, :]
@@ -704,7 +711,7 @@
                 rows = jnp.where(
                     sub == near, add[f][e : e + 1, :], jnp.where(sub == far, behind[f][e : e + 1, :], 0.0)
                 )
-                out_ref[f, e] = held[f, e, place : place + SUB, :] + rows
+                out_ref[f, e] = edge[f, e] + rows
         copy = pltpu.make_async_copy(out_ref, final.at[:, :, pl.ds(place, SUB), :], sems.at[side])
         copy.start()
         waits.append(copy)
@@ -737,9 +744,9 @@
         copy.wait()
 
 
-def edges(n_items, faces, packs, coefs, gots, held, items, grad, final, blocks, size):
+def edges(n_items, faces, packs, coefs, gots, tiles, items, grad, final, blocks, size):
     _, ce, cn, cz = final.shape
-    args = (n_items, *faces, *packs, *coefs, *gots, held, items, grad, final)
+    args = (n_items, *faces, *packs, *coefs, *gots, *tiles, items, grad, final)
     tile = VMEM((5, ce, SUB, cz), F32)
     return pl.pallas_call(
         functools.partial(edge_kernel, ce, cn, cz, blocks, size),
@@ -765,15 +772,22 @@
 
 
 def raw_kernel(ce, cn, cz, own, *refs):
-    count, start, source, flow, eddy, *lists = refs[:9]
-    rows, refs = refs[9], refs[10:]
-    faces, refs = (refs[:1], refs[1:]) if own else ((), refs)
-    tiles_v, tiles_u, tiles_s, tiles_e, cells, turbine, sector, weight, sems = refs
+    if own:
+        count, refs = refs[0], refs[1:]
+    start, source, flow, eddy, refs = *refs[:4], refs[4:]
+    if own:
+        lists, (rows, face, *items), refs = refs[:4], refs[4:8], refs[8:]
+        cells, turbine, sector, weight, sems = refs[4:]
+    else:
+        rows, sems = refs[0], refs[-1]
+        refs = refs[1:]
+    tiles_v, tiles_u, tiles_s, tiles_e = refs[:4]
     copies = Copies(sems)
     high = side(own)
     first = pl.multiple_of(high * (cn - SUB), SUB)
-    held = copies.take(*zip(lists, (cells, turbine, sector, weight)))
-    copies.start(held)
+    if own:
+        held = copies.take(*zip(lists, (cells, turbine, sector, weight)))
+        copies.start(held)
     pairs = []
     for h in range(2):
         cut = (pl.ds(first, SUB), pl.ds(h * LANES, LANES))
@@ -785,38 +799,22 @@
         ]
     needed = copies.take(*pairs)
     copies.start(needed)
-    later = []
-    for (near, far), face in zip(facing(ce), faces):
-        later.append(
-            copies.take(
-                (start.at[:, near], face.at[0:5]),
-                (flow.at[:, near], face.at[5:8]),
-                (eddy.at[near], face.at[8]),
-                (source.at[:, near], face.at[9:14]),
-                (start.at[:, far], face.at[14:19]),
-                (flow.at[:, far], face.at[19:22]),
-            )
+    if own:
+        ((near, far),) = facing(ce)
+        later = copies.take(
+            (start.at[:, near], face.at[0:5]),
+            (flow.at[:, near], face.at[5:8]),
+            (eddy.at[near], face.at[8]),
+            (source.at[:, near], face.at[9:14]),
+            (start.at[:, far], face.at[14:19]),
+            (flow.at[:, far], face.at[19:22]),
         )
-        copies.start(later[-1])
-
-    copies.wait(held)
-    live = count[0]
-    slot, line, level, key, local, load = entries(live, cells, turbine, sector, weight, cz)
-    north = jnp.bitwise_and(line, cn - 1)
-    column = lax.shift_right_logical(line, cn.bit_length() - 1) + lax.axis_index("east") * ce
-    edge = high * (cn - 1)
-    behind = edge + 1 - 2 * high
-    chosen = jnp.where(jnp.logical_and(jnp.logical_or(north == edge, north == behind), slot < live), 1.0, 0.0)
-    edge_row = (jnp.where(north == behind, 2 * ce, 0) + column).astype(F32)
-    base = RAW * ce
-    tail = rows.shape[0] - base
-    rows[base:, :] = jnp.zeros((tail, cz), F32)
-
-    def put(q, x):
-        rows[base + q // 2 * ITEM : base + (q // 2 + 1) * ITEM, q % 2 * LANES : (q % 2 + 1) * LANES] = x
-
-    total = gather_edge(chosen, edge_row, level, key, local, load, put)
-    rows[base + tail - ITEM :, :] = jnp.full((ITEM, cz), total.astype(F32))
+        copies.start(later)
+        copies.wait(held)
+        live = count[0, 0]
+        listed = entries(live, cells, turbine, sector, weight, cz)
+        for ref, which in zip(items, (high, 1 - high)):
+            edge_items(ce, cn, cz, live, listed, which, ref)
 
     def plane(ref, f, low, top):
         flat = ref.reshape(ref.shape[0], ce * 2 * SUB, LANES)
@@ -832,33 +830,49 @@
     planes += [(tiles_v, f, 1) for f in range(5)] + [(tiles_u, k, 1) for k in range(3)] + [(tiles_e, 0, 1)]
     for k, (ref, f, at) in enumerate(planes):
         rows[k * ce : (k + 1) * ce, :] = plane(ref, f, at, SUB - 1 - at)
-    for taken in later:
-        copies.wait(taken)
-
-
-def raw_rows(own, count, start, source, flow, eddy, lists):
+    if own:
+        copies.wait(later)
+
+
+def edge_items(ce, cn, cz, live, listed, high, out):
+    slot, line, level, key, local, load = listed
+    north = jnp.bitwise_and(line, cn - 1)
+    column = lax.shift_right_logical(line, cn.bit_length() - 1) + lax.axis_index("east") * ce
+    edge = high * (cn - 1)
+    behind = edge + 1 - 2 * high
+    chosen = jnp.where(jnp.logical_and(jnp.logical_or(north == edge, north == behind), slot < live), 1.0, 0.0)
+    edge_row = (jnp.where(north == behind, 2 * ce, 0) + column).astype(F32)
+    out[...] = jnp.zeros_like(out)
+
+    def put(q, x):
+        out[q // 2 * ITEM : (q // 2 + 1) * ITEM, q % 2 * LANES : (q % 2 + 1) * LANES] = x
+
+    total = gather_edge(chosen, edge_row, level, key, local, load, put)
+    out[out.shape[0] - ITEM :, :] = jnp.full((ITEM, cz), total.astype(F32))
+
+
+def raw_rows(own, start, source, flow, eddy, count=None, lists=()):
     _, ce, cn, cz = start.shape
-    chunks = lists[0].shape[0]
-    out = [shape(RAW * ce + (chunks * LANES // cz + 1) * ITEM, cz)] + ([shape(FACE, cn, cz)] if own else [])
+    out = [shape(RAW * ce, cz)]
+    scratch = [
+        VMEM((5, ce, 2, SUB, LANES), F32),
+        VMEM((3, ce, 2, SUB, LANES), F32),
+        VMEM((5, ce, 2, SUB, LANES), F32),
+        VMEM((1, ce, 2, SUB, LANES), F32),
+    ]
+    if own:
+        chunks = lists[0].shape[0]
+        out += [shape(FACE, cn, cz)] + [shape((chunks * LANES // cz + 1) * ITEM, cz)] * 2
+        scratch += [VMEM((chunks, LANES), x.dtype) for x in lists]
     return pl.pallas_call(
         functools.partial(raw_kernel, ce, cn, cz, own),
         out_shape=out,
-        in_specs=[whole(pltpu.SMEM)] + [whole(pltpu.HBM)] * 8,
+        in_specs=([whole(pltpu.SMEM)] if own else []) + [whole(pltpu.HBM)] * (4 + len(lists)),
         out_specs=[whole()] * len(out),
-        scratch_shapes=[
-            VMEM((5, ce, 2, SUB, LANES), F32),
-            VMEM((3, ce, 2, SUB, LANES), F32),
-            VMEM((5, ce, 2, SUB, LANES), F32),
-            VMEM((1, ce, 2, SUB, LANES), F32),
-            VMEM((chunks, LANES), jnp.int32),
-            VMEM((chunks, LANES), jnp.int32),
-            VMEM((chunks, LANES), jnp.int32),
-            VMEM((chunks, LANES), F32),
-            pltpu.SemaphoreType.DMA((18,)),
-        ],
-        compiler_params=params(59),
+        scratch_shapes=scratch + [pltpu.SemaphoreType.DMA((18,))],
+        compiler_params=params(16),
         cost_estimate=cost(0, 1 << 10),
-    )(count, start, source, flow, eddy, *lists)
+    )(*([count] if own else []), *in_hbm(start, source, flow, eddy, *lists))
 
 
 def joined(ce, own, other, k):
@@ -913,25 +927,11 @@
     )(own, other)
 
 
-def put_rows(ce, cn, high, planes, tile, out_ref):
-    cz = out_ref.shape[3]
-    sub = lax.broadcasted_iota(jnp.int32, (SUB, cz), 0)
-    near, far = high * (SUB - 1), 1 + high * (SUB - 3)
-    place = pl.multiple_of(high * (cn - SUB), SUB)
-    for f in range(5):
-        for e in range(ce):
-            rows = jnp.where(
-                sub == near, planes[f][e : e + 1, :], jnp.where(sub == far, planes[5 + f][e : e + 1, :], 0.0)
-            )
-            out_ref[f, e] = tile(f, e, pl.ds(place, SUB)) + rows
-    return pl.ds(place, SUB)
-
-
 def both_kernel(
     ce, cn, cz, blocks, copies_out,
-    own, other, pack, coef, got, held, grad, final_in,
-    final, chunks, fix, rest,
-    mine, tile_out, table, acc, sems,
+    own, other, pack, coef, got, grad,
+    chunks, mine, fix,
+    table, acc,
 ):
     wide = 2 * ce
     high = side(True)
@@ -975,7 +975,7 @@
     behind = one_way(1, sign, rw, ru1, delta, *inverses(rw))
     west = lax.axis_index("east") == 0
     for k, x in enumerate(add + behind):
-        mine[k] = jnp.where(west, x[:ce], x[ce:])
+        mine[k * ce : (k + 1) * ce, :] = jnp.where(west, x[:ce], x[ce:])
         fix[k * ce : (k + 1) * ce, :] = jnp.where(west, x[ce:], x[:ce])
     for row, u0, values in ((0, u[0], add), (1, ru0, behind)):
         force = u0 * jnp.abs(u0)
@@ -983,21 +983,12 @@
             hi, lo = split(values[c if c < 3 else 4] * force)
             table[row * wide : (row + 1) * wide, c * cz : (c + 1) * cz] = hi
             table[(2 + row) * wide : (3 + row) * wide, c * cz : (c + 1) * cz] = lo
-    place = put_rows(ce, cn, high, mine, lambda f, e, at: held[f, e, at, :], tile_out)
-    copy = pltpu.make_async_copy(tile_out, final.at[:, :, place, :], sems.at[0])
-    copy.start()
-    away = pl.ds(pl.multiple_of((1 - high) * (cn - SUB), SUB), SUB)
-    for f in range(5):
-        for e in range(ce):
-            rest[f, e] = held[f, e, away, :]
 
     acc[...] = grad[...]
-    base = RAW * ce
-    tail = own.shape[0] - base
-    most = (tail - ITEM) // ITEM * (cz // LANES)
+    most = (own.shape[0] // ITEM - 1) * (cz // LANES)
 
     def chunk(ref, q):
-        return ref[base + q // 2 * ITEM : base + (q // 2 + 1) * ITEM, q % 2 * LANES : (q % 2 + 1) * LANES]
+        return ref[q // 2 * ITEM : (q // 2 + 1) * ITEM, q % 2 * LANES : (q % 2 + 1) * LANES]
 
     def terms(lists):
         turned = [x.T for x in lists]
@@ -1010,7 +1001,7 @@
 
     terms([chunk(own, 0), chunk(other, 0)])
     for ref in (own, other):
-        live = jnp.max(ref[base + tail - ITEM :, :LANES])
+        live = jnp.max(ref[ref.shape[0] - ITEM :, :LANES])
 
         @pl.when(live > float(LANES))
         def _():
@@ -1022,55 +1013,66 @@
 
     for k in range(copies_out):
         chunks[k] = acc[...]
-    copy.wait()
-
-
-def both_edges(own, other, pack, coef, got, held, grad, final, blocks, size):
-    _, ce, cn, cz = final.shape
-    args = (own, other, pack, coef, got, held, grad, final)
+
+
+def both_edges(own, other, pack, coef, got, grad, size, blocks, copies_out):
+    _, ce, cn, cz = size
     return pl.pallas_call(
-        functools.partial(both_kernel, ce, cn, cz, blocks, size),
-        out_shape=(shape(*final.shape), shape(size, blocks * SECT, LANES), shape(10 * ce, cz), shape(5, ce, SUB, cz)),
-        in_specs=[whole()] * (len(args) - 1) + [whole(pltpu.HBM)],
-        out_specs=(whole(pltpu.HBM), whole(), whole(), whole()),
+        functools.partial(both_kernel, ce, cn, cz, blocks, copies_out),
+        out_shape=(shape(copies_out, blocks * SECT, LANES), shape(10 * ce, cz), shape(10 * ce, cz)),
+        in_specs=[whole()] * 6,
+        out_specs=(whole(), whole(), whole()),
         scratch_shapes=[
-            VMEM((10, ce, cz), F32),
-            VMEM((5, ce, SUB, cz), F32),
             VMEM((8 * ce, COMPS * cz), BF16),
             VMEM((blocks * SECT, LANES), F32),
-            pltpu.SemaphoreType.DMA((1,)),
         ],
-        input_output_aliases={len(args) - 1: 0},
         compiler_params=params(32),
         cost_estimate=cost(0, 1 << 10),
-    )(*args)
-
-
-def home_kernel(ce, cn, fix, rest, final_in, final, mine, tile_out, sems):
-    for k in range(10):
-        mine[k] = fix[k * ce : (k + 1) * ce, :]
-    place = put_rows(ce, cn, side(False), mine, lambda f, e, at: rest[f, e], tile_out)
-    copy = pltpu.make_async_copy(tile_out, final.at[:, :, place, :], sems.at[0])
-    copy.start()
-    copy.wait()
-
-
-def rows_home(fix, rest, final):
+    )(own, other, pack, coef, got, grad)
+
+
+def home_kernel(ce, cn, mine, fix, edge_low, edge_high, final_in, final, low_out, high_out, sems):
+    cz = edge_low.shape[3]
+    sub = lax.broadcasted_iota(jnp.int32, (SUB, cz), 0)
+    high = side(True) > 0
+    waits = []
+    for k, (edge, out, near, far, place) in enumerate(
+        ((edge_low, low_out, 0, 1, 0), (edge_high, high_out, SUB - 1, SUB - 2, cn - SUB))
+    ):
+        from_mine = high if k else jnp.logical_not(high)
+        for f in range(5):
+
+            def plane(at):
+                span = pl.ds(at * ce, ce)
+                return jnp.where(from_mine, mine[span, :], fix[span, :])
+
+            a, b = plane(f), plane(5 + f)
+            for e in range(ce):
+                rows = jnp.where(sub == near, a[e : e + 1, :], jnp.where(sub == far, b[e : e + 1, :], 0.0))
+                out[f, e] = edge[f, e] + rows
+        copy = pltpu.make_async_copy(out, final.at[:, :, pl.ds(place, SUB), :], sems.at[k])
+        copy.start()
+        waits.append(copy)
+    for copy in waits:
+        copy.wait()
+
+
+def rows_home(mine, fix, tiles, final):
     _, ce, cn, cz = final.shape
     return pl.pallas_call(
         functools.partial(home_kernel, ce, cn),
         out_shape=shape(*final.shape),
-        in_specs=[whole()] * 2 + [whole(pltpu.HBM)],
+        in_specs=[whole()] * 4 + [whole(pltpu.HBM)],
         out_specs=whole(pltpu.HBM),
         scratch_shapes=[
-            VMEM((10, ce, cz), F32),
             VMEM((5, ce, SUB, cz), F32),
-            pltpu.SemaphoreType.DMA((1,)),
+            VMEM((5, ce, SUB, cz), F32),
+            pltpu.SemaphoreType.DMA((2,)),
         ],
-        input_output_aliases={2: 0},
+        input_output_aliases={4: 0},
         compiler_params=params(16),
         cost_estimate=cost(0, 1 << 10),
-    )(fix, rest, final)
+    )(mine, fix, *tiles, final)
 
 
 def sum_kernel(parts, out):
@@ -1118,7 +1120,7 @@
 ):
     _, ce, cn, cz = adjoint_start.shape
     n_east, n_north = lax.axis_size("east"), lax.axis_size("north")
-    count = rotor_count.reshape(1)
+    count = rotor_count
     slots = rotor_cell.shape[-1]
     lists = [x.reshape(slots // LANES, LANES) for x in (rotor_cell, rotor_turbine, rotor_sector, rotor_weight)]
 
@@ -1130,9 +1132,9 @@
     packs, own = pack(ends, *fields, n_faces)
     gots = north_ways(packs, n_north)
     faces = beside(own, n_east)
-    final, held, grad, coef_low, coef_high, items, n_items = sweeps(count, *fields, faces, lists, n_north, False)
+    final, *tiles, grad, coef_low, coef_high, items, n_items = sweeps(count, *fields, faces, lists, n_north, False)
     final, chunks = edges(
-        n_items, faces, packs, (coef_low, coef_high), gots, held, items, grad, final, n_north, n_east
+        n_items, faces, packs, (coef_low, coef_high), gots, tiles, items, grad, final, n_north, n_east
     )
     chunks = chunks.reshape(n_east * n_north, SECT, LANES)
     parts = lax.all_to_all(chunks, ("east", "north"), 0, 0, tiled=True)
@@ -1142,17 +1144,18 @@
 def pair_shards(count, fields, lists, n_north):
     ce = fields[0].shape[1]
     swap = [(0, 1), (1, 0)]
-    (rows,) = raw_rows(False, count, *fields, lists)
+    (rows,) = raw_rows(False, *fields)
     other = lax.ppermute(rows, "east", swap)
-    own, face = raw_rows(True, count, *fields, lists)
+    own, face, items, items_out = raw_rows(True, *fields, count, lists)
     pack_both, coef = join_rows(own, other, ce)
     ways = [(n, n_north + n + 1) for n in range(n_north - 1)] + [(n_north + n, n - 1) for n in range(1, n_north)]
     got = lax.ppermute(pack_both, ("east", "north"), ways)
     faces = (lax.ppermute(face, "east", swap),) * 2
-    final, held, grad = sweeps(count, *fields, faces, lists, n_north, True)
-    final, chunks, fix, rest = both_edges(own, other, pack_both, coef, got, held, grad, final, n_north, 2)
+    items_in = lax.ppermute(items_out, "east", swap)
+    final, *tiles, grad = sweeps(count, *fields, faces, lists, n_north, True)
+    chunks, mine, fix = both_edges(items, items_in, pack_both, coef, got, grad, fields[0].shape, n_north, 2)
     parts = lax.all_to_all(chunks.reshape(2 * n_north, SECT, LANES), ("east", "north"), 0, 0, tiled=True)
-    final = rows_home(lax.ppermute(fix, "east", swap), rest, final)
+    final = rows_home(mine, lax.ppermute(fix, "east", swap), tiles, final)
     return (final, sum_parts(parts))
 
 

time: 41.8 us -> 39 us (0.933)
  Pallas kernels: 20.2 us -> 18.3 us
  local copies, waits for them, and re-layouts: 1.04 us -> 0.03 us
    pallas_call x2, Pallas kernels: 5.74 us -> 3.84 us  [raw_rows(): pl.pallas_call(functools.partial(raw_kernel, ce, cn, cz, own), out_shape=...]
    unnamed x16 -> x8, local copies, waits for them, and re-layouts: 1.04 us -> 0.03 us
    ppermute x1 -> x2, waiting for transfers between devices: 1.14 us -> 1.15 us  [the longest x1 1.14 us: pair_shards(): final = rows_home(mine, lax.ppermute(fix, 'east', swap), tiles, final)]
  transfers between devices with their start and end apart: 5 -> 6, of which waited for: 3 -> 3; matrix products, arithmetic and copies ran while one was open for 0% -> 0% of each run, Pallas kernels for 36% -> 36%
where the time goes in v5:
time: 39 us; the launch traced here: 38.6 us
  Pallas kernels  18.3 us (47%)
  starting transfers between devices  12 us (31%)
  waiting for transfers between devices  6.79 us (17%)
  between operations  1.43 us (4%)
    pallas_call x1, Pallas kernels, sweeps(): pl.pallas_call(functools.partial(sweeps_kernel, ce, cn, cz, blocks, pair)...  10.4 us
    all_to_all x1, starting transfers between devices, pair_shards(): lax.all_to_all(chunks.reshape(2 * n_north, SECT, LANES), ('east', 'north'...  6.5 us
    all_to_all x1, waiting for transfers between devices, pair_shards(): lax.all_to_all(chunks.reshape(2 * n_north, SECT, LANES), ('east', 'north'...  5.25 us
    ppermute x1, starting transfers between devices, pair_shards(): got = lax.ppermute(pack_both, ('east', 'north'), ways)  4.48 us
    pallas_call x2, Pallas kernels, raw_rows(): pl.pallas_call(functools.partial(raw_kernel, ce, cn, cz, own), out_shape=...  3.84 us
    pallas_call x1, Pallas kernels, both_edges(): pl.pallas_call(functools.partial(both_kernel, ce, cn, cz, blocks, copies_...  1.96 us
    pallas_call x1, Pallas kernels, rows_home(): pl.pallas_call(functools.partial(home_kernel, ce, cn), out_shape=shape(*f...  1.19 us
    ppermute x1, waiting for transfers between devices, pair_shards(): final = rows_home(mine, lax.ppermute(fix, 'east', swap), tiles, final)  1.14 us
  transfers between devices with their start and end apart: 6, of which 3 were waited for; matrix products, arithmetic and copies ran while one was open for 0% of the time, Pallas kernels for 36%

profile of v5, /device:TPU:0, one launch (start us, length us, event | category | flops | bytes accessed | tf_op | source)
XLA Modules:
  0.0 38.6 jit_solution(2599068164286805966)
XLA Ops:
  0.6 1.9 %shard_map.105 = f32[368,256]{1,0:T(8,128)S(1)} custom-call(f32[5,16,32,256]{3,2,1,0:T(8,128)} %start.1, f32[5,16,32,256]{3,2,1,0:T(8,128)} %source.1, f32[3,16,32,256]{3,2,1,0:T(8,128)} %flow.1, f32[16,32,256]{2,1,0:T(8,128)} %eddy.1), custom_call_target="tpu_custom_call" | custom-call | bytes 1024 | tf_op jit(solution)/shard_map/pallas_call | solution.py:867
  2.5 0.5 %collective-permute-start.1 = (f32[368,256]{1,0:T(8,128)S(1)}, f32[368,256]{1,0:T(8,128)S(1)}, u32[]{:S(2)}, u32[]{:S(2)}) collective-permute-start(f32[368,256]{1,0:T(8,128)S(1)} %shard_map.105), channel_id=1, source_target_pairs={{0,16},{16,0},{1,17},{17,1},{2,18},{18,2},{3,19},{19,3},{4,20},{20... | collective-permute-start | bytes 1130504 | tf_op jit(solution)/shard_map/ppermute | solution.py:1148
  3.7 0.0 copy-start
  3.7 0.0 copy-start.1
  3.7 0.0 copy-start.2
  3.7 0.0 copy-start.3
  3.7 2.0 %shard_map.104 = (f32[368,256]{1,0:T(8,128)S(1)}, f32[22,32,256]{2,1,0:T(8,128)S(1)}, f32[40,256]{1,0:T(8,128)S(1)}, f32[40,256]{1,0:T(8,128)S(1)}) custom-call(s32[1,1]{1,0:T(1,128)S(6)} %copy.13.refs_0_.count, f32[5,16,32,256]{3,2,1,0:T(8,128)} %start.1, f32[5,16,32,256]{3,2,1,0:T(8,128)} %source.1, f32[3,16,32,256]{3,2,1,0:T(8,128)} %flow.1, ...), custom_call_target="tpu_custom_call" | custom-call | bytes 1024 | tf_op jit(solution)/shard_map/pallas_call | solution.py:867
  5.7 0.1 collective-permute-start.3
  5.8 0.0 collective-permute-done.1.other
  5.8 0.3 shard_map.106
  6.1 4.5 %collective-permute-start.2 = (f32[448,256]{1,0:T(8,128)S(1)}, f32[448,256]{1,0:T(8,128)S(1)}, u32[]{:S(2)}, u32[]{:S(2)}) collective-permute-start(f32[448,256]{1,0:T(8,128)S(1)} %get-tuple-element.18.pack), channel_id=1, source_target_pairs={{0,17},{1,18},{2,19},{3,20},{4,21},{5,22},{6,23},{7,24},{8,25},{9,... | collective-permute-start | bytes 1376264 | tf_op jit(solution)/shard_map/ppermute | solution.py:1152
  10.6 0.1 collective-permute-start
  10.7 0.0 collective-permute-done.3.facep.facen
  10.7 0.0 copy-done
  10.7 0.0 copy-done.1
  10.7 0.0 copy-done.2
  10.7 0.0 copy-done.3
  10.7 10.4 %shard_map.107 = (f32[5,16,32,256]{3,2,1,0:T(8,128)}, f32[5,16,8,256]{3,2,1,0:T(8,128)S(1)}, f32[5,16,8,256]{3,2,1,0:T(8,128)S(1)}, f32[128,128]{1,0:T(8,128)S(1)}) custom-call(s32[1,1]{1,0:T(1,128)S(6)} %copy.13.refs_0_.count, f32[5,16,32,256]{3,2,1,0:T(8,128)} %start.1, f32[5,16,32,256]{3,2,1,0:T(8,128)} %source.1, f32[3,16,32,256]{3,2,1,0:T(8,128)} %flow.1, ...), custom_call_target="tpu_custom_call" | custom-call | bytes 1024 | tf_op jit(solution)/shard_map/pallas_call | solution.py:628
  21.1 0.0 collective-permute-done.other
  21.1 0.4 %collective-permute-done.2.got = f32[448,256]{1,0:T(8,128)S(1)} collective-permute-done((f32[448,256]{1,0:T(8,128)S(1)}, f32[448,256]{1,0:T(8,128)S(1)}, u32[]{:S(2)}, u32[]{:S(2)}) %collective-permute-start.2) | collective-permute-done | bytes 458784 | tf_op jit(solution)/shard_map/ppermute | solution.py:1152
  21.5 2.0 %shard_map.108 = (f32[2,128,128]{2,1,0:T(8,128)}, f32[160,256]{1,0:T(8,128)S(1)}, f32[160,256]{1,0:T(8,128)S(1)}) custom-call(f32[40,256]{1,0:T(8,128)S(1)} %get-tuple-element.15.own, f32[40,256]{1,0:T(8,128)S(1)} %collective-permute-done.other, f32[448,256]{1,0:T(8,128)S(1)} %get-tuple-element.18.pack, f32[192,256]{1,0:T(8,128)S(1)} %get-tuple-element.19.coef, ...), custom_call_target="tpu_custom_call" | custom-call | bytes 1024 | tf_op jit(solution)/shard_map/pallas_call | solution.py:1020
  23.4 6.5 %all-to-all-start = ((f32[32,8,128]{2,1,0:T(8,128)}), f32[32,8,128]{2,1,0:T(8,128)S(1)}, u32[]{:S(2)}, u32[]{:S(2)}) async-start(f32[32,8,128]{2,1,0:T(8,128)} %bitcast.4), calls=%async_computation | async-start | bytes 262144 | tf_op jit(solution)/shard_map/all_to_all | solution.py:1157
  29.9 0.3 collective-permute-start.4
  30.3 1.1 %collective-permute-done.4.fix = f32[160,256]{1,0:T(8,128)S(1)} collective-permute-done((f32[160,256]{1,0:T(8,128)S(1)}, f32[160,256]{1,0:T(8,128)S(1)}, u32[]{:S(2)}, u32[]{:S(2)}) %collective-permute-start.4) | collective-permute-done | bytes 163872 | tf_op jit(solution)/shard_map/ppermute | solution.py:1158
  31.4 1.2 %shard_map.109 = f32[5,16,32,256]{3,2,1,0:T(8,128)} custom-call(f32[160,256]{1,0:T(8,128)S(1)} %get-tuple-element.22.mine, f32[160,256]{1,0:T(8,128)S(1)} %collective-permute-done.4.fix, f32[5,16,8,256]{3,2,1,0:T(8,128)S(1)} %get-tuple-element.24.edge_low, f32[5,16,8,256]{3,2,1,0:T(8,128)S(1)} %get-tuple-element.25.edge_high, ...), custom_call_target="tpu_custom_call", output_to_operand_aliasing={{}: (4, {})} | custom-call | bytes 1024 | tf_op jit(solution)/shard_map/pallas_call | solution.py:1062
  32.6 5.3 %all-to-all-done.parts = f32[32,8,128]{2,1,0:T(8,128)S(1)} async-done(((f32[32,8,128]{2,1,0:T(8,128)}), f32[32,8,128]{2,1,0:T(8,128)S(1)}, u32[]{:S(2)}, u32[]{:S(2)}) %all-to-all-start) | async-done | bytes 131104 | tf_op jit(solution)/shard_map/all_to_all | solution.py:1157
  37.8 0.7 %shard_map.110 = f32[4,8,12]{2,1,0:T(8,128)} custom-call(f32[32,8,128]{2,1,0:T(8,128)S(1)} %all-to-all-done.parts), custom_call_target="tpu_custom_call" | custom-call | flops 32768 | bytes 131072 | tf_op jit(solution)/shard_map/pallas_call | solution.py:1085
Async XLA Ops:
  2.5 3.3 %collective-permute-start.1 = (f32[368,256]{1,0:T(8,128)S(1)}, f32[368,256]{1,0:T(8,128)S(1)}, u32[]{:S(2)}, u32[]{:S(2)}) collective-permute-start(f32[368,256]{1,0:T(8,128)S(1)} %shard_map.105), channel_id=1, source_target_pairs={{0,16},{16,0},{1,17},{17,1},{2,18},{18,2},{3,19},{19,3},{4,20},{20... | collective-permute-start | bytes 1130504 | tf_op jit(solution)/shard_map/ppermute | solution.py:1148
  3.7 7.0 %copy-start = (s32[1,1,1024]{2,1,0:T(1,128)S(1)}, s32[1,1,1024]{2,1,0:T(1,128)}, u32[]{:S(2)}) copy-start(s32[1,1,1024]{2,1,0:T(1,128)} %param.14) | copy-start | bytes 12292
  3.7 7.0 %copy-start.1 = (s32[1,1,1024]{2,1,0:T(1,128)S(1)}, s32[1,1,1024]{2,1,0:T(1,128)}, u32[]{:S(2)}) copy-start(s32[1,1,1024]{2,1,0:T(1,128)} %param.15) | copy-start | bytes 12292
  3.7 7.0 %copy-start.2 = (s32[1,1,1024]{2,1,0:T(1,128)S(1)}, s32[1,1,1024]{2,1,0:T(1,128)}, u32[]{:S(2)}) copy-start(s32[1,1,1024]{2,1,0:T(1,128)} %param.16) | copy-start | bytes 12292
  3.7 7.0 %copy-start.3 = (f32[1,1,1024]{2,1,0:T(1,128)S(1)}, f32[1,1,1024]{2,1,0:T(1,128)}, u32[]{:S(2)}) copy-start(f32[1,1,1024]{2,1,0:T(1,128)} %param.17) | copy-start | bytes 12292
  5.7 5.0 %collective-permute-start.3 = (f32[22,32,256]{2,1,0:T(8,128)S(1)}, f32[22,32,256]{2,1,0:T(8,128)S(1)}, u32[]{:S(2)}, u32[]{:S(2)}) collective-permute-start(f32[22,32,256]{2,1,0:T(8,128)S(1)} %get-tuple-element.20), channel_id=1, source_target_pairs={{0,16},{16,0},{1,17},{17,1},{2,18},{18,2},{3,19},{19,3},{4,20},{20... | collective-permute-start | bytes 2162696 | tf_op jit(solution)/shard_map/ppermute | solution.py:1153
  6.1 15.4 %collective-permute-start.2 = (f32[448,256]{1,0:T(8,128)S(1)}, f32[448,256]{1,0:T(8,128)S(1)}, u32[]{:S(2)}, u32[]{:S(2)}) collective-permute-start(f32[448,256]{1,0:T(8,128)S(1)} %get-tuple-element.18.pack), channel_id=1, source_target_pairs={{0,17},{1,18},{2,19},{3,20},{4,21},{5,22},{6,23},{7,24},{8,25},{9,... | collective-permute-start | bytes 1376264 | tf_op jit(solution)/shard_map/ppermute | solution.py:1152
  10.6 10.5 %collective-permute-start = (f32[40,256]{1,0:T(8,128)S(1)}, f32[40,256]{1,0:T(8,128)S(1)}, u32[]{:S(2)}, u32[]{:S(2)}) collective-permute-start(f32[40,256]{1,0:T(8,128)S(1)} %get-tuple-element.16), channel_id=1, source_target_pairs={{0,16},{16,0},{1,17},{17,1},{2,18},{18,2},{3,19},{19,3},{4,20},{20... | collective-permute-start | bytes 122888 | tf_op jit(solution)/shard_map/ppermute | solution.py:1154
  23.4 14.4 %all-to-all-start = ((f32[32,8,128]{2,1,0:T(8,128)}), f32[32,8,128]{2,1,0:T(8,128)S(1)}, u32[]{:S(2)}, u32[]{:S(2)}) async-start(f32[32,8,128]{2,1,0:T(8,128)} %bitcast.4), calls=%async_computation | async-start | bytes 262144 | tf_op jit(solution)/shard_map/all_to_all | solution.py:1157
  29.9 1.5 %collective-permute-start.4 = (f32[160,256]{1,0:T(8,128)S(1)}, f32[160,256]{1,0:T(8,128)S(1)}, u32[]{:S(2)}, u32[]{:S(2)}) collective-permute-start(f32[160,256]{1,0:T(8,128)S(1)} %get-tuple-element.23), channel_id=1, source_target_pairs={{0,16},{16,0},{1,17},{17,1},{2,18},{18,2},{3,19},{19,3},{4,20},{20... | collective-permute-start | bytes 491528 | tf_op jit(solution)/shard_map/ppermute | solution.py:1158

commit v6 on v5

--- a/solution.py
+++ b/solution.py
@@ -288,7 +288,7 @@
 
 
 def steps_of(chunks):
-    sizes = [0] + [x for x in (LANES, 2 * LANES) if x < chunks * LANES] + [chunks * LANES]
+    sizes = [0] + [x for x in (2 * LANES,) if x < chunks * LANES] + [chunks * LANES]
     return list(zip(sizes[:-1], sizes[1:]))
 
 
@@ -326,15 +326,15 @@
         for k in range(chunks)
     ]
     to = lax.broadcasted_iota(jnp.int32, (LANES, LANES), 0).astype(F32)
-    for q in range(chunks):
-
-        @pl.when(q * LANES < total)
-        def _():
-            where = jnp.concatenate(
-                [jnp.where(rank[k : k + 1] - float(q * LANES) == to, 1.0, 0.0) for k in range(chunks)], axis=1
-            ).astype(BF16)
-            entries = jnp.concatenate(rows, axis=1).astype(BF16)
-            put(q, lax.dot_general(entries, where, (((1,), (1,)), ((), ())), preferred_element_type=F32))
+    listed = jnp.concatenate(rows, axis=1).astype(BF16)
+
+    @pl.loop(0, lax.div(total + (LANES - 1), LANES))
+    def _(q):
+        first = lax.convert_element_type(q * LANES, F32)
+        where = jnp.concatenate(
+            [jnp.where(rank[k : k + 1] - first == to, 1.0, 0.0) for k in range(chunks)], axis=1
+        ).astype(BF16)
+        put(q, lax.dot_general(listed, where, (((1,), (1,)), ((), ())), preferred_element_type=F32))
 
     return total
 
@@ -776,7 +776,7 @@
         count, refs = refs[0], refs[1:]
     start, source, flow, eddy, refs = *refs[:4], refs[4:]
     if own:
-        lists, (rows, face, *items), refs = refs[:4], refs[4:8], refs[8:]
+        lists, (rows, face, items), refs = refs[:4], refs[4:7], refs[7:]
         cells, turbine, sector, weight, sems = refs[4:]
     else:
         rows, sems = refs[0], refs[-1]
@@ -784,21 +784,31 @@
     tiles_v, tiles_u, tiles_s, tiles_e = refs[:4]
     copies = Copies(sems)
     high = side(own)
-    first = pl.multiple_of(high * (cn - SUB), SUB)
     if own:
         held = copies.take(*zip(lists, (cells, turbine, sector, weight)))
         copies.start(held)
-    pairs = []
-    for h in range(2):
-        cut = (pl.ds(first, SUB), pl.ds(h * LANES, LANES))
-        pairs += [
-            (start.at[(slice(None), slice(None)) + cut], tiles_v.at[:, :, h]),
-            (flow.at[(slice(None), slice(None)) + cut], tiles_u.at[:, :, h]),
-            (eddy.at[(slice(None),) + cut], tiles_e.at[0, :, h]),
-            (source.at[(slice(None), slice(None)) + cut], tiles_s.at[:, :, h]),
-        ]
-    needed = copies.take(*pairs)
-    copies.start(needed)
+    def two_rows(at, to):
+        pairs = []
+        for h in range(2):
+            cut, place = (pl.ds(at, 2), pl.ds(h * LANES, LANES)), pl.ds(to, 2)
+            pairs += [
+                (start.at[(slice(None), slice(None)) + cut], tiles_v.at[:, :, h, place]),
+                (flow.at[(slice(None), slice(None)) + cut], tiles_u.at[:, :, h, place]),
+                (eddy.at[(slice(None),) + cut], tiles_e.at[0, :, h, place]),
+                (source.at[(slice(None), slice(None)) + cut], tiles_s.at[:, :, h, place]),
+            ]
+        return pairs
+
+    sides = [copies.take(*two_rows(0, 0)), copies.take(*two_rows(cn - 2, SUB - 2))]
+
+    def both_ways(act):
+        for k, taken in enumerate(sides):
+
+            @pl.when(high == k)
+            def _():
+                act(taken)
+
+    both_ways(copies.start)
     if own:
         ((near, far),) = facing(ce)
         later = copies.take(
@@ -813,8 +823,8 @@
         copies.wait(held)
         live = count[0, 0]
         listed = entries(live, cells, turbine, sector, weight, cz)
-        for ref, which in zip(items, (high, 1 - high)):
-            edge_items(ce, cn, cz, live, listed, which, ref)
+        edge_items(ce, cn, cz, live, listed, high, items)
+        edge_items(ce, cn, cz, live, listed, 1 - high, face.at[FACE:].reshape(-1, cz))
 
     def plane(ref, f, low, top):
         flat = ref.reshape(ref.shape[0], ce * 2 * SUB, LANES)
@@ -824,7 +834,7 @@
             parts.append(jnp.where(high > 0, y, x))
         return jnp.concatenate(parts, axis=1)
 
-    copies.wait(needed)
+    both_ways(copies.wait)
     planes = [(tiles_v, f, 0) for f in range(5)] + [(tiles_u, k, 0) for k in range(3)] + [(tiles_e, 0, 0)]
     planes += [(tiles_s, f, 0) for f in range(5)]
     planes += [(tiles_v, f, 1) for f in range(5)] + [(tiles_u, k, 1) for k in range(3)] + [(tiles_e, 0, 1)]
@@ -842,10 +852,10 @@
     behind = edge + 1 - 2 * high
     chosen = jnp.where(jnp.logical_and(jnp.logical_or(north == edge, north == behind), slot < live), 1.0, 0.0)
     edge_row = (jnp.where(north == behind, 2 * ce, 0) + column).astype(F32)
-    out[...] = jnp.zeros_like(out)
+    out[...] = jnp.zeros(out.shape, F32)
 
     def put(q, x):
-        out[q // 2 * ITEM : (q // 2 + 1) * ITEM, q % 2 * LANES : (q % 2 + 1) * LANES] = x
+        out[pl.ds(pl.multiple_of(q * ITEM, ITEM), ITEM), :LANES] = x
 
     total = gather_edge(chosen, edge_row, level, key, local, load, put)
     out[out.shape[0] - ITEM :, :] = jnp.full((ITEM, cz), total.astype(F32))
@@ -862,14 +872,16 @@
     ]
     if own:
         chunks = lists[0].shape[0]
-        out += [shape(FACE, cn, cz)] + [shape((chunks * LANES // cz + 1) * ITEM, cz)] * 2
+        most = (chunks + 1) * ITEM
+        planes = pl.cdiv(most, cn)
+        out += [shape(FACE + planes, cn, cz), shape(planes * cn, cz)]
         scratch += [VMEM((chunks, LANES), x.dtype) for x in lists]
     return pl.pallas_call(
         functools.partial(raw_kernel, ce, cn, cz, own),
         out_shape=out,
         in_specs=([whole(pltpu.SMEM)] if own else []) + [whole(pltpu.HBM)] * (4 + len(lists)),
         out_specs=[whole()] * len(out),
-        scratch_shapes=scratch + [pltpu.SemaphoreType.DMA((18,))],
+        scratch_shapes=scratch + [pltpu.SemaphoreType.DMA((26,))],
         compiler_params=params(16),
         cost_estimate=cost(0, 1 << 10),
     )(*([count] if own else []), *in_hbm(start, source, flow, eddy, *lists))
@@ -928,11 +940,12 @@
 
 
 def both_kernel(
-    ce, cn, cz, blocks, copies_out,
+    ce, cn, cz, blocks, copies_out, n_chunks,
     own, other, pack, coef, got, grad,
     chunks, mine, fix,
     table, acc,
 ):
+    other = other.at[FACE:].reshape(-1, cz)
     wide = 2 * ce
     high = side(True)
     sign = (2 * high - 1).astype(F32)
@@ -985,10 +998,10 @@
             table[(2 + row) * wide : (3 + row) * wide, c * cz : (c + 1) * cz] = lo
 
     acc[...] = grad[...]
-    most = (own.shape[0] // ITEM - 1) * (cz // LANES)
+    most = n_chunks
 
     def chunk(ref, q):
-        return ref[q // 2 * ITEM : (q // 2 + 1) * ITEM, q % 2 * LANES : (q % 2 + 1) * LANES]
+        return ref[q * ITEM : (q + 1) * ITEM, :LANES]
 
     def terms(lists):
         turned = [x.T for x in lists]
@@ -1000,25 +1013,20 @@
         rotor_terms(col(0), col(1), col(3), col(4) + col(5) + col(6), key, table, blocks, acc)
 
     terms([chunk(own, 0), chunk(other, 0)])
-    for ref in (own, other):
-        live = jnp.max(ref[ref.shape[0] - ITEM :, :LANES])
-
-        @pl.when(live > float(LANES))
-        def _():
-            terms([chunk(ref, q) for q in range(1, min(2, most))])
-
-        @pl.when(live > 2.0 * LANES)
-        def _():
-            terms([chunk(ref, q) for q in range(2, most)])
+    longest = jnp.max(jnp.maximum(own[own.shape[0] - ITEM :, :LANES], other[other.shape[0] - ITEM :, :LANES]))
+
+    @pl.when(longest > float(LANES))
+    def _():
+        terms([chunk(ref, q) for ref in (own, other) for q in range(1, most)])
 
     for k in range(copies_out):
         chunks[k] = acc[...]
 
 
-def both_edges(own, other, pack, coef, got, grad, size, blocks, copies_out):
+def both_edges(own, other, pack, coef, got, grad, size, blocks, copies_out, n_chunks):
     _, ce, cn, cz = size
     return pl.pallas_call(
-        functools.partial(both_kernel, ce, cn, cz, blocks, copies_out),
+        functools.partial(both_kernel, ce, cn, cz, blocks, copies_out, n_chunks),
         out_shape=(shape(copies_out, blocks * SECT, LANES), shape(10 * ce, cz), shape(10 * ce, cz)),
         in_specs=[whole()] * 6,
         out_specs=(whole(), whole(), whole()),
@@ -1146,14 +1154,15 @@
     swap = [(0, 1), (1, 0)]
     (rows,) = raw_rows(False, *fields)
     other = lax.ppermute(rows, "east", swap)
-    own, face, items, items_out = raw_rows(True, *fields, count, lists)
+    own, face, items = raw_rows(True, *fields, count, lists)
     pack_both, coef = join_rows(own, other, ce)
     ways = [(n, n_north + n + 1) for n in range(n_north - 1)] + [(n_north + n, n - 1) for n in range(1, n_north)]
     got = lax.ppermute(pack_both, ("east", "north"), ways)
     faces = (lax.ppermute(face, "east", swap),) * 2
-    items_in = lax.ppermute(items_out, "east", swap)
     final, *tiles, grad = sweeps(count, *fields, faces, lists, n_north, True)
-    chunks, mine, fix = both_edges(items, items_in, pack_both, coef, got, grad, fields[0].shape, n_north, 2)
+    chunks, mine, fix = both_edges(
+        items, faces[0], pack_both, coef, got, grad, fields[0].shape, n_north, 2, lists[0].shape[0]
+    )
     parts = lax.all_to_all(chunks.reshape(2 * n_north, SECT, LANES), ("east", "north"), 0, 0, tiled=True)
     final = rows_home(mine, lax.ppermute(fix, "east", swap), tiles, final)
     return (final, sum_parts(parts))

time: 39 us -> 38.2 us (0.979)
  Pallas kernels: 18.3 us -> 17.9 us
  transfers between devices with their start and end apart: 6 -> 5, of which waited for: 3 -> 3; matrix products, arithmetic and copies ran while one was open for 0% -> 0% of each run, Pallas kernels for 36% -> 36%
where the time goes in v6:
time: 38.2 us; the launch traced here: 37.9 us
  Pallas kernels  17.9 us (47%)
  starting transfers between devices  11.7 us (31%)
  waiting for transfers between devices  6.88 us (18%)
  between operations  1.41 us (4%)
    pallas_call x1, Pallas kernels, sweeps(): pl.pallas_call(functools.partial(sweeps_kernel, ce, cn, cz, blocks, pair)...  10.4 us
    all_to_all x1, starting transfers between devices, pair_shards(): lax.all_to_all(chunks.reshape(2 * n_north, SECT, LANES), ('east', 'north'...  6.31 us
    all_to_all x1, waiting for transfers between devices, pair_shards(): lax.all_to_all(chunks.reshape(2 * n_north, SECT, LANES), ('east', 'north'...  5.25 us
    ppermute x1, starting transfers between devices, pair_shards(): got = lax.ppermute(pack_both, ('east', 'north'), ways)  4.48 us
    pallas_call x2, Pallas kernels, raw_rows(): pl.pallas_call(functools.partial(raw_kernel, ce, cn, cz, own), out_shape=...  3.52 us
    pallas_call x1, Pallas kernels, both_edges(): pl.pallas_call(functools.partial(both_kernel, ce, cn, cz, blocks, copies_...  1.84 us
    pallas_call x1, Pallas kernels, rows_home(): pl.pallas_call(functools.partial(home_kernel, ce, cn), out_shape=shape(*f...  1.19 us
    ppermute x1, waiting for transfers between devices, pair_shards(): final = rows_home(mine, lax.ppermute(fix, 'east', swap), tiles, final)  1.14 us
  transfers between devices with their start and end apart: 5, of which 3 were waited for; matrix products, arithmetic and copies ran while one was open for 0% of the time, Pallas kernels for 36%

profile of v6, /device:TPU:0, one launch (start us, length us, event | category | flops | bytes accessed | tf_op | source)
XLA Modules:
  0.0 37.9 jit_solution(2067874539426680357)
XLA Ops:
  0.6 1.6 %shard_map.105 = f32[368,256]{1,0:T(8,128)S(1)} custom-call(f32[5,16,32,256]{3,2,1,0:T(8,128)} %start.1, f32[5,16,32,256]{3,2,1,0:T(8,128)} %source.1, f32[3,16,32,256]{3,2,1,0:T(8,128)} %flow.1, f32[16,32,256]{2,1,0:T(8,128)} %eddy.1), custom_call_target="tpu_custom_call" | custom-call | bytes 1024 | tf_op jit(solution)/shard_map/pallas_call | solution.py:879
  2.2 0.5 %collective-permute-start.1 = (f32[368,256]{1,0:T(8,128)S(1)}, f32[368,256]{1,0:T(8,128)S(1)}, u32[]{:S(2)}, u32[]{:S(2)}) collective-permute-start(f32[368,256]{1,0:T(8,128)S(1)} %shard_map.105), channel_id=1, source_target_pairs={{0,16},{16,0},{1,17},{17,1},{2,18},{18,2},{3,19},{19,3},{4,20},{20... | collective-permute-start | bytes 1130504 | tf_op jit(solution)/shard_map/ppermute | solution.py:1156
  3.4 0.0 copy-start
  3.4 0.0 copy-start.1
  3.4 0.0 copy-start.2
  3.4 0.0 copy-start.3
  3.4 1.9 %shard_map.104 = (f32[368,256]{1,0:T(8,128)S(1)}, f32[25,32,256]{2,1,0:T(8,128)S(1)}, f32[96,256]{1,0:T(8,128)S(1)}) custom-call(s32[1,1]{1,0:T(1,128)S(6)} %copy.13.refs_0_.count, f32[5,16,32,256]{3,2,1,0:T(8,128)} %start.1, f32[5,16,32,256]{3,2,1,0:T(8,128)} %source.1, f32[3,16,32,256]{3,2,1,0:T(8,128)} %flow.1, f32[16,32,256]{2,1,0:T(8,128)} %eddy.1, ...), custom_call_target="tpu_custom_call" | custom-call | bytes 1024 | tf_op jit(solution)/shard_map/pallas_call | solution.py:879
  5.4 0.1 collective-permute-start
  5.5 0.0 collective-permute-done.1.other
  5.5 0.3 shard_map.106
  5.8 4.5 %collective-permute-start.2 = (f32[448,256]{1,0:T(8,128)S(1)}, f32[448,256]{1,0:T(8,128)S(1)}, u32[]{:S(2)}, u32[]{:S(2)}) collective-permute-start(f32[448,256]{1,0:T(8,128)S(1)} %get-tuple-element.17.pack), channel_id=1, source_target_pairs={{0,17},{1,18},{2,19},{3,20},{4,21},{5,22},{6,23},{7,24},{8,25},{9,... | collective-permute-start | bytes 1376264 | tf_op jit(solution)/shard_map/ppermute | solution.py:1160
  10.3 0.0 collective-permute-done.facep.facen.other
  10.3 0.0 copy-done
  10.3 0.0 copy-done.1
  10.3 0.0 copy-done.2
  10.3 0.0 copy-done.3
  10.3 10.4 %shard_map.107 = (f32[5,16,32,256]{3,2,1,0:T(8,128)}, f32[5,16,8,256]{3,2,1,0:T(8,128)S(1)}, f32[5,16,8,256]{3,2,1,0:T(8,128)S(1)}, f32[128,128]{1,0:T(8,128)S(1)}) custom-call(s32[1,1]{1,0:T(1,128)S(6)} %copy.13.refs_0_.count, f32[5,16,32,256]{3,2,1,0:T(8,128)} %start.1, f32[5,16,32,256]{3,2,1,0:T(8,128)} %source.1, f32[3,16,32,256]{3,2,1,0:T(8,128)} %flow.1, ...), custom_call_target="tpu_custom_call" | custom-call | bytes 1024 | tf_op jit(solution)/shard_map/pallas_call | solution.py:628
  20.7 0.5 %collective-permute-done.2.got = f32[448,256]{1,0:T(8,128)S(1)} collective-permute-done((f32[448,256]{1,0:T(8,128)S(1)}, f32[448,256]{1,0:T(8,128)S(1)}, u32[]{:S(2)}, u32[]{:S(2)}) %collective-permute-start.2) | collective-permute-done | bytes 458784 | tf_op jit(solution)/shard_map/ppermute | solution.py:1160
  21.2 1.8 %shard_map.108 = (f32[2,128,128]{2,1,0:T(8,128)}, f32[160,256]{1,0:T(8,128)S(1)}, f32[160,256]{1,0:T(8,128)S(1)}) custom-call(f32[96,256]{1,0:T(8,128)S(1)} %get-tuple-element.14.own, f32[25,32,256]{2,1,0:T(8,128)S(1)} %collective-permute-done.facep.facen.other, f32[448,256]{1,0:T(8,128)S(1)} %get-tuple-element.17.pack, ...), custom_call_target="tpu_custom_call" | custom-call | bytes 1024 | tf_op jit(solution)/shard_map/pallas_call | solution.py:1028
  23.0 6.3 %all-to-all-start = ((f32[32,8,128]{2,1,0:T(8,128)}), f32[32,8,128]{2,1,0:T(8,128)S(1)}, u32[]{:S(2)}, u32[]{:S(2)}) async-start(f32[32,8,128]{2,1,0:T(8,128)} %bitcast.4), calls=%async_computation | async-start | bytes 262144 | tf_op jit(solution)/shard_map/all_to_all | solution.py:1166
  29.3 0.3 collective-permute-start.3
  29.6 1.1 %collective-permute-done.3.fix = f32[160,256]{1,0:T(8,128)S(1)} collective-permute-done((f32[160,256]{1,0:T(8,128)S(1)}, f32[160,256]{1,0:T(8,128)S(1)}, u32[]{:S(2)}, u32[]{:S(2)}) %collective-permute-start.3) | collective-permute-done | bytes 163872 | tf_op jit(solution)/shard_map/ppermute | solution.py:1167
  30.8 1.2 %shard_map.109 = f32[5,16,32,256]{3,2,1,0:T(8,128)} custom-call(f32[160,256]{1,0:T(8,128)S(1)} %get-tuple-element.20.mine, f32[160,256]{1,0:T(8,128)S(1)} %collective-permute-done.3.fix, f32[5,16,8,256]{3,2,1,0:T(8,128)S(1)} %get-tuple-element.22.edge_low, f32[5,16,8,256]{3,2,1,0:T(8,128)S(1)} %get-tuple-element.23.edge_high, ...), custom_call_target="tpu_custom_call", output_to_operand_aliasing={{}: (4, {})} | custom-call | bytes 1024 | tf_op jit(solution)/shard_map/pallas_call | solution.py:1070
  32.0 5.3 %all-to-all-done.parts = f32[32,8,128]{2,1,0:T(8,128)S(1)} async-done(((f32[32,8,128]{2,1,0:T(8,128)}), f32[32,8,128]{2,1,0:T(8,128)S(1)}, u32[]{:S(2)}, u32[]{:S(2)}) %all-to-all-start) | async-done | bytes 131104 | tf_op jit(solution)/shard_map/all_to_all | solution.py:1166
  37.2 0.7 %shard_map.110 = f32[4,8,12]{2,1,0:T(8,128)} custom-call(f32[32,8,128]{2,1,0:T(8,128)S(1)} %all-to-all-done.parts), custom_call_target="tpu_custom_call" | custom-call | flops 32768 | bytes 131072 | tf_op jit(solution)/shard_map/pallas_call | solution.py:1093
Async XLA Ops:
  2.2 3.3 %collective-permute-start.1 = (f32[368,256]{1,0:T(8,128)S(1)}, f32[368,256]{1,0:T(8,128)S(1)}, u32[]{:S(2)}, u32[]{:S(2)}) collective-permute-start(f32[368,256]{1,0:T(8,128)S(1)} %shard_map.105), channel_id=1, source_target_pairs={{0,16},{16,0},{1,17},{17,1},{2,18},{18,2},{3,19},{19,3},{4,20},{20... | collective-permute-start | bytes 1130504 | tf_op jit(solution)/shard_map/ppermute | solution.py:1156
  3.4 6.9 %copy-start = (s32[1,1,1024]{2,1,0:T(1,128)S(1)}, s32[1,1,1024]{2,1,0:T(1,128)}, u32[]{:S(2)}) copy-start(s32[1,1,1024]{2,1,0:T(1,128)} %param.14) | copy-start | bytes 12292
  3.4 6.9 %copy-start.1 = (s32[1,1,1024]{2,1,0:T(1,128)S(1)}, s32[1,1,1024]{2,1,0:T(1,128)}, u32[]{:S(2)}) copy-start(s32[1,1,1024]{2,1,0:T(1,128)} %param.15) | copy-start | bytes 12292
  3.4 6.9 %copy-start.2 = (s32[1,1,1024]{2,1,0:T(1,128)S(1)}, s32[1,1,1024]{2,1,0:T(1,128)}, u32[]{:S(2)}) copy-start(s32[1,1,1024]{2,1,0:T(1,128)} %param.16) | copy-start | bytes 12292
  3.4 6.9 %copy-start.3 = (f32[1,1,1024]{2,1,0:T(1,128)S(1)}, f32[1,1,1024]{2,1,0:T(1,128)}, u32[]{:S(2)}) copy-start(f32[1,1,1024]{2,1,0:T(1,128)} %param.17) | copy-start | bytes 12292
  5.4 4.9 %collective-permute-start = (f32[25,32,256]{2,1,0:T(8,128)S(1)}, f32[25,32,256]{2,1,0:T(8,128)S(1)}, u32[]{:S(2)}, u32[]{:S(2)}) collective-permute-start(f32[25,32,256]{2,1,0:T(8,128)S(1)} %get-tuple-element.15), channel_id=1, source_target_pairs={{0,16},{16,0},{1,17},{17,1},{2,18},{18,2},{3,19},{19,3},{4,20},{20... | collective-permute-start | bytes 2457608 | tf_op jit(solution)/shard_map/ppermute | solution.py:1161
  5.8 15.4 %collective-permute-start.2 = (f32[448,256]{1,0:T(8,128)S(1)}, f32[448,256]{1,0:T(8,128)S(1)}, u32[]{:S(2)}, u32[]{:S(2)}) collective-permute-start(f32[448,256]{1,0:T(8,128)S(1)} %get-tuple-element.17.pack), channel_id=1, source_target_pairs={{0,17},{1,18},{2,19},{3,20},{4,21},{5,22},{6,23},{7,24},{8,25},{9,... | collective-permute-start | bytes 1376264 | tf_op jit(solution)/shard_map/ppermute | solution.py:1160
  23.0 14.2 %all-to-all-start = ((f32[32,8,128]{2,1,0:T(8,128)}), f32[32,8,128]{2,1,0:T(8,128)S(1)}, u32[]{:S(2)}, u32[]{:S(2)}) async-start(f32[32,8,128]{2,1,0:T(8,128)} %bitcast.4), calls=%async_computation | async-start | bytes 262144 | tf_op jit(solution)/shard_map/all_to_all | solution.py:1166
  29.3 1.5 %collective-permute-start.3 = (f32[160,256]{1,0:T(8,128)S(1)}, f32[160,256]{1,0:T(8,128)S(1)}, u32[]{:S(2)}, u32[]{:S(2)}) collective-permute-start(f32[160,256]{1,0:T(8,128)S(1)} %get-tuple-element.21), channel_id=1, source_target_pairs={{0,16},{16,0},{1,17},{17,1},{2,18},{18,2},{3,19},{19,3},{4,20},{20... | collective-permute-start | bytes 491528 | tf_op jit(solution)/shard_map/ppermute | solution.py:1167

commit v7 on v6

--- a/solution.py
+++ b/solution.py
@@ -8,6 +8,7 @@
 from jax.sharding import PartitionSpec as P
 
 SECT = 8
+HALF = SECT // 2
 TURB_DEV = 12
 COMPS = 4
 LANES = 128
@@ -270,6 +271,15 @@
     return got[:2], got[2:]
 
 
+def leave_chunks(chunks, acc, copies_out):
+    whole_acc = acc[...]
+    blocks = whole_acc.shape[0] // HALF
+    for n in range(blocks):
+        chunk = whole_acc[n * HALF : (n + 1) * HALF]
+        for k in range(copies_out):
+            chunks[k * blocks + n] = chunk
+
+
 def split(x):
     high = x.astype(BF16)
     return high, (x - high.astype(F32)).astype(BF16)
@@ -295,8 +305,9 @@
 def entries(live, cells, turbine, sector, weight, cz):
     cell, tur = cells[...], turbine[...]
     owner = owner_of(tur)
-    key = (owner * SECT + sector[...]).astype(F32)
-    local = (tur - owner * TURB_DEV).astype(F32)
+    pair = sector[...]
+    key = (owner * HALF + lax.shift_right_logical(pair, 1)).astype(F32)
+    local = (tur - owner * TURB_DEV + jnp.bitwise_and(pair, 1) * (COMPS * TURB_DEV)).astype(F32)
     slot = lax.broadcasted_iota(jnp.int32, cell.shape, 0) * LANES + lax.broadcasted_iota(jnp.int32, cell.shape, 1)
     load = jnp.where(slot < live, weight[...], 0.0)
     line = lax.shift_right_logical(cell, cz.bit_length() - 1)
@@ -348,14 +359,14 @@
     got = jnp.dot(jnp.concatenate([pick, pick], axis=1), table[...], preferred_element_type=F32)
     here = level == lax.broadcasted_iota(jnp.int32, (size, cz), 1).astype(F32)
     lane = lax.broadcasted_iota(jnp.int32, (size, LANES), 1)
-    lane_comp = owner_of(lane)
+    lane_comp = jnp.bitwise_and(owner_of(lane), COMPS - 1)
     lane_tur = (lane - lane_comp * TURB_DEV).astype(F32)
     spread = jnp.zeros((size, LANES), F32)
     for c in range(COMPS):
         part = jnp.where(here, got[:, c * cz : (c + 1) * cz], 0.0)
         spread = jnp.where(lane_comp == c, jnp.sum(part, axis=1, keepdims=True), spread)
     spread = jnp.where(turbine == lane_tur, spread * weight, 0.0)
-    lane_key = lax.broadcasted_iota(jnp.int32, (blocks * SECT, size), 0).astype(F32)
+    lane_key = lax.broadcasted_iota(jnp.int32, (blocks * HALF, size), 0).astype(F32)
     to = jnp.where(lane_key == key, 1.0, 0.0).astype(BF16)
     high = spread.astype(BF16)
     rest = spread - high.astype(F32)
@@ -627,7 +638,7 @@
     more = [shape(EDGE * ce, cz)] * 2 + [shape(chunks, ITEM, LANES), jax.ShapeDtypeStruct((1,), jnp.int32)]
     return pl.pallas_call(
         functools.partial(sweeps_kernel, ce, cn, cz, blocks, pair),
-        out_shape=[shape(*start.shape)] + [shape(5, ce, SUB, cz)] * 2 + [shape(blocks * SECT, LANES)] + ([] if pair else more),
+        out_shape=[shape(*start.shape)] + [shape(5, ce, SUB, cz)] * 2 + [shape(blocks * HALF, LANES)] + ([] if pair else more),
         in_specs=[whole(pltpu.SMEM)] + [whole(pltpu.HBM)] * 6 + [whole()] * 4,
         out_specs=[whole(pltpu.HBM), whole(), whole(), whole()] + ([] if pair else [whole()] * 3 + [whole(pltpu.SMEM)]),
         scratch_shapes=[
@@ -738,8 +749,7 @@
             key = jnp.concatenate([x[2:3] for x in lists], axis=1)
             rotor_terms(col(0), col(1), col(3), col(4) + col(5) + col(6), key, table, blocks, acc)
 
-    for copy in range(copies_out):
-        chunks[copy] = acc[...]
+    leave_chunks(chunks, acc, copies_out)
     for copy in waits:
         copy.wait()
 
@@ -750,14 +760,14 @@
     tile = VMEM((5, ce, SUB, cz), F32)
     return pl.pallas_call(
         functools.partial(edge_kernel, ce, cn, cz, blocks, size),
-        out_shape=(shape(*final.shape), shape(size, blocks * SECT, LANES)),
+        out_shape=(shape(*final.shape), shape(size * blocks, HALF, LANES)),
         in_specs=[whole(pltpu.SMEM)] + [whole()] * (len(args) - 2) + [whole(pltpu.HBM)],
         out_specs=(whole(pltpu.HBM), whole()),
         scratch_shapes=[
             tile,
             tile,
             VMEM((8 * ce, COMPS * cz), BF16),
-            VMEM((blocks * SECT, LANES), F32),
+            VMEM((blocks * HALF, LANES), F32),
             pltpu.SemaphoreType.DMA((2,)),
         ],
         input_output_aliases={len(args) - 1: 0},
@@ -1019,27 +1029,26 @@
     def _():
         terms([chunk(ref, q) for ref in (own, other) for q in range(1, most)])
 
-    for k in range(copies_out):
-        chunks[k] = acc[...]
+    leave_chunks(chunks, acc, copies_out)
 
 
 def both_edges(own, other, pack, coef, got, grad, size, blocks, copies_out, n_chunks):
     _, ce, cn, cz = size
     return pl.pallas_call(
         functools.partial(both_kernel, ce, cn, cz, blocks, copies_out, n_chunks),
-        out_shape=(shape(copies_out, blocks * SECT, LANES), shape(10 * ce, cz), shape(10 * ce, cz)),
+        out_shape=(shape(copies_out * blocks, HALF, LANES), shape(10 * ce, cz), shape(10 * ce, cz)),
         in_specs=[whole()] * 6,
         out_specs=(whole(), whole(), whole()),
         scratch_shapes=[
             VMEM((8 * ce, COMPS * cz), BF16),
-            VMEM((blocks * SECT, LANES), F32),
+            VMEM((blocks * HALF, LANES), F32),
         ],
         compiler_params=params(32),
         cost_estimate=cost(0, 1 << 10),
     )(own, other, pack, coef, got, grad)
 
 
-def home_kernel(ce, cn, mine, fix, edge_low, edge_high, final_in, final, low_out, high_out, sems):
+def last_kernel(ce, cn, parts, mine, fix, edge_low, edge_high, final_in, final, out_sum, low_out, high_out, sems):
     cz = edge_low.shape[3]
     sub = lax.broadcasted_iota(jnp.int32, (SUB, cz), 0)
     high = side(True) > 0
@@ -1061,32 +1070,35 @@
         copy = pltpu.make_async_copy(out, final.at[:, :, pl.ds(place, SUB), :], sems.at[k])
         copy.start()
         waits.append(copy)
+    sum_kernel(parts, out_sum)
     for copy in waits:
         copy.wait()
 
 
-def rows_home(mine, fix, tiles, final):
+def last_step(parts, mine, fix, tiles, final):
     _, ce, cn, cz = final.shape
     return pl.pallas_call(
-        functools.partial(home_kernel, ce, cn),
-        out_shape=shape(*final.shape),
-        in_specs=[whole()] * 4 + [whole(pltpu.HBM)],
-        out_specs=whole(pltpu.HBM),
+        functools.partial(last_kernel, ce, cn),
+        out_shape=(shape(*final.shape), shape(COMPS, SECT, TURB_DEV)),
+        in_specs=[whole()] * 5 + [whole(pltpu.HBM)],
+        out_specs=(whole(pltpu.HBM), whole()),
         scratch_shapes=[
             VMEM((5, ce, SUB, cz), F32),
             VMEM((5, ce, SUB, cz), F32),
             pltpu.SemaphoreType.DMA((2,)),
         ],
-        input_output_aliases={4: 0},
+        input_output_aliases={5: 0},
         compiler_params=params(16),
         cost_estimate=cost(0, 1 << 10),
-    )(mine, fix, *tiles, final)
+    )(parts, mine, fix, *tiles, final)
 
 
 def sum_kernel(parts, out):
     total = jnp.sum(parts[...], axis=0)
     for c in range(COMPS):
-        out[c] = total[:, c * TURB_DEV : (c + 1) * TURB_DEV]
+        for k in range(SECT):
+            at = (k % 2 * COMPS + c) * TURB_DEV
+            out[c, k : k + 1, :] = total[k // 2 : k // 2 + 1, at : at + TURB_DEV]
 
 
 def sum_parts(parts):
@@ -1144,7 +1156,6 @@
     final, chunks = edges(
         n_items, faces, packs, (coef_low, coef_high), gots, tiles, items, grad, final, n_north, n_east
     )
-    chunks = chunks.reshape(n_east * n_north, SECT, LANES)
     parts = lax.all_to_all(chunks, ("east", "north"), 0, 0, tiled=True)
     return (final, sum_parts(parts))
 
@@ -1163,9 +1174,8 @@
     chunks, mine, fix = both_edges(
         items, faces[0], pack_both, coef, got, grad, fields[0].shape, n_north, 2, lists[0].shape[0]
     )
-    parts = lax.all_to_all(chunks.reshape(2 * n_north, SECT, LANES), ("east", "north"), 0, 0, tiled=True)
-    final = rows_home(mine, lax.ppermute(fix, "east", swap), tiles, final)
-    return (final, sum_parts(parts))
+    parts = lax.all_to_all(chunks, ("east", "north"), 0, 0, tiled=True)
+    return last_step(parts, mine, lax.ppermute(fix, "east", swap), tiles, final)
 
 
 def solution(mesh):

time: 38.2 us -> 38 us (level)
  blocking collectives: 0 us -> 13.5 us
  starting transfers between devices: 11.7 us -> 5.19 us
  waiting for transfers between devices: 6.88 us -> 0.54 us
  Pallas kernels: 17.9 us -> 17.1 us
    all_to_all x0 -> x1, blocking collectives: none -> 13.5 us  [pair_shards(): parts = lax.all_to_all(chunks, ('east', 'north'), 0, 0, tiled=True)]
    all_to_all x1 -> x0, starting transfers between devices: 6.31 us -> none  [pair_shards(): lax.all_to_all(chunks.reshape(2 * n_north, SECT, LANES), ('east', 'north'...]
    all_to_all x1 -> x0, waiting for transfers between devices: 5.25 us -> none  [pair_shards(): lax.all_to_all(chunks.reshape(2 * n_north, SECT, LANES), ('east', 'north'...]
    ppermute x1, waiting for transfers between devices: 1.14 us -> 0.01 us  [pair_shards(): return last_step(parts, mine, lax.ppermute(fix, 'east', swap), tiles, final)]
    pallas_call x1, Pallas kernels: 1.84 us -> 1.17 us  [both_edges(): pl.pallas_call(functools.partial(both_kernel, ce, cn, cz, blocks, copies_...]
    pallas_call x2 -> x1, Pallas kernels: 1.9 us -> 1.81 us  [last_step(): pl.pallas_call(functools.partial(last_kernel, ce, cn), out_shape=(shape(*...]
  transfers between devices with their start and end apart: 5 -> 4, of which waited for: 3 -> 1; matrix products, arithmetic and copies ran while one was open for 0% -> 0% of each run, Pallas kernels for 36% -> 33%
where the time goes in v7:
time: 38 us; the launch traced here: 37.8 us
  Pallas kernels  17.1 us (45%)
  blocking collectives  13.5 us (36%)
  starting transfers between devices  5.19 us (14%)
  between operations  1.41 us (4%)
  waiting for transfers between devices  0.54 us (1%)
    all_to_all x1, blocking collectives, pair_shards(): parts = lax.all_to_all(chunks, ('east', 'north'), 0, 0, tiled=True)  13.5 us
    pallas_call x1, Pallas kernels, sweeps(): pl.pallas_call(functools.partial(sweeps_kernel, ce, cn, cz, blocks, pair)...  10.3 us
    ppermute x1, starting transfers between devices, pair_shards(): got = lax.ppermute(pack_both, ('east', 'north'), ways)  4.48 us
    pallas_call x2, Pallas kernels, raw_rows(): pl.pallas_call(functools.partial(raw_kernel, ce, cn, cz, own), out_shape=...  3.52 us
    pallas_call x1, Pallas kernels, last_step(): pl.pallas_call(functools.partial(last_kernel, ce, cn), out_shape=(shape(*...  1.81 us
    pallas_call x1, Pallas kernels, both_edges(): pl.pallas_call(functools.partial(both_kernel, ce, cn, cz, blocks, copies_...  1.17 us
  transfers between devices with their start and end apart: 4, of which 1 were waited for; matrix products, arithmetic and copies ran while one was open for 0% of the time, Pallas kernels for 33%

profile of v7, /device:TPU:0, one launch (start us, length us, event | category | flops | bytes accessed | tf_op | source)
XLA Modules:
  0.0 37.8 jit_solution(10234987711009574065)
XLA Ops:
  0.6 1.6 %shard_map.105 = f32[368,256]{1,0:T(8,128)S(1)} custom-call(f32[5,16,32,256]{3,2,1,0:T(8,128)} %start.1, f32[5,16,32,256]{3,2,1,0:T(8,128)} %source.1, f32[3,16,32,256]{3,2,1,0:T(8,128)} %flow.1, f32[16,32,256]{2,1,0:T(8,128)} %eddy.1), custom_call_target="tpu_custom_call" | custom-call | bytes 1024 | tf_op jit(solution)/shard_map/pallas_call | solution.py:889
  2.2 0.5 %collective-permute-start.1 = (f32[368,256]{1,0:T(8,128)S(1)}, f32[368,256]{1,0:T(8,128)S(1)}, u32[]{:S(2)}, u32[]{:S(2)}) collective-permute-start(f32[368,256]{1,0:T(8,128)S(1)} %shard_map.105), channel_id=1, source_target_pairs={{0,16},{16,0},{1,17},{17,1},{2,18},{18,2},{3,19},{19,3},{4,20},{20... | collective-permute-start | bytes 1130504 | tf_op jit(solution)/shard_map/ppermute | solution.py:1167
  3.4 0.0 copy-start
  3.4 0.0 copy-start.1
  3.4 0.0 copy-start.2
  3.4 0.0 copy-start.3
  3.4 1.9 %shard_map.104 = (f32[368,256]{1,0:T(8,128)S(1)}, f32[25,32,256]{2,1,0:T(8,128)S(1)}, f32[96,256]{1,0:T(8,128)S(1)}) custom-call(s32[1,1]{1,0:T(1,128)S(6)} %copy.13.refs_0_.count, f32[5,16,32,256]{3,2,1,0:T(8,128)} %start.1, f32[5,16,32,256]{3,2,1,0:T(8,128)} %source.1, f32[3,16,32,256]{3,2,1,0:T(8,128)} %flow.1, f32[16,32,256]{2,1,0:T(8,128)} %eddy.1, ...), custom_call_target="tpu_custom_call" | custom-call | bytes 1024 | tf_op jit(solution)/shard_map/pallas_call | solution.py:889
  5.4 0.1 collective-permute-start
  5.5 0.0 collective-permute-done.1.other
  5.5 0.3 shard_map.106
  5.8 4.5 %collective-permute-start.2 = (f32[448,256]{1,0:T(8,128)S(1)}, f32[448,256]{1,0:T(8,128)S(1)}, u32[]{:S(2)}, u32[]{:S(2)}) collective-permute-start(f32[448,256]{1,0:T(8,128)S(1)} %get-tuple-element.17.pack), channel_id=1, source_target_pairs={{0,17},{1,18},{2,19},{3,20},{4,21},{5,22},{6,23},{7,24},{8,25},{9,... | collective-permute-start | bytes 1376264 | tf_op jit(solution)/shard_map/ppermute | solution.py:1171
  10.3 0.0 collective-permute-done.facep.facen.other
  10.3 0.0 copy-done
  10.3 0.0 copy-done.1
  10.3 0.0 copy-done.2
  10.3 0.0 copy-done.3
  10.3 10.3 %shard_map.107 = (f32[5,16,32,256]{3,2,1,0:T(8,128)}, f32[5,16,8,256]{3,2,1,0:T(8,128)S(1)}, f32[5,16,8,256]{3,2,1,0:T(8,128)S(1)}, f32[64,128]{1,0:T(8,128)S(1)}) custom-call(s32[1,1]{1,0:T(1,128)S(6)} %copy.13.refs_0_.count, f32[5,16,32,256]{3,2,1,0:T(8,128)} %start.1, f32[5,16,32,256]{3,2,1,0:T(8,128)} %source.1, f32[3,16,32,256]{3,2,1,0:T(8,128)} %flow.1, ...), custom_call_target="tpu_custom_call" | custom-call | bytes 1024 | tf_op jit(solution)/shard_map/pallas_call | solution.py:639
  20.6 0.5 %collective-permute-done.2.got = f32[448,256]{1,0:T(8,128)S(1)} collective-permute-done((f32[448,256]{1,0:T(8,128)S(1)}, f32[448,256]{1,0:T(8,128)S(1)}, u32[]{:S(2)}, u32[]{:S(2)}) %collective-permute-start.2) | collective-permute-done | bytes 458784 | tf_op jit(solution)/shard_map/ppermute | solution.py:1171
  21.2 1.2 %shard_map.108 = (f32[32,4,128]{2,1,0:T(4,128)S(1)}, f32[160,256]{1,0:T(8,128)S(1)}, f32[160,256]{1,0:T(8,128)S(1)}) custom-call(f32[96,256]{1,0:T(8,128)S(1)} %get-tuple-element.14.own, f32[25,32,256]{2,1,0:T(8,128)S(1)} %collective-permute-done.facep.facen.other, f32[448,256]{1,0:T(8,128)S(1)} %get-tuple-element.17.pack, ...), custom_call_target="tpu_custom_call" | custom-call | bytes 1024 | tf_op jit(solution)/shard_map/pallas_call | solution.py:1037
  22.3 0.1 collective-permute-start.3
  22.4 13.5 %all_to_all.5.parts = f32[32,4,128]{2,1,0:T(4,128)S(1)} all-to-all(f32[32,4,128]{2,1,0:T(4,128)S(1)} %get-tuple-element.20), channel_id=1, replica_groups=mesh['east'=2,'north'=16] {'east','north'}, dimensions={0} | all-to-all | bytes 131072 | tf_op jit(solution)/shard_map/all_to_all | solution.py:1177
  35.9 0.0 collective-permute-done.3.fix
  35.9 1.8 %shard_map.109 = (f32[5,16,32,256]{3,2,1,0:T(8,128)}, f32[4,8,12]{2,1,0:T(8,128)}) custom-call(f32[32,4,128]{2,1,0:T(4,128)S(1)} %all_to_all.5.parts, f32[160,256]{1,0:T(8,128)S(1)} %get-tuple-element.21.mine, f32[160,256]{1,0:T(8,128)S(1)} %collective-permute-done.3.fix, ...), custom_call_target="tpu_custom_call", output_to_operand_aliasing={{0}: (5, {})} | custom-call | bytes 1024 | tf_op jit(solution)/shard_map/pallas_call | solution.py:1080
Async XLA Ops:
  2.2 3.3 %collective-permute-start.1 = (f32[368,256]{1,0:T(8,128)S(1)}, f32[368,256]{1,0:T(8,128)S(1)}, u32[]{:S(2)}, u32[]{:S(2)}) collective-permute-start(f32[368,256]{1,0:T(8,128)S(1)} %shard_map.105), channel_id=1, source_target_pairs={{0,16},{16,0},{1,17},{17,1},{2,18},{18,2},{3,19},{19,3},{4,20},{20... | collective-permute-start | bytes 1130504 | tf_op jit(solution)/shard_map/ppermute | solution.py:1167
  3.4 6.9 %copy-start = (s32[1,1,1024]{2,1,0:T(1,128)S(1)}, s32[1,1,1024]{2,1,0:T(1,128)}, u32[]{:S(2)}) copy-start(s32[1,1,1024]{2,1,0:T(1,128)} %param.14) | copy-start | bytes 12292
  3.4 6.9 %copy-start.1 = (s32[1,1,1024]{2,1,0:T(1,128)S(1)}, s32[1,1,1024]{2,1,0:T(1,128)}, u32[]{:S(2)}) copy-start(s32[1,1,1024]{2,1,0:T(1,128)} %param.15) | copy-start | bytes 12292
  3.4 6.9 %copy-start.2 = (s32[1,1,1024]{2,1,0:T(1,128)S(1)}, s32[1,1,1024]{2,1,0:T(1,128)}, u32[]{:S(2)}) copy-start(s32[1,1,1024]{2,1,0:T(1,128)} %param.16) | copy-start | bytes 12292
  3.4 6.9 %copy-start.3 = (f32[1,1,1024]{2,1,0:T(1,128)S(1)}, f32[1,1,1024]{2,1,0:T(1,128)}, u32[]{:S(2)}) copy-start(f32[1,1,1024]{2,1,0:T(1,128)} %param.17) | copy-start | bytes 12292
  5.4 4.9 %collective-permute-start = (f32[25,32,256]{2,1,0:T(8,128)S(1)}, f32[25,32,256]{2,1,0:T(8,128)S(1)}, u32[]{:S(2)}, u32[]{:S(2)}) collective-permute-start(f32[25,32,256]{2,1,0:T(8,128)S(1)} %get-tuple-element.15), channel_id=1, source_target_pairs={{0,16},{16,0},{1,17},{17,1},{2,18},{18,2},{3,19},{19,3},{4,20},{20... | collective-permute-start | bytes 2457608 | tf_op jit(solution)/shard_map/ppermute | solution.py:1172
  5.8 15.4 %collective-permute-start.2 = (f32[448,256]{1,0:T(8,128)S(1)}, f32[448,256]{1,0:T(8,128)S(1)}, u32[]{:S(2)}, u32[]{:S(2)}) collective-permute-start(f32[448,256]{1,0:T(8,128)S(1)} %get-tuple-element.17.pack), channel_id=1, source_target_pairs={{0,17},{1,18},{2,19},{3,20},{4,21},{5,22},{6,23},{7,24},{8,25},{9,... | collective-permute-start | bytes 1376264 | tf_op jit(solution)/shard_map/ppermute | solution.py:1171
  22.3 13.6 %collective-permute-start.3 = (f32[160,256]{1,0:T(8,128)S(1)}, f32[160,256]{1,0:T(8,128)S(1)}, u32[]{:S(2)}, u32[]{:S(2)}) collective-permute-start(f32[160,256]{1,0:T(8,128)S(1)} %get-tuple-element.22), channel_id=1, source_target_pairs={{0,16},{16,0},{1,17},{17,1},{2,18},{18,2},{3,19},{19,3},{4,20},{20... | collective-permute-start | bytes 491528 | tf_op jit(solution)/shard_map/ppermute | solution.py:1178

commit v8 on v7

--- a/solution.py
+++ b/solution.py
@@ -1049,25 +1049,19 @@
 
 
 def last_kernel(ce, cn, parts, mine, fix, edge_low, edge_high, final_in, final, out_sum, low_out, high_out, sems):
-    cz = edge_low.shape[3]
-    sub = lax.broadcasted_iota(jnp.int32, (SUB, cz), 0)
     high = side(True) > 0
     waits = []
-    for k, (edge, out, near, far, place) in enumerate(
-        ((edge_low, low_out, 0, 1, 0), (edge_high, high_out, SUB - 1, SUB - 2, cn - SUB))
+    for k, (edge, out, rows, place) in enumerate(
+        ((edge_low, low_out, (0, 1), 0), (edge_high, high_out, (SUB - 1, SUB - 2), cn - 2))
     ):
         from_mine = high if k else jnp.logical_not(high)
-        for f in range(5):
-
-            def plane(at):
-                span = pl.ds(at * ce, ce)
-                return jnp.where(from_mine, mine[span, :], fix[span, :])
-
-            a, b = plane(f), plane(5 + f)
-            for e in range(ce):
-                rows = jnp.where(sub == near, a[e : e + 1, :], jnp.where(sub == far, b[e : e + 1, :], 0.0))
-                out[f, e] = edge[f, e] + rows
-        copy = pltpu.make_async_copy(out, final.at[:, :, pl.ds(place, SUB), :], sems.at[k])
+        for part, row in enumerate(rows):
+            for f in range(5):
+                span = pl.ds((part * 5 + f) * ce, ce)
+                add = jnp.where(from_mine, mine[span, :], fix[span, :])
+                for e in range(ce):
+                    out[f, e, row % 2 : row % 2 + 1, :] = edge[f, e, row : row + 1, :] + add[e : e + 1, :]
+        copy = pltpu.make_async_copy(out, final.at[:, :, pl.ds(place, 2), :], sems.at[k])
         copy.start()
         waits.append(copy)
     sum_kernel(parts, out_sum)
@@ -1083,8 +1077,8 @@
         in_specs=[whole()] * 5 + [whole(pltpu.HBM)],
         out_specs=(whole(pltpu.HBM), whole()),
         scratch_shapes=[
-            VMEM((5, ce, SUB, cz), F32),
-            VMEM((5, ce, SUB, cz), F32),
+            VMEM((5, ce, 2, cz), F32),
+            VMEM((5, ce, 2, cz), F32),
             pltpu.SemaphoreType.DMA((2,)),
         ],
         input_output_aliases={5: 0},

time: 38 us -> 37.8 us (level)
  Pallas kernels: 17.1 us -> 16.7 us
where the time goes in v8:
time: 37.8 us; the launch traced here: 37.7 us
  Pallas kernels  16.7 us (44%)
  blocking collectives  13.8 us (37%)
  starting transfers between devices  5.19 us (14%)
  between operations  1.41 us (4%)
  waiting for transfers between devices  0.54 us (1%)
    all_to_all x1, blocking collectives, pair_shards(): parts = lax.all_to_all(chunks, ('east', 'north'), 0, 0, tiled=True)  13.8 us
    pallas_call x1, Pallas kernels, sweeps(): pl.pallas_call(functools.partial(sweeps_kernel, ce, cn, cz, blocks, pair)...  10.3 us
    ppermute x1, starting transfers between devices, pair_shards(): got = lax.ppermute(pack_both, ('east', 'north'), ways)  4.48 us
    pallas_call x2, Pallas kernels, raw_rows(): pl.pallas_call(functools.partial(raw_kernel, ce, cn, cz, own), out_shape=...  3.52 us
    pallas_call x1, Pallas kernels, last_step(): pl.pallas_call(functools.partial(last_kernel, ce, cn), out_shape=(shape(*...  1.48 us
    pallas_call x1, Pallas kernels, both_edges(): pl.pallas_call(functools.partial(both_kernel, ce, cn, cz, blocks, copies_...  1.17 us
  transfers between devices with their start and end apart: 4, of which 1 were waited for; matrix products, arithmetic and copies ran while one was open for 0% of the time, Pallas kernels for 33%

profile of v8, /device:TPU:0, one launch (start us, length us, event | category | flops | bytes accessed | tf_op | source)
XLA Modules:
  0.0 37.7 jit_solution(4854186077064424770)
XLA Ops:
  0.6 1.6 %shard_map.105 = f32[368,256]{1,0:T(8,128)S(1)} custom-call(f32[5,16,32,256]{3,2,1,0:T(8,128)} %start.1, f32[5,16,32,256]{3,2,1,0:T(8,128)} %source.1, f32[3,16,32,256]{3,2,1,0:T(8,128)} %flow.1, f32[16,32,256]{2,1,0:T(8,128)} %eddy.1), custom_call_target="tpu_custom_call" | custom-call | bytes 1024 | tf_op jit(solution)/shard_map/pallas_call | solution.py:889
  2.2 0.5 %collective-permute-start.1 = (f32[368,256]{1,0:T(8,128)S(1)}, f32[368,256]{1,0:T(8,128)S(1)}, u32[]{:S(2)}, u32[]{:S(2)}) collective-permute-start(f32[368,256]{1,0:T(8,128)S(1)} %shard_map.105), channel_id=1, source_target_pairs={{0,16},{16,0},{1,17},{17,1},{2,18},{18,2},{3,19},{19,3},{4,20},{20... | collective-permute-start | bytes 1130504 | tf_op jit(solution)/shard_map/ppermute | solution.py:1161
  3.4 0.0 copy-start
  3.4 0.0 copy-start.1
  3.4 0.0 copy-start.2
  3.4 0.0 copy-start.3
  3.4 1.9 %shard_map.104 = (f32[368,256]{1,0:T(8,128)S(1)}, f32[25,32,256]{2,1,0:T(8,128)S(1)}, f32[96,256]{1,0:T(8,128)S(1)}) custom-call(s32[1,1]{1,0:T(1,128)S(6)} %copy.13.refs_0_.count, f32[5,16,32,256]{3,2,1,0:T(8,128)} %start.1, f32[5,16,32,256]{3,2,1,0:T(8,128)} %source.1, f32[3,16,32,256]{3,2,1,0:T(8,128)} %flow.1, f32[16,32,256]{2,1,0:T(8,128)} %eddy.1, ...), custom_call_target="tpu_custom_call" | custom-call | bytes 1024 | tf_op jit(solution)/shard_map/pallas_call | solution.py:889
  5.4 0.1 collective-permute-start
  5.5 0.0 collective-permute-done.1.other
  5.5 0.3 shard_map.106
  5.8 4.5 %collective-permute-start.2 = (f32[448,256]{1,0:T(8,128)S(1)}, f32[448,256]{1,0:T(8,128)S(1)}, u32[]{:S(2)}, u32[]{:S(2)}) collective-permute-start(f32[448,256]{1,0:T(8,128)S(1)} %get-tuple-element.17.pack), channel_id=1, source_target_pairs={{0,17},{1,18},{2,19},{3,20},{4,21},{5,22},{6,23},{7,24},{8,25},{9,... | collective-permute-start | bytes 1376264 | tf_op jit(solution)/shard_map/ppermute | solution.py:1165
  10.3 0.0 collective-permute-done.facep.facen.other
  10.3 0.0 copy-done
  10.3 0.0 copy-done.1
  10.3 0.0 copy-done.2
  10.3 0.0 copy-done.3
  10.3 10.3 %shard_map.107 = (f32[5,16,32,256]{3,2,1,0:T(8,128)}, f32[5,16,8,256]{3,2,1,0:T(8,128)S(1)}, f32[5,16,8,256]{3,2,1,0:T(8,128)S(1)}, f32[64,128]{1,0:T(8,128)S(1)}) custom-call(s32[1,1]{1,0:T(1,128)S(6)} %copy.13.refs_0_.count, f32[5,16,32,256]{3,2,1,0:T(8,128)} %start.1, f32[5,16,32,256]{3,2,1,0:T(8,128)} %source.1, f32[3,16,32,256]{3,2,1,0:T(8,128)} %flow.1, ...), custom_call_target="tpu_custom_call" | custom-call | bytes 1024 | tf_op jit(solution)/shard_map/pallas_call | solution.py:639
  20.6 0.5 %collective-permute-done.2.got = f32[448,256]{1,0:T(8,128)S(1)} collective-permute-done((f32[448,256]{1,0:T(8,128)S(1)}, f32[448,256]{1,0:T(8,128)S(1)}, u32[]{:S(2)}, u32[]{:S(2)}) %collective-permute-start.2) | collective-permute-done | bytes 458784 | tf_op jit(solution)/shard_map/ppermute | solution.py:1165
  21.2 1.2 %shard_map.108 = (f32[32,4,128]{2,1,0:T(4,128)S(1)}, f32[160,256]{1,0:T(8,128)S(1)}, f32[160,256]{1,0:T(8,128)S(1)}) custom-call(f32[96,256]{1,0:T(8,128)S(1)} %get-tuple-element.14.own, f32[25,32,256]{2,1,0:T(8,128)S(1)} %collective-permute-done.facep.facen.other, f32[448,256]{1,0:T(8,128)S(1)} %get-tuple-element.17.pack, ...), custom_call_target="tpu_custom_call" | custom-call | bytes 1024 | tf_op jit(solution)/shard_map/pallas_call | solution.py:1037
  22.3 0.1 collective-permute-start.3
  22.4 13.8 %all_to_all.5.parts = f32[32,4,128]{2,1,0:T(4,128)S(1)} all-to-all(f32[32,4,128]{2,1,0:T(4,128)S(1)} %get-tuple-element.20), channel_id=1, replica_groups=mesh['east'=2,'north'=16] {'east','north'}, dimensions={0} | all-to-all | bytes 131072 | tf_op jit(solution)/shard_map/all_to_all | solution.py:1171
  36.2 0.0 collective-permute-done.3.fix
  36.2 1.5 %shard_map.109 = (f32[5,16,32,256]{3,2,1,0:T(8,128)}, f32[4,8,12]{2,1,0:T(8,128)}) custom-call(f32[32,4,128]{2,1,0:T(4,128)S(1)} %all_to_all.5.parts, f32[160,256]{1,0:T(8,128)S(1)} %get-tuple-element.21.mine, f32[160,256]{1,0:T(8,128)S(1)} %collective-permute-done.3.fix, ...), custom_call_target="tpu_custom_call", output_to_operand_aliasing={{0}: (5, {})} | custom-call | bytes 1024 | tf_op jit(solution)/shard_map/pallas_call | solution.py:1074
Async XLA Ops:
  2.2 3.3 %collective-permute-start.1 = (f32[368,256]{1,0:T(8,128)S(1)}, f32[368,256]{1,0:T(8,128)S(1)}, u32[]{:S(2)}, u32[]{:S(2)}) collective-permute-start(f32[368,256]{1,0:T(8,128)S(1)} %shard_map.105), channel_id=1, source_target_pairs={{0,16},{16,0},{1,17},{17,1},{2,18},{18,2},{3,19},{19,3},{4,20},{20... | collective-permute-start | bytes 1130504 | tf_op jit(solution)/shard_map/ppermute | solution.py:1161
  3.4 6.9 %copy-start = (s32[1,1,1024]{2,1,0:T(1,128)S(1)}, s32[1,1,1024]{2,1,0:T(1,128)}, u32[]{:S(2)}) copy-start(s32[1,1,1024]{2,1,0:T(1,128)} %param.14) | copy-start | bytes 12292
  3.4 6.9 %copy-start.1 = (s32[1,1,1024]{2,1,0:T(1,128)S(1)}, s32[1,1,1024]{2,1,0:T(1,128)}, u32[]{:S(2)}) copy-start(s32[1,1,1024]{2,1,0:T(1,128)} %param.15) | copy-start | bytes 12292
  3.4 6.9 %copy-start.2 = (s32[1,1,1024]{2,1,0:T(1,128)S(1)}, s32[1,1,1024]{2,1,0:T(1,128)}, u32[]{:S(2)}) copy-start(s32[1,1,1024]{2,1,0:T(1,128)} %param.16) | copy-start | bytes 12292
  3.4 6.9 %copy-start.3 = (f32[1,1,1024]{2,1,0:T(1,128)S(1)}, f32[1,1,1024]{2,1,0:T(1,128)}, u32[]{:S(2)}) copy-start(f32[1,1,1024]{2,1,0:T(1,128)} %param.17) | copy-start | bytes 12292
  5.4 4.9 %collective-permute-start = (f32[25,32,256]{2,1,0:T(8,128)S(1)}, f32[25,32,256]{2,1,0:T(8,128)S(1)}, u32[]{:S(2)}, u32[]{:S(2)}) collective-permute-start(f32[25,32,256]{2,1,0:T(8,128)S(1)} %get-tuple-element.15), channel_id=1, source_target_pairs={{0,16},{16,0},{1,17},{17,1},{2,18},{18,2},{3,19},{19,3},{4,20},{20... | collective-permute-start | bytes 2457608 | tf_op jit(solution)/shard_map/ppermute | solution.py:1166
  5.8 15.4 %collective-permute-start.2 = (f32[448,256]{1,0:T(8,128)S(1)}, f32[448,256]{1,0:T(8,128)S(1)}, u32[]{:S(2)}, u32[]{:S(2)}) collective-permute-start(f32[448,256]{1,0:T(8,128)S(1)} %get-tuple-element.17.pack), channel_id=1, source_target_pairs={{0,17},{1,18},{2,19},{3,20},{4,21},{5,22},{6,23},{7,24},{8,25},{9,... | collective-permute-start | bytes 1376264 | tf_op jit(solution)/shard_map/ppermute | solution.py:1165
  22.3 13.9 %collective-permute-start.3 = (f32[160,256]{1,0:T(8,128)S(1)}, f32[160,256]{1,0:T(8,128)S(1)}, u32[]{:S(2)}, u32[]{:S(2)}) collective-permute-start(f32[160,256]{1,0:T(8,128)S(1)} %get-tuple-element.22), channel_id=1, source_target_pairs={{0,16},{16,0},{1,17},{17,1},{2,18},{18,2},{3,19},{19,3},{4,20},{20... | collective-permute-start | bytes 491528 | tf_op jit(solution)/shard_map/ppermute | solution.py:1172
